TPU v7x, 128 devices: a whole 4x4x4 slice. The times are simulated.
128 devices in a mesh: enc: 4 (over y), fsdp: 32 (over z, x, core).
Axes of the slice: x: 4, y: 4, z: 4, core: 2. Of those that a mesh axis runs over, the one named last changes fastest.
Arguments:
- hidden: bfloat16 [24576, 4096], P(('enc', 'fsdp')), may hold values from -60 to 60
- query_weight: bfloat16 [4096, 2048], P('fsdp'), may hold values from -0.09375 to 0.09375
- neighbour_keys: bfloat16 [768, 128, 2048], P(('enc', 'fsdp')), may hold values from -50 to 50
- neighbour_values: bfloat16 [768, 128, 2048], P(('enc', 'fsdp')), may hold values from -6 to 6
- neighbour_owner: int32 [384, 2], P(('enc', 'fsdp')), may hold values from 0 to 3, all different within a row; in each aligned block of 3 rows (0 to 2, 3 to 5, ...) at most 2 rows name the same one
- neighbour_row: int32 [384, 2], P(('enc', 'fsdp')), may hold values from 0 to 5
- output_cotangent: bfloat16 [24576, 2048], P(('enc', 'fsdp')), may hold values from -6 to 6
Outputs:
- attended: bfloat16 [24576, 2048], P(('enc', 'fsdp'))
- grad_hidden: bfloat16 [24576, 4096], P(('enc', 'fsdp'))
- grad_keys: bfloat16 [768, 128, 2048], P(('enc', 'fsdp'))
- grad_values: bfloat16 [768, 128, 2048], P(('enc', 'fsdp'))
Inputs may be any that keep to these rules, and one draw needn't show every extreme that they name: `neighbour_owner`: the two owners of a group differ. Among the 3 groups of one device (aligned blocks of rows), no owner is named more than 2 times.
All inputs are finite; a program needn't handle non-finite values.
Results may differ from a plain program's by a relative error of at most 0.012.
The roundings to bfloat16 on the way count: a program that leaves them out, or rounds other values in their place, can miss the bound.
Values may be sent and summed in bfloat16 or wider, within the bound.
No kernel may reach another device: no remote copies, remote signals or barrier semaphores. Data moves between devices by JAX's collectives and lax.ppermute only.
A program may use at most 128 MiB of HBM per device.

v0:
```python
import math

import jax
import jax.numpy as jnp
from jax import lax
from jax.sharding import PartitionSpec as P

HEADS = 16
HEAD_DIM = 128


def split_heads(block):
    return block.reshape(block.shape[0], HEADS, HEAD_DIM)


def partial_attend(query, keys, values):
    score_scale = 1.0 / math.sqrt(HEAD_DIM)
    scores = (
        jnp.einsum(
            "chd,lhd->hcl",
            split_heads(query),
            split_heads(keys),
            preferred_element_type=jnp.float32,
        )
        * score_scale
    )
    peak = jnp.max(scores, axis=2)
    exponent = jnp.exp(scores - peak[:, :, None])
    row_total = jnp.sum(exponent, axis=2)
    partial_out = jnp.einsum(
        "hcl,lhd->chd",
        exponent.astype(jnp.bfloat16),
        split_heads(values),
        preferred_element_type=jnp.float32,
    )
    return (partial_out.reshape(query.shape), peak.T, row_total.T)


def partial_grad(query, keys, values, cotangent, log_total, delta_rows):
    score_scale = 1.0 / math.sqrt(HEAD_DIM)
    query_heads = split_heads(query)
    key_heads = split_heads(keys)
    value_heads = split_heads(values)
    cot_heads = split_heads(cotangent)
    scores = (
        jnp.einsum("chd,lhd->hcl", query_heads, key_heads, preferred_element_type=jnp.float32)
        * score_scale
    )
    probs = jnp.exp(scores - log_total.T[:, :, None])
    grad_probs = jnp.einsum(
        "chd,lhd->hcl", cot_heads, value_heads, preferred_element_type=jnp.float32
    )
    grad_scores = (probs * (grad_probs - delta_rows.T[:, :, None]) * score_scale).astype(
        jnp.bfloat16
    )
    grad_query = jnp.einsum(
        "hcl,lhd->chd", grad_scores, key_heads, preferred_element_type=jnp.float32
    ).reshape(query.shape)
    grad_key = jnp.einsum(
        "hcl,chd->lhd", grad_scores, query_heads, preferred_element_type=jnp.float32
    ).reshape(keys.shape)
    grad_value = jnp.einsum(
        "hcl,chd->lhd", probs.astype(jnp.bfloat16), cot_heads, preferred_element_type=jnp.float32
    ).reshape(values.shape)
    return (grad_query, grad_key.astype(jnp.bfloat16), grad_value.astype(jnp.bfloat16))


def combine(first, second):
    out_a, peak_a, total_a = first
    out_b, peak_b, total_b = second
    peak = jnp.maximum(peak_a, peak_b)
    weight_a = jnp.exp(peak_a - peak)
    weight_b = jnp.exp(peak_b - peak)
    denominator = weight_a * total_a + weight_b * total_b
    leading = out_a.shape[:-1]
    summed = out_a.reshape(leading + (HEADS, HEAD_DIM)) * weight_a[..., None]
    summed = summed + out_b.reshape(leading + (HEADS, HEAD_DIM)) * weight_b[..., None]
    combined = summed / denominator[..., None]
    return (combined.reshape(out_a.shape), peak + jnp.log(denominator))


def row_delta(cotangent, combined):
    leading = combined.shape[:-1]
    product = cotangent.astype(jnp.float32) * combined
    return jnp.sum(product.reshape(leading + (HEADS, HEAD_DIM)), axis=-1)


def by_request(received, position, group_count):
    flat = received.reshape((-1,) + received.shape[2:])
    taken = jnp.take(flat, position, axis=0)
    return taken.reshape((group_count, 2) + received.shape[2:])


def pair_up(array):
    return jnp.broadcast_to(array[:, None], (array.shape[0], 2) + array.shape[1:])


def per_device(
    hidden,
    query_weight,
    neighbour_keys,
    neighbour_values,
    neighbour_owner,
    neighbour_row,
    output_cotangent,
):
    tok_rows = hidden.shape[0]
    group_count = neighbour_owner.shape[0]
    group_len = tok_rows // group_count
    feature_width = query_weight.shape[1]
    stored = neighbour_keys.shape[0]
    nbr_tokens = neighbour_keys.shape[1]
    enc_count = lax.axis_size("enc")
    capacity = 2 * group_count // enc_count + 1
    request_count = 2 * group_count
    slot_count = enc_count * capacity
    weights = lax.all_gather(query_weight, "fsdp", axis=0, tiled=True)
    query = jnp.dot(hidden, weights, preferred_element_type=jnp.float32).astype(jnp.bfloat16)
    query_groups = query.reshape(group_count, group_len, feature_width)
    cot_groups = output_cotangent.reshape(group_count, group_len, feature_width)
    owner_flat = neighbour_owner.reshape(request_count)
    row_flat = neighbour_row.reshape(request_count)
    owner_hits = (owner_flat[:, None] == jnp.arange(enc_count, dtype=jnp.int32)[None, :]).astype(
        jnp.int32
    )
    earlier = jnp.cumsum(owner_hits, axis=0) - owner_hits
    slot_index = jnp.sum(earlier * owner_hits, axis=1)
    position = owner_flat * capacity + slot_index
    slot_match = (position[None, :] == jnp.arange(slot_count, dtype=jnp.int32)[:, None]).astype(
        jnp.int32
    )
    filled = jnp.sum(slot_match, axis=1)
    source = jnp.sum(slot_match * jnp.arange(request_count, dtype=jnp.int32)[None, :], axis=1)
    wanted = jnp.where(filled > 0, jnp.take(row_flat, source, axis=0), -1).reshape(
        enc_count, capacity
    )
    asked = lax.all_to_all(wanted, "enc", split_axis=0, concat_axis=0, tiled=True).reshape(
        slot_count
    )
    safe_rows = jnp.maximum(asked, 0)
    collect = (asked[None, :] == jnp.arange(stored, dtype=jnp.int32)[:, None]).astype(jnp.bfloat16)

    def accumulate(terms):
        summed = jnp.dot(
            collect,
            terms.reshape(slot_count, nbr_tokens * feature_width),
            preferred_element_type=jnp.float32,
        )
        return summed.reshape(neighbour_keys.shape).astype(jnp.bfloat16)

    sent_keys = jnp.take(neighbour_keys, safe_rows, axis=0).reshape(
        enc_count, capacity, nbr_tokens, feature_width
    )
    sent_values = jnp.take(neighbour_values, safe_rows, axis=0).reshape(
        enc_count, capacity, nbr_tokens, feature_width
    )
    got_keys, got_values = (
        lax.all_to_all(sent_keys, "enc", split_axis=0, concat_axis=0, tiled=True),
        lax.all_to_all(sent_values, "enc", split_axis=0, concat_axis=0, tiled=True),
    )
    pair_keys = by_request(got_keys, position, group_count)
    pair_values = by_request(got_values, position, group_count)
    pair_query = pair_up(query_groups)
    pair_out, pair_peak, pair_total = jax.vmap(jax.vmap(partial_attend))(
        pair_query, pair_keys, pair_values
    )
    combined, log_total = combine(
        (pair_out[:, 0], pair_peak[:, 0], pair_total[:, 0]),
        (pair_out[:, 1], pair_peak[:, 1], pair_total[:, 1]),
    )
    delta_rows = row_delta(cot_groups, combined)
    pair_grads = jax.vmap(jax.vmap(partial_grad))(
        pair_query,
        pair_keys,
        pair_values,
        pair_up(cot_groups),
        pair_up(log_total),
        pair_up(delta_rows),
    )
    grad_query = pair_grads[0][:, 0] + pair_grads[0][:, 1]
    key_flat = pair_grads[1].reshape(request_count, nbr_tokens, feature_width)
    value_flat = pair_grads[2].reshape(request_count, nbr_tokens, feature_width)
    key_send = jnp.take(key_flat, source, axis=0).reshape(
        enc_count, capacity, nbr_tokens, feature_width
    )
    value_send = jnp.take(value_flat, source, axis=0).reshape(
        enc_count, capacity, nbr_tokens, feature_width
    )
    back_keys, back_values = (
        lax.all_to_all(key_send, "enc", split_axis=0, concat_axis=0, tiled=True),
        lax.all_to_all(value_send, "enc", split_axis=0, concat_axis=0, tiled=True),
    )
    grad_keys = accumulate(back_keys)
    grad_values = accumulate(back_values)
    attended = combined.astype(jnp.bfloat16).reshape(tok_rows, feature_width)
    grad_query = grad_query.astype(jnp.bfloat16).reshape(tok_rows, feature_width)
    grad_hidden = lax.dot_general(
        grad_query, weights, (((1,), (1,)), ((), ())), preferred_element_type=jnp.float32
    ).astype(jnp.bfloat16)
    return (attended, grad_hidden, grad_keys, grad_values)


def solution(mesh):
    in_specs = (
        P(("enc", "fsdp"), None),
        P("fsdp", None),
        P(("enc", "fsdp"), None, None),
        P(("enc", "fsdp"), None, None),
        P(("enc", "fsdp"), None),
        P(("enc", "fsdp"), None),
        P(("enc", "fsdp"), None),
    )
    out_specs = (
        P(("enc", "fsdp"), None),
        P(("enc", "fsdp"), None),
        P(("enc", "fsdp"), None, None),
        P(("enc", "fsdp"), None, None),
    )
    return jax.shard_map(
        per_device, mesh=mesh, in_specs=in_specs, out_specs=out_specs, check_vma=False
    )
```

profile of v0, /device:TPU:106, one launch (start us, length us, event | category | flops | bytes accessed | tf_op | source)
XLA Modules:
  0.0 325.6 jit_solution(4076497601142207396)
XLA Ops:
  11.1 8.5 %all_to_all.26 = s32[4,1,2]{2,1,0:T(1,128)S(1)} all-to-all(s32[4,1,2]{2,1,0:T(1,128)S(1)} %bitcast.204), channel_id=1, replica_groups=mesh['enc'=4,'fsdp'=32] {'enc'}, dimensions={0} | all-to-all | bytes 64 | tf_op jit(solution)/shard_map/all_to_all | solution.py:137
  23.7 4.7 %gather_fusion.3 = bf16[8,128,2048]{2,1,0:T(8,128)(2,1)} fusion(bf16[6,128,2048]{2,1,0:T(8,128)(2,1)} %param.13, s32[1024]{0:T(1024)S(1)} %pad_clamp_fusion.2), kind=kCustom, calls=%fused_computation.2.clone | custom fusion | bytes 8388640 | tf_op jit(solution)/shard_map/jit(_take)/gather | solution.py:151
  28.4 6.3 %broadcast_select_fusion.3 = (bf16[8,128,2048]{2,1,0:T(8,128)(2,1)S(1)}, bf16[8,128,2048]{2,1,0:T(8,128)(2,1)}) fusion(bf16[8,128,2048]{2,1,0:T(8,128)(2,1)} %gather_fusion.1, pred[8]{0:T(512)(128)(4,1)S(1)} %broadcast_compare_fusion, bf16[8,128,2048]{2,1,0:T(8,128)(2,1)} %gather_fusion.3), kind=kLoop, calls=%fused_computation.11 | loop fusion | flops 4194304 | bytes 16777224 | tf_op jit(solution)/shard_map/jit(_take)/select_n | solution.py:154
  34.6 51.1 %all_to_all.27 = bf16[4,2,128,2048]{3,2,1,0:T(8,128)(2,1)} all-to-all(bf16[4,2,128,2048]{3,2,1,0:T(8,128)(2,1)S(1)} %bitcast.180), channel_id=1, replica_groups=mesh['enc'=4,'fsdp'=32] {'enc'}, dimensions={0} | all-to-all | bytes 8388608 | tf_op jit(solution)/shard_map/all_to_all | solution.py:159
  85.8 6.4 %all-to-all-start.2 = ((bf16[4,2,128,2048]{3,2,1,0:T(8,128)(2,1)}), bf16[4,2,128,2048]{3,2,1,0:T(8,128)(2,1)}, u32[]{:S(2)}, u32[]{:S(2)}) async-start(bf16[4,2,128,2048]{3,2,1,0:T(8,128)(2,1)} %bitcast.179), calls=%async_computation.2 | async-start | bytes 8388608 | tf_op jit(solution)/shard_map/all_to_all | solution.py:158
  96.5 40.7 %all-to-all-done.2 = bf16[4,2,128,2048]{3,2,1,0:T(8,128)(2,1)} async-done(((bf16[4,2,128,2048]{3,2,1,0:T(8,128)(2,1)}), bf16[4,2,128,2048]{3,2,1,0:T(8,128)(2,1)}, u32[]{:S(2)}, u32[]{:S(2)}) %all-to-all-start.2) | async-done | bytes 4194336 | tf_op jit(solution)/shard_map/all_to_all | solution.py:158
  137.2 4.7 %gather_fusion.4 = bf16[6,128,2048]{2,1,0:T(8,128)(2,1)} fusion(bf16[8,128,2048]{2,1,0:T(8,128)(2,1)} %bitcast.7, s32[1024]{0:T(1024)S(1)} %pad_clamp_fusion.1), kind=kCustom, calls=%fused_computation.5.clone | custom fusion | bytes 6291480 | tf_op jit(solution)/shard_map/jit(_take)/gather | solution.py:90
  141.9 5.2 %broadcast_select_fusion.5 = (bf16[6,128,2048]{2,1,0:T(8,128)(2,1)}, bf16[6,128,2048]{2,1,0:T(8,128)(2,1)}) fusion(bf16[6,128,2048]{2,1,0:T(8,128)(2,1)S(1)} %gather_fusion.2, pred[6]{0:T(512)(128)(4,1)S(1)} %get-tuple-element.35, bf16[6,128,2048]{2,1,0:T(8,128)(2,1)} %gather_fusion.4), kind=kLoop, calls=%fused_computation.22 | loop fusion | flops 3145728 | bytes 12582918 | tf_op jit(solution)/shard_map/jit(_take)/select_n | solution.py:90
  147.1 4.8 %copy.130 = bf16[6,128,2048]{1,2,0:T(8,128)(2,1)} copy(bf16[6,128,2048]{2,1,0:T(8,128)(2,1)} %get-tuple-element.42) | data formatting | bytes 6291456 | tf_op jit(solution)/shard_map/jit(_take)/select_n | solution.py:90
  154.7 9.7 %fusion.18 = bf16[24,8,16,128]{3,1,2,0:T(8,128)(2,1)S(1)} fusion(bf16[192,4096]{1,0:T(8,128)(2,1)} %param.11, bf16[4096,2048]{1,0:T(8,128)(2,1)} %all-gather.2.cloned.1.call-done), kind=kOutput, calls=%fused_computation.49 | convolution fusion | flops 3221618688 | bytes 19136512 | tf_op jit(solution)/shard_map/dot_general | solution.py:118
  169.8 3.8 %convolution_bitcast_fusion.1 = f32[3,2,16,8,8,128]{5,4,3,2,1,0:T(8,128)S(1)} fusion(bf16[3,2,128,16,128]{2,4,3,1,0:T(8,128)(2,1)} %bitcast.175, f32[3,2,16,64,128]{4,3,2,1,0:T(8,128)S(1)} %get-tuple-element.46, f32[3,2,16,64]{3,2,1,0:T(8,128)S(1)} %get-tuple-element.45), kind=kOutput, calls=%fused_computation.31 | convolution fusion | flops 203685888 | bytes 9461760 | tf_op jit(solution)/shard_map/vmap(vmap(hcl,lhd->chd))/dot_general | solution.py:30
  179.9 4.5 %convolution_convert_fusion.4 = bf16[3,2,16,128,128]{3,4,2,1,0:T(8,128)(2,1)} fusion(f32[3,2,16,64,128]{4,3,2,1,0:T(8,128)S(1)} %get-tuple-element.46, f32[3,2,16,64]{3,2,1,0:T(8,128)S(1)} %broadcast_bitcast_fusion.1, bf16[3,64,16,128]{3,1,2,0:T(8,128)(2,1)} %copy.143), kind=kOutput, calls=%fused_computation.28 | convolution fusion | flops 205258752 | bytes 7102464 | tf_op jit(solution)/shard_map/vmap(vmap(hcl,chd->lhd))/dot_general | solution.py:62
  188.0 4.9 %gather_fusion.6 = bf16[8,128,2048]{1,2,0:T(8,128)(2,1)} fusion(bf16[6,128,2048]{1,2,0:T(8,128)(2,1)} %bitcast.178, s32[1024]{0:T(1024)S(1)} %pad_clamp_fusion), kind=kCustom, calls=%fused_computation.4.clone | custom fusion | bytes 8388640 | tf_op jit(solution)/shard_map/jit(_take)/gather | solution.py:186
  195.9 7.5 %broadcast_select_fusion = (bf16[8,128,2048]{1,2,0:T(8,128)(2,1)}, bf16[8,128,2048]{1,2,0:T(8,128)(2,1)}) fusion(bf16[8,128,2048]{1,2,0:T(8,128)(2,1)} %gather_fusion.6, pred[8]{0:T(512)(128)(4,1)S(1)} %get-tuple-element.47, bf16[8,128,2048]{1,2,0:T(8,128)(2,1)} %gather_fusion.5), kind=kLoop, calls=%fused_computation.8 | loop fusion | flops 4194304 | bytes 16777224 | tf_op jit(solution)/shard_map/jit(_take)/select_n | solution.py:186
  203.4 6.5 %copy.148 = bf16[8,128,2048]{2,1,0:T(8,128)(2,1)} copy(bf16[8,128,2048]{1,2,0:T(8,128)(2,1)} %get-tuple-element.40) | data formatting | bytes 8388608 | tf_op jit(solution)/shard_map/jit(_take)/select_n | solution.py:183
  209.9 6.3 %all-to-all-start.3 = ((bf16[4,2,128,2048]{3,2,1,0:T(8,128)(2,1)}), bf16[4,2,128,2048]{3,2,1,0:T(8,128)(2,1)}, u32[]{:S(2)}, u32[]{:S(2)}) async-start(bf16[4,2,128,2048]{3,2,1,0:T(8,128)(2,1)} %bitcast.182), calls=%async_computation.3 | async-start | bytes 8388608 | tf_op jit(solution)/shard_map/all_to_all | solution.py:190
  216.1 6.5 %copy.149 = bf16[8,128,2048]{2,1,0:T(8,128)(2,1)} copy(bf16[8,128,2048]{1,2,0:T(8,128)(2,1)} %get-tuple-element.39) | data formatting | bytes 8388608 | tf_op jit(solution)/shard_map/jit(_take)/select_n | solution.py:186
  222.7 37.6 %all-to-all-done.3 = bf16[4,2,128,2048]{3,2,1,0:T(8,128)(2,1)} async-done(((bf16[4,2,128,2048]{3,2,1,0:T(8,128)(2,1)}), bf16[4,2,128,2048]{3,2,1,0:T(8,128)(2,1)}, u32[]{:S(2)}, u32[]{:S(2)}) %all-to-all-start.3) | async-done | bytes 4194336 | tf_op jit(solution)/shard_map/all_to_all | solution.py:190
  260.3 6.6 %all-to-all-start.4 = ((bf16[4,2,128,2048]{3,2,1,0:T(8,128)(2,1)}), bf16[4,2,128,2048]{3,2,1,0:T(8,128)(2,1)}, u32[]{:S(2)}, u32[]{:S(2)}) async-start(bf16[4,2,128,2048]{3,2,1,0:T(8,128)(2,1)} %bitcast.181), calls=%async_computation.4 | async-start | bytes 8388608 | tf_op jit(solution)/shard_map/all_to_all | solution.py:191
  276.5 12.8 %convolution_convert_fusion = bf16[192,4096]{1,0:T(8,128)(2,1)} fusion(bf16[192,2048]{1,0:T(8,128)(2,1)} %bitcast.199, bf16[4096,2048]{1,0:T(8,128)(2,1)} %all-gather.2.cloned.1.call-done), kind=kOutput, calls=%fused_computation.7 | convolution fusion | flops 3222011904 | bytes 19136512 | tf_op jit(solution)/shard_map/dot_general | solution.py:197
  289.4 5.1 %convolution_convert_fusion.2 = bf16[6,128,2048]{2,0,1:T(8,128)(2,1)S(1)} fusion(s32[8]{0:T(128)S(1)} %reshape.250, bf16[1,8,128,2048]{3,2,1,0:T(8,128)(2,1)} %bitcast.76), kind=kOutput, calls=%fused_computation.13 | convolution fusion | flops 26738736 | bytes 7340064 | tf_op jit(solution)/shard_map/dot_general | solution.py:144
  294.4 3.6 %copy.150 = bf16[6,128,2048]{2,1,0:T(8,128)(2,1)} copy(bf16[6,128,2048]{2,0,1:T(8,128)(2,1)S(1)} %convolution_convert_fusion.2) | data formatting | bytes 6291456
  298.1 12.0 %all-to-all-done.4 = bf16[4,2,128,2048]{3,2,1,0:T(8,128)(2,1)} async-done(((bf16[4,2,128,2048]{3,2,1,0:T(8,128)(2,1)}), bf16[4,2,128,2048]{3,2,1,0:T(8,128)(2,1)}, u32[]{:S(2)}, u32[]{:S(2)}) %all-to-all-start.4) | async-done | bytes 4194336 | tf_op jit(solution)/shard_map/all_to_all | solution.py:191
  310.1 5.2 %convolution_convert_fusion.1 = bf16[6,128,2048]{2,0,1:T(8,128)(2,1)S(1)} fusion(s32[8]{0:T(128)S(1)} %reshape.250, bf16[1,8,128,2048]{3,2,1,0:T(8,128)(2,1)} %bitcast.79), kind=kOutput, calls=%fused_computation.12 | convolution fusion | flops 26738736 | bytes 7340064 | tf_op jit(solution)/shard_map/dot_general | solution.py:144
  (98 shorter events, 46.1 us)
Async XLA Ops:
  7.2 13.8 %copy-start = (bf16[6,128,2048]{2,1,0:T(8,128)(2,1)S(1)}, bf16[6,128,2048]{2,1,0:T(8,128)(2,1)}, u32[]{:S(2)}) copy-start(bf16[6,128,2048]{2,1,0:T(8,128)(2,1)} %param.14) | copy-start | bytes 9437188
  7.2 147.5 %all-gather.2.cloned.1.call-start = ((), (), s32[]{:S(2)}) async-start(), calls=%async_computation.5 | async-start | bytes 17301504 | tf_op jit(solution)/shard_map/all_gather | solution.py:117
  85.8 6.4 %copy-start.16 = (bf16[192,2048]{1,0:T(8,128)(2,1)S(1)}, bf16[192,2048]{1,0:T(8,128)(2,1)}, u32[]{:S(2)}) copy-start(bf16[192,2048]{1,0:T(8,128)(2,1)} %param.17) | copy-start | bytes 2359300
  85.8 51.5 %all-to-all-start.2 = ((bf16[4,2,128,2048]{3,2,1,0:T(8,128)(2,1)}), bf16[4,2,128,2048]{3,2,1,0:T(8,128)(2,1)}, u32[]{:S(2)}, u32[]{:S(2)}) async-start(bf16[4,2,128,2048]{3,2,1,0:T(8,128)(2,1)} %bitcast.179), calls=%async_computation.2 | async-start | bytes 8388608 | tf_op jit(solution)/shard_map/all_to_all | solution.py:158
  92.3 1.2 copy-start.14
  147.1 4.8 %copy-start.10 = (bf16[6,128,2048]{2,1,0:T(8,128)(2,1)S(1)}, bf16[6,128,2048]{2,1,0:T(8,128)(2,1)}, u32[]{:S(2)}) copy-start(bf16[6,128,2048]{2,1,0:T(8,128)(2,1)} %get-tuple-element.41) | copy-start | bytes 9437188
  164.4 2.2 copy-start.2
  164.8 2.8 copy-start.11
  174.4 1.2 copy-start.6
  174.4 1.7 copy-start.8
  174.4 1.7 copy-start.15
  179.9 4.5 %copy-start.4 = (bf16[6,128,2048]{1,2,0:T(8,128)(2,1)S(1)}, bf16[6,128,2048]{1,2,0:T(8,128)(2,1)}, u32[]{:S(2)}) copy-start(bf16[6,128,2048]{1,2,0:T(8,128)(2,1)} %copy.128) | copy-start | bytes 9437188
  179.9 4.5 %copy-start.13 = (bf16[3,64,16,128]{3,1,2,0:T(8,128)(2,1)S(1)}, bf16[3,64,16,128]{3,1,2,0:T(8,128)(2,1)}, u32[]{:S(2)}) copy-start(bf16[3,64,16,128]{3,1,2,0:T(8,128)(2,1)} %copy.143) | copy-start | bytes 2359300
  184.4 2.4 copy-start.12
  186.8 1.1 copy-start.5
  209.9 50.4 %all-to-all-start.3 = ((bf16[4,2,128,2048]{3,2,1,0:T(8,128)(2,1)}), bf16[4,2,128,2048]{3,2,1,0:T(8,128)(2,1)}, u32[]{:S(2)}, u32[]{:S(2)}) async-start(bf16[4,2,128,2048]{3,2,1,0:T(8,128)(2,1)} %bitcast.182), calls=%async_computation.3 | async-start | bytes 8388608 | tf_op jit(solution)/shard_map/all_to_all | solution.py:190
  260.3 6.6 %copy-start.3 = (bf16[6,128,2048]{1,2,0:T(8,128)(2,1)S(1)}, bf16[6,128,2048]{1,2,0:T(8,128)(2,1)}, u32[]{:S(2)}) copy-start(bf16[6,128,2048]{1,2,0:T(8,128)(2,1)} %copy.130) | copy-start | bytes 9437188
  260.3 49.8 %all-to-all-start.4 = ((bf16[4,2,128,2048]{3,2,1,0:T(8,128)(2,1)}), bf16[4,2,128,2048]{3,2,1,0:T(8,128)(2,1)}, u32[]{:S(2)}, u32[]{:S(2)}) async-start(bf16[4,2,128,2048]{3,2,1,0:T(8,128)(2,1)} %bitcast.181), calls=%async_computation.4 | async-start | bytes 8388608 | tf_op jit(solution)/shard_map/all_to_all | solution.py:191
  272.0 1.4 copy-start.7
  272.0 1.9 copy-start.9
  310.1 8.6 %copy-start.1 = (bf16[6,128,2048]{2,1,0:T(8,128)(2,1)S(1)}, bf16[6,128,2048]{2,1,0:T(8,128)(2,1)}, u32[]{:S(2)}) copy-start(bf16[6,128,2048]{2,1,0:T(8,128)(2,1)} %param.14) | copy-start | bytes 9437188
Sparse Core Ops, SparseCore 0:
  10.3 71.7 all-gather.1
where the time goes:
time: 330 us; the launch traced here: 326 us
  waiting for transfers between devices  91 us (28%)
  local copies, waits for them, and re-layouts  63.6 us (19%)
  blocking collectives  59.6 us (18%)
  matrix products  49.2 us (15%)
  other arithmetic  28.4 us (9%)
  starting transfers between devices  19.3 us (6%)
  between operations  14.4 us (4%)
    all_to_all x1, blocking collectives, per_device(): lax.all_to_all(sent_values, 'enc', split_axis=0, concat_axis=0, tiled=True)  51.1 us
    all_to_all x1, waiting for transfers between devices, per_device(): lax.all_to_all(sent_keys, 'enc', split_axis=0, concat_axis=0, tiled=True)  40.7 us
    all_to_all x1, waiting for transfers between devices, per_device(): lax.all_to_all(key_send, 'enc', split_axis=0, concat_axis=0, tiled=True)  37.6 us
    unnamed x42, local copies, waits for them, and re-layouts  13.2 us
    dot_general x1, matrix products, per_device(): lax.dot_general(grad_query, weights, (((1,), (1,)), ((), ())), preferred_...  12.8 us
    all_to_all x1, waiting for transfers between devices, per_device(): lax.all_to_all(value_send, 'enc', split_axis=0, concat_axis=0, tiled=True)  12 us
    dot_general x2, matrix products, accumulate(): jnp.dot(collect, terms.reshape(slot_count, nbr_tokens * feature_width), p...  10.3 us
    dot_general x1, matrix products, per_device(): jnp.dot(hidden, weights, preferred_element_type=jnp.float32)  9.67 us
  transfers between devices with their start and end apart: 4, of which 3 were waited for; matrix products, arithmetic and copies ran while one was open for 24% of the time, Pallas kernels for 0%

commit v1 on v0

v1 whole, which is shorter than its diff:
```python
import functools
import math

import jax
import jax.numpy as jnp
from jax import lax
from jax.experimental import pallas as pl
from jax.experimental.pallas import tpu as pltpu
from jax.sharding import PartitionSpec as P

HEAD = 128
LEN = 128
ROWS = 64
GROUPS = 3
STORED = 6
SLOTS = 8
WIDTH = 2048
SCALE = 1.0 / math.sqrt(HEAD)
F32 = jnp.float32
BF16 = jnp.bfloat16
ANY = pl.BlockSpec(memory_space=pltpu.HBM)
SMEM = pl.BlockSpec(memory_space=pltpu.SMEM)
VMEM = pl.BlockSpec(memory_space=pltpu.VMEM)
CHUNKS = 2
GANG = 8
STEP = 2048


def params(mib):
    return pltpu.CompilerParams(vmem_limit_bytes=mib << 20)


def cost(flops, data, exps=0):
    return pl.CostEstimate(flops=int(flops), bytes_accessed=int(data), transcendentals=int(exps))


def shape(dims, dtype):
    return jax.ShapeDtypeStruct(dims, dtype)


def dot(a, b, ca, cb):
    return lax.dot_general(a, b, (((ca,), (cb,)), ((), ())), preferred_element_type=F32)


def head(h):
    return slice(h * HEAD, (h + 1) * HEAD)


def route_kernel(me, owner, row, pick, want, place, count):
    for k in range(SLOTS):
        pick[k] = 0
        want[k] = -1
    for d in range(4):
        count[d] = 0
    for g in range(GROUPS):
        for j in range(2):
            d = (owner[g, j] - me[0] + 4) % 4
            k = d * 2 + jnp.minimum(count[d], 1)
            count[d] = count[d] + 1
            pick[k] = g
            want[k] = row[g, j]
            place[g * 2 + j] = k


def route(me, owner, row):
    return pl.pallas_call(
        route_kernel,
        out_shape=(shape((SLOTS,), jnp.int32), shape((SLOTS,), jnp.int32), shape((SLOTS,), jnp.int32)),
        in_specs=[SMEM] * 3,
        out_specs=(SMEM, SMEM, SMEM),
        scratch_shapes=[pltpu.SMEM((4,), jnp.int32)],
        name="route",
    )(me, owner, row)


def spread_kernel(pick, cot, *outs):
    for d in range(1, 4):
        for s in range(2):
            outs[d - 1][s] = cot[pick[2 * d + s]]


def spread(pick, cot):
    one = shape((2, ROWS, WIDTH), BF16)
    return pl.pallas_call(
        spread_kernel,
        out_shape=(one,) * 3,
        in_specs=[SMEM, VMEM],
        out_specs=(VMEM,) * 3,
        compiler_params=params(24),
        cost_estimate=cost(1, 20 * ROWS * WIDTH),
        name="spread",
    )(pick, cot)


def query_kernel(steps, pick, hid, w, q, s1, s2, s3, acc):
    i = pl.program_id(0)
    part = dot(hid[...], w[...], 1, 0)

    @pl.when(i == 0)
    def _():
        acc[...] = part

    @pl.when(i > 0)
    def _():
        acc[...] += part

    @pl.when(i == steps - 1)
    def _():
        for g in range(GROUPS):
            q[g] = acc[g * ROWS : (g + 1) * ROWS].astype(BF16)
        for d, out in ((1, s1), (2, s2), (3, s3)):
            for s in range(2):
                out[s] = q[pick[2 * d + s]]


def query(pick, hidden, weights, col, cw):
    depth = hidden.shape[1]
    step = STEP
    steps = depth // step
    c = col // cw
    const = lambda i: (0, 0, 0)
    piece = shape((2, ROWS, cw), BF16)
    return pl.pallas_call(
        functools.partial(query_kernel, steps),
        out_shape=(shape((GROUPS, ROWS, cw), BF16), piece, piece, piece),
        grid=(steps,),
        in_specs=[
            SMEM,
            pl.BlockSpec((GROUPS * ROWS, step), lambda i: (0, i)),
            pl.BlockSpec((step, cw), lambda i: (i, c)),
        ],
        out_specs=(pl.BlockSpec((GROUPS, ROWS, cw), const),) + (pl.BlockSpec((2, ROWS, cw), const),) * 3,
        scratch_shapes=[pltpu.VMEM((GROUPS * ROWS, cw), F32)],
        compiler_params=params(48),
        cost_estimate=cost(2 * 192 * depth * cw, 2 * depth * (192 + cw)),
        name="query",
    )(pick, hidden, weights)


def slot_copies(k, pick, rows, q, c, keys, values, bufs, sems, col, cw):
    d, s = divmod(k, 2)
    cols = pl.ds(col, cw)
    at = pick[k] if d == 0 else s
    row = jnp.maximum(rows[k], 0)
    qb, cb, kb, vb = bufs
    out = [
        pltpu.make_async_copy(q[d].at[at], qb.at[k], sems.at[k, 0]),
        pltpu.make_async_copy(c[d].at[at, :, cols], cb.at[k], sems.at[k, 1]),
    ]
    if keys is not None:
        out += [
            pltpu.make_async_copy(keys.at[row, :, cols], kb.at[k], sems.at[k, 2]),
            pltpu.make_async_copy(values.at[row, :, cols], vb.at[k], sems.at[k, 3]),
        ]
    return out


def wait_slot(k, bufs, sems):
    for n, buf in enumerate(bufs):
        pltpu.make_async_copy(buf.at[k], buf.at[k], sems.at[k, n]).wait()


def rows_of(k, asked):
    d, s = divmod(k, 2)
    return asked[d][2 * d + s]


def fill_rows(asked, rows):
    for k in range(SLOTS):
        rows[k] = rows_of(k, asked)


def forward_kernel(col, cw, *refs):
    pick, asked, refs = refs[0], refs[1:5], refs[5:]
    q, c, keys, values = refs[:4], refs[4:8], refs[8], refs[9]
    p, st = refs[10:14], refs[14:18]
    rows, qb, cb, kb, vb, pb, sb, sems, osems = refs[18:]
    fill_rows(asked, rows)
    bufs = (qb, cb, kb, vb)
    for k in range(SLOTS):
        for one in slot_copies(k, pick, rows, q, c, keys, values, bufs, sems, col, cw):
            one.start()
    lane = lax.broadcasted_iota(jnp.int32, (ROWS, HEAD), 1)
    heads = cw // HEAD

    @pl.loop(0, SLOTS)
    def _(k):
        wait_slot(k, bufs, sems)

        @pl.when(rows[k] >= 0)
        def _():
            stats = jnp.zeros((ROWS, HEAD), F32)
            for base in range(0, heads, GANG):
                span = range(base, base + GANG)
                vals = [vb[k, :, head(h)] for h in span]
                scores = [dot(qb[k, :, head(h)], kb[k, :, head(h)], 1, 1) * SCALE for h in span]
                peaks = [jnp.max(x, axis=1, keepdims=True) for x in scores]
                exps = [jnp.exp(x - m) for x, m in zip(scores, peaks)]
                totals = [jnp.sum(x, axis=1, keepdims=True) for x in exps]
                rounded = [x.astype(BF16) for x in exps]
                parts = [dot(x, v, 1, 0) for x, v in zip(rounded, vals)]
                mixed = [jnp.sum(cb[k, :, head(h)].astype(F32) * x, axis=1, keepdims=True) for h, x in zip(span, parts)]
                for n, h in enumerate(span):
                    stats = jnp.where(lane == h, peaks[n], stats)
                    stats = jnp.where(lane == heads + h, totals[n], stats)
                    stats = jnp.where(lane == 2 * heads + h, mixed[n], stats)
                    pb[k, :, head(h)] = parts[n].astype(BF16)
            sb[k] = stats

    copies = []
    for k in range(SLOTS):
        d, s = divmod(k, 2)
        copies.append(pltpu.make_async_copy(sb.at[k], st[d].at[s], osems.at[k, 0]))
        copies.append(pltpu.make_async_copy(pb.at[k], p[d].at[s], osems.at[k, 1]))
    for one in copies:
        one.start()
    for one in copies:
        one.wait()


def forward(pick, asked, q, c, keys, values, col, cw):
    piece = shape((2, ROWS, cw), BF16)
    small = shape((2, ROWS, HEAD), F32)
    return pl.pallas_call(
        functools.partial(forward_kernel, col, cw),
        out_shape=(piece,) * 4 + (small,) * 4,
        in_specs=[SMEM] * 5 + [ANY] * 10,
        out_specs=(ANY,) * 8,
        scratch_shapes=[
            pltpu.SMEM((SLOTS,), jnp.int32),
            pltpu.VMEM((SLOTS, ROWS, cw), BF16),
            pltpu.VMEM((SLOTS, ROWS, cw), BF16),
            pltpu.VMEM((SLOTS, LEN, cw), BF16),
            pltpu.VMEM((SLOTS, LEN, cw), BF16),
            pltpu.VMEM((SLOTS, ROWS, cw), BF16),
            pltpu.VMEM((SLOTS, ROWS, HEAD), F32),
            pltpu.SemaphoreType.DMA((SLOTS, 4)),
            pltpu.SemaphoreType.DMA((SLOTS, 2)),
        ],
        compiler_params=params(48),
        cost_estimate=cost(SLOTS * 6 * ROWS * LEN * cw, SLOTS * 8 * LEN * cw, SLOTS * ROWS * cw),
        name="forward",
    )(pick, *asked, *q, *c, keys, values)


def backward_kernel(col, cw, *refs):
    pick, asked, refs = refs[0], refs[1:5], refs[5:]
    q, c, keys, values, back = refs[:4], refs[4:8], refs[8], refs[9], refs[10:14]
    gq, gs, pr = refs[14:18], refs[18], refs[19]
    rows, qb, cb, kb, vb, bb, gb, sems, osems = refs[20:]
    fill_rows(asked, rows)
    bufs = (qb, cb, kb, vb, bb)
    for k in range(SLOTS):
        d, s = divmod(k, 2)
        pltpu.make_async_copy(back[d].at[s], bb.at[k], sems.at[k, 4]).start()
        for one in slot_copies(k, pick, rows, q, c, keys, values, bufs[:4], sems, col, cw):
            one.start()
    heads = cw // HEAD

    @pl.loop(0, SLOTS)
    def _(k):
        wait_slot(k, bufs, sems)

        @pl.when(rows[k] >= 0)
        def _():
            stats = bb[k]
            for base in range(0, heads, GANG):
                span = range(base, base + GANG)
                ks = [kb[k, :, head(h)] for h in span]
                scores = [dot(qb[k, :, head(h)], x, 1, 1) * SCALE for h, x in zip(span, ks)]
                grads = [dot(cb[k, :, head(h)], vb[k, :, head(h)], 1, 1) for h in span]
                probs = [jnp.exp(x - stats[:, h : h + 1]) for h, x in zip(span, scores)]
                terms = [
                    (x * (y - stats[:, heads + h : heads + h + 1]) * SCALE).astype(BF16)
                    for h, x, y in zip(span, probs, grads)
                ]
                parts = [dot(x, y, 1, 0) for x, y in zip(terms, ks)]
                for n, h in enumerate(span):
                    pr[k, :, head(h)] = probs[n].astype(BF16)
                    gs[k, :, head(h)] = terms[n]
                    gb[k, :, head(h)] = parts[n].astype(BF16)

    copies = []
    for k in range(SLOTS):
        d, s = divmod(k, 2)
        copies.append(pltpu.make_async_copy(gb.at[k], gq[d].at[s], osems.at[k]))
    for one in copies:
        one.start()
    for one in copies:
        one.wait()


def backward(pick, asked, q, c, keys, values, back, col, cw):
    piece = shape((2, ROWS, cw), BF16)
    every = shape((SLOTS, ROWS, cw), BF16)
    return pl.pallas_call(
        functools.partial(backward_kernel, col, cw),
        out_shape=(piece,) * 4 + (every,) * 2,
        in_specs=[SMEM] * 5 + [ANY] * 14,
        out_specs=(ANY,) * 4 + (VMEM,) * 2,
        scratch_shapes=[
            pltpu.SMEM((SLOTS,), jnp.int32),
            pltpu.VMEM((SLOTS, ROWS, cw), BF16),
            pltpu.VMEM((SLOTS, ROWS, cw), BF16),
            pltpu.VMEM((SLOTS, LEN, cw), BF16),
            pltpu.VMEM((SLOTS, LEN, cw), BF16),
            pltpu.VMEM((SLOTS, ROWS, HEAD), F32),
            pltpu.VMEM((SLOTS, ROWS, cw), BF16),
            pltpu.SemaphoreType.DMA((SLOTS, 5)),
            pltpu.SemaphoreType.DMA((SLOTS,)),
        ],
        compiler_params=params(48),
        cost_estimate=cost(SLOTS * 6 * ROWS * LEN * cw, SLOTS * 8 * LEN * cw, SLOTS * ROWS * cw),
        name="backward",
    )(pick, *asked, *q, *c, keys, values, *back)


def terms_kernel(col, cw, first, *refs):
    pick, asked, refs = refs[0], refs[1:5], refs[5:]
    q, c, gs, pr = refs[:4], refs[4:8], refs[8], refs[9]
    refs = refs[10:] if first else refs[12:]
    dk, dv, rows, qb, cb, ak, av, sems = refs
    fill_rows(asked, rows)
    bufs = (qb, cb)
    for k in range(SLOTS):
        for one in slot_copies(k, pick, rows, q, c, None, None, (qb, cb, None, None), sems, col, cw):
            one.start()
    ak[...] = jnp.zeros_like(ak)
    av[...] = jnp.zeros_like(av)

    @pl.loop(0, SLOTS)
    def _(k):
        wait_slot(k, bufs, sems)

        @pl.when(rows[k] >= 0)
        def _():
            row = jnp.maximum(rows[k], 0)
            for h in range(cw // HEAD):
                kt = dot(gs[k, :, head(h)], qb[k, :, head(h)], 0, 0)
                vt = dot(pr[k, :, head(h)], cb[k, :, head(h)], 0, 0)
                ak[row, :, head(h)] += kt.astype(BF16).astype(F32)
                av[row, :, head(h)] += vt.astype(BF16).astype(F32)

    dk[...] = ak[...].astype(BF16)
    dv[...] = av[...].astype(BF16)


def terms(pick, asked, q, c, gs, pr, before, col, cw):
    whole = shape((STORED, LEN, WIDTH), BF16)
    out = pl.BlockSpec((STORED, LEN, cw), lambda i: (0, 0, col // cw))
    first = before is None
    args = (pick, *asked, *q, *c, gs, pr) + (() if first else before)
    return pl.pallas_call(
        functools.partial(terms_kernel, col, cw, first),
        out_shape=(whole,) * 2,
        grid=(1,),
        in_specs=[SMEM] * 5 + [ANY] * 8 + [VMEM] * 2 + ([] if first else [ANY] * 2),
        out_specs=(out,) * 2,
        scratch_shapes=[
            pltpu.SMEM((SLOTS,), jnp.int32),
            pltpu.VMEM((SLOTS, ROWS, cw), BF16),
            pltpu.VMEM((SLOTS, ROWS, cw), BF16),
            pltpu.VMEM((STORED, LEN, cw), F32),
            pltpu.VMEM((STORED, LEN, cw), F32),
            pltpu.SemaphoreType.DMA((SLOTS, 2)),
        ],
        input_output_aliases={} if first else {15: 0, 16: 1},
        compiler_params=params(56),
        cost_estimate=cost(SLOTS * 4 * ROWS * LEN * cw, SLOTS * 8 * ROWS * cw + 24 * LEN * cw),
        name="terms",
    )(*args)


def settle_kernel(heads, pick, place, s0, s1, s2, s3, b0, b1, b2, b3, weight, sb, res):
    for d, ref in enumerate((s0, s1, s2, s3)):
        for s in range(2):
            sb[2 * d + s] = ref[s]
    lane = lax.broadcasted_iota(jnp.int32, (ROWS, HEAD), 1)
    for g in range(GROUPS):
        x, y = sb[place[2 * g]], sb[place[2 * g + 1]]
        move = lambda a, n: pltpu.roll(a, (HEAD - n * heads) % HEAD, 1)
        keep = lane < heads
        px, py = jnp.where(keep, x, 0.0), jnp.where(keep, y, 0.0)
        tx = jnp.where(keep, move(x, 1), 1.0)
        ty = jnp.where(keep, move(y, 1), 1.0)
        mx = jnp.where(keep, move(x, 2), 0.0)
        my = jnp.where(keep, move(y, 2), 0.0)
        top = jnp.maximum(px, py)
        ax, ay = jnp.exp(px - top), jnp.exp(py - top)
        total = ax * tx + ay * ty
        log_total = top + jnp.log(total)
        delta = (ax * mx + ay * my) / total
        res[g] = jnp.where(keep, log_total, pltpu.roll(delta, heads, 1))
        weight[g] = jnp.where(keep, ax / total, pltpu.roll(ay / total, heads, 1))
    for d, ref in enumerate((b0, b1, b2, b3)):
        for s in range(2):
            ref[s] = res[pick[2 * d + s]]


def settle(pick, place, stats, heads):
    small = shape((2, ROWS, HEAD), F32)
    return pl.pallas_call(
        functools.partial(settle_kernel, heads),
        out_shape=(small,) * 4 + (shape((GROUPS, ROWS, HEAD), F32),),
        in_specs=[SMEM] * 2 + [VMEM] * 4,
        out_specs=(VMEM,) * 5,
        scratch_shapes=[pltpu.VMEM((SLOTS, ROWS, HEAD), F32), pltpu.VMEM((GROUPS, ROWS, HEAD), F32)],
        cost_estimate=cost(1e5, 1e6, 1e5),
        name="settle",
    )(pick, place, *stats)


def attend_kernel(heads, first, place, p0, p1, p2, p3, weight, *refs):
    out, pb = refs if first else refs[1:]
    for d, ref in enumerate((p0, p1, p2, p3)):
        for s in range(2):
            pb[2 * d + s] = ref[s]
    for g in range(GROUPS):
        a, b = place[2 * g], place[2 * g + 1]
        w = weight[g]
        for h in range(heads):
            x = pb[a, :, head(h)].astype(F32) * w[:, h : h + 1]
            y = pb[b, :, head(h)].astype(F32) * w[:, heads + h : heads + h + 1]
            out[g * ROWS : (g + 1) * ROWS, head(h)] = (x + y).astype(BF16)


def attend(place, p, weight, before, col, cw):
    first = before is None
    return pl.pallas_call(
        functools.partial(attend_kernel, cw // HEAD, first),
        out_shape=shape((GROUPS * ROWS, WIDTH), BF16),
        grid=(1,),
        in_specs=[SMEM] + [VMEM] * 5 + ([] if first else [ANY]),
        out_specs=pl.BlockSpec((GROUPS * ROWS, cw), lambda i: (0, col // cw)),
        scratch_shapes=[pltpu.VMEM((SLOTS, ROWS, cw), BF16)],
        input_output_aliases={} if first else {6: 0},
        compiler_params=params(32),
        cost_estimate=cost(1e6, 12 * ROWS * cw * 2),
        name="attend",
    )(place, *p, weight, *(() if first else (before,)))


def grad_kernel(first, last, place, g0, g1, g2, g3, w, *refs):
    before, refs = (None, refs) if first else (refs[0], refs[1:])
    out, gb, gq, sems = refs

    @pl.when(pl.program_id(0) == 0)
    def _():
        copies = []
        for d, ref in enumerate((g0, g1, g2, g3)):
            copies.append(pltpu.make_async_copy(ref, gb.at[pl.ds(2 * d, 2)], sems.at[d]))
        for one in copies:
            one.start()
        for one in copies:
            one.wait()
        for g in range(GROUPS):
            both = gb[place[2 * g]].astype(F32) + gb[place[2 * g + 1]].astype(F32)
            gq[g * ROWS : (g + 1) * ROWS] = both.astype(BF16)

    part = dot(gq[...], w[...], 1, 1)
    if not first:
        part = part + before[...]
    out[...] = part.astype(out.dtype)


def grad(place, g, weights, before, last, col, cw):
    depth = weights.shape[0]
    step = STEP
    first = before is None
    block = pl.BlockSpec((GROUPS * ROWS, step), lambda i: (0, i))
    return pl.pallas_call(
        functools.partial(grad_kernel, first, last),
        out_shape=shape((GROUPS * ROWS, depth), BF16 if last else F32),
        grid=(depth // step,),
        in_specs=[SMEM] + [ANY] * 4 + [pl.BlockSpec((step, cw), lambda i: (i, col // cw))] + ([] if first else [block]),
        out_specs=block,
        scratch_shapes=[
            pltpu.VMEM((SLOTS, ROWS, cw), BF16),
            pltpu.VMEM((GROUPS * ROWS, cw), BF16),
            pltpu.SemaphoreType.DMA((4,)),
        ],
        compiler_params=params(48),
        cost_estimate=cost(2 * 192 * depth * cw, 2 * depth * (384 + cw)),
        name="grad",
    )(place, *g, weights, *(() if first else (before,)))


def shift(x, d):
    return lax.ppermute(x, "enc", [(i, (i + d) % 4) for i in range(4)])


def to_owner(pieces):
    return [shift(x, d + 1) for d, x in enumerate(pieces)]


def to_home(pieces):
    return [shift(x, -(d + 1)) for d, x in enumerate(pieces)]


def per_device(hidden, query_weight, keys, values, owner, row, cotangent):
    me = lax.axis_index("enc").astype(jnp.int32).reshape(1)
    pick, want, place = route(me, owner, row)
    asked = [want] + to_owner([want] * 3)
    cot = cotangent.reshape(GROUPS, ROWS, WIDTH)
    c = [cot] + to_owner(spread(pick, cot))
    weights = lax.all_gather(query_weight, "fsdp", axis=0, tiled=True)
    cw = WIDTH // CHUNKS
    cols = [i * cw for i in range(CHUNKS)]
    qs, gqs, ps, scales = [], [], [], []
    for col in cols:
        q, *sends = query(pick, hidden, weights, col, cw)
        qs.append([q] + to_owner(sends))
    stats = []
    for col, q in zip(cols, qs):
        out = forward(pick, asked, q, c, keys, values, col, cw)
        ps.append([out[0]] + to_home(out[1:4]))
        stats.append([out[4]] + to_home(out[5:8]))
    grads, attended = None, None
    backs = []
    for col, q, st in zip(cols, qs, stats):
        *back, weight = settle(pick, place, st, cw // HEAD)
        backs.append([back[0]] + to_owner(back[1:4]))
        scales.append(weight)
    for col, q, back in zip(cols, qs, backs):
        out = backward(pick, asked, q, c, keys, values, back, col, cw)
        gqs.append([out[0]] + to_home(out[1:4]))
        grads = terms(pick, asked, q, c, out[4], out[5], grads, col, cw)
    for col, p, weight in zip(cols, ps, scales):
        attended = attend(place, p, weight, attended, col, cw)
    total = None
    for col, g in zip(cols, gqs):
        total = grad(place, g, weights, total, col == cols[-1], col, cw)
    return attended, total, grads[0], grads[1]


def solution(mesh):
    rows = P(("enc", "fsdp"), None)
    blocks = P(("enc", "fsdp"), None, None)
    return jax.shard_map(
        per_device,
        mesh=mesh,
        in_specs=(rows, P("fsdp", None), blocks, blocks, rows, rows, rows),
        out_specs=(rows, rows, blocks, blocks),
        check_vma=False,
    )
```

time: 330 us -> 262 us (0.79)
  the two profiles are of different devices: /device:TPU:106 before, /device:TPU:16 now
where the time goes in v1:
time: 262 us; the launch traced here: 260 us
  waiting for transfers between devices  87.8 us (34%)
  Pallas kernels  87.8 us (34%)
  starting transfers between devices  49.9 us (19%)
  local copies, waits for them, and re-layouts  20.2 us (8%)
  between operations  14.5 us (6%)
    all_gather x1, waiting for transfers between devices, per_device(): weights = lax.all_gather(query_weight, 'fsdp', axis=0, tiled=True)  66.9 us
    ppermute x36, starting transfers between devices, shift(): return lax.ppermute(x, 'enc', [(i, (i + d) % 4) for i in range(4)])  49.9 us
    pallas_call x2, Pallas kernels, backward(): pl.pallas_call(functools.partial(backward_kernel, col, cw), out_shape=(pi...  20.8 us
    unnamed x104, local copies, waits for them, and re-layouts  20.2 us
    ppermute x36, waiting for transfers between devices, shift(): return lax.ppermute(x, 'enc', [(i, (i + d) % 4) for i in range(4)])  20.2 us
    pallas_call x2, Pallas kernels, forward(): pl.pallas_call(functools.partial(forward_kernel, col, cw), out_shape=(pie...  19 us
    pallas_call x2, Pallas kernels, terms(): pl.pallas_call(functools.partial(terms_kernel, col, cw, first), out_shape...  15.4 us
    pallas_call x2, Pallas kernels, grad(): pl.pallas_call(functools.partial(grad_kernel, first, last), out_shape=sha...  12 us
  transfers between devices with their start and end apart: 37, of which 7 were waited for; matrix products, arithmetic and copies ran while one was open for 1% of the time, Pallas kernels for 31%

profile of v1, /device:TPU:16, one launch (start us, length us, event | category | flops | bytes accessed | tf_op | source)
XLA Modules:
  0.0 260.2 jit_solution(6519225908806994770)
XLA Ops:
  18.1 66.9 %all-gather.2.cloned.1.call-done.w = bf16[4096,2048]{1,0:T(8,128)(2,1)} async-done(((bf16[128,2048]{1,0:T(8,128)(2,1)}), bf16[4096,2048]{1,0:T(8,128)(2,1)}) %all-gather.2.cloned.1.call-update) | async-done | bytes 16777232 | tf_op jit(solution)/shard_map/all_gather | solution.py:506
  87.1 4.7 %query.3 = (bf16[3,64,1024]{2,1,0:T(8,128)(2,1)S(1)}, bf16[2,64,1024]{2,1,0:T(8,128)(2,1)S(1)}, bf16[2,64,1024]{2,1,0:T(8,128)(2,1)S(1)}, bf16[2,64,1024]{2,1,0:T(8,128)(2,1)S(1)}) custom-call(s32[8]{0:T(128)S(1)} %copy-done.32, bf16[192,4096]{1,0:T(8,128)(2,1)S(1)} %copy-done.5, bf16[4096,2048]{1,0:T(8,128)(2,1)} %all-gather.2.cloned.1.call-done.w), custom_call_target="tpu_custom_call" | custom-call | flops 1610612736 | bytes 9961472 | tf_op jit(solution)/shard_map/query/pallas_call | solution.py:123
  94.0 2.7 %collective-permute-done.2.refs_4_ = s32[8]{0:T(128)S(1)} collective-permute-done((s32[8]{0:T(128)S(1)}, s32[8]{0:T(128)S(1)}, u32[]{:S(2)}, u32[]{:S(2)}) %collective-permute-start.2) | collective-permute-done | bytes 64 | tf_op jit(solution)/shard_map/ppermute | solution.py:489
  97.5 4.2 %collective-permute-done.1.refs_3_ = s32[8]{0:T(128)S(1)} collective-permute-done((s32[8]{0:T(128)S(1)}, s32[8]{0:T(128)S(1)}, u32[]{:S(2)}, u32[]{:S(2)}) %collective-permute-start.1) | collective-permute-done | bytes 64 | tf_op jit(solution)/shard_map/ppermute | solution.py:489
  105.3 2.6 collective-permute-start.16
  108.4 4.7 %query.2 = (bf16[3,64,1024]{2,1,0:T(8,128)(2,1)S(1)}, bf16[2,64,1024]{2,1,0:T(8,128)(2,1)S(1)}, bf16[2,64,1024]{2,1,0:T(8,128)(2,1)S(1)}, bf16[2,64,1024]{2,1,0:T(8,128)(2,1)S(1)}) custom-call(s32[8]{0:T(128)S(1)} %copy-done.32, bf16[192,4096]{1,0:T(8,128)(2,1)S(1)} %copy-done.5, bf16[4096,2048]{1,0:T(8,128)(2,1)} %all-gather.2.cloned.1.call-done.w), custom_call_target="tpu_custom_call" | custom-call | flops 1610612736 | bytes 9961472 | tf_op jit(solution)/shard_map/query/pallas_call | solution.py:123
  117.7 4.0 %collective-permute-done.17.refs_8_ = bf16[2,64,1024]{2,1,0:T(8,128)(2,1)S(1)} collective-permute-done((bf16[2,64,1024]{2,1,0:T(8,128)(2,1)S(1)}, bf16[2,64,1024]{2,1,0:T(8,128)(2,1)S(1)}, u32[]{:S(2)}, u32[]{:S(2)}) %collective-permute-start.17) | collective-permute-done | bytes 262176 | tf_op jit(solution)/shard_map/ppermute | solution.py:489
  121.7 9.4 %forward.3 = (bf16[2,64,1024]{2,1,0:T(8,128)(2,1)S(1)}, bf16[2,64,1024]{2,1,0:T(8,128)(2,1)S(1)}, bf16[2,64,1024]{2,1,0:T(8,128)(2,1)S(1)}, bf16[2,64,1024]{2,1,...) custom-call(s32[8]{0:T(128)S(1)} %copy-done.32, ...), custom_call_target="tpu_custom_call" | custom-call | flops 402653184 | bytes 8388608 | tf_op jit(solution)/shard_map/forward/pallas_call | solution.py:224
  134.5 3.1 %collective-permute-start.22 = (f32[2,64,128]{2,1,0:T(8,128)S(1)}, f32[2,64,128]{2,1,0:T(8,128)S(1)}, u32[]{:S(2)}, u32[]{:S(2)}) collective-permute-start(f32[2,64,128]{2,1,0:T(8,128)S(1)} %get-tuple-element.89), channel_id=1, source_target_pairs={{0,64},{32,96},{64,0},{96,32},{1,65},{33,97},{65,1},{97,33},{2,66}... | collective-permute-start | bytes 196616 | tf_op jit(solution)/shard_map/ppermute | solution.py:489
  138.5 9.6 %forward.2 = (bf16[2,64,1024]{2,1,0:T(8,128)(2,1)S(1)}, bf16[2,64,1024]{2,1,0:T(8,128)(2,1)S(1)}, bf16[2,64,1024]{2,1,0:T(8,128)(2,1)S(1)}, bf16[2,64,1024]{2,1,...) custom-call(s32[8]{0:T(128)S(1)} %copy-done.32, ...), custom_call_target="tpu_custom_call" | custom-call | flops 402653184 | bytes 8388608 | tf_op jit(solution)/shard_map/forward/pallas_call | solution.py:224
  152.1 2.6 collective-permute-start.14
  159.9 3.1 %collective-permute-start.19 = (bf16[2,64,1024]{2,1,0:T(8,128)(2,1)}, bf16[2,64,1024]{2,1,0:T(8,128)(2,1)}, u32[]{:S(2)}, u32[]{:S(2)}) collective-permute-start(bf16[2,64,1024]{2,1,0:T(8,128)(2,1)} %copy-done.45), channel_id=1, source_target_pairs={{0,64},{32,96},{64,0},{96,32},{1,65},{33,97},{65,1},{97,33},{2,66}... | collective-permute-start | bytes 786440 | tf_op jit(solution)/shard_map/ppermute | solution.py:489
  167.5 3.9 %collective-permute-done.31.refs_17_ = f32[2,64,128]{2,1,0:T(8,128)S(1)} collective-permute-done((f32[2,64,128]{2,1,0:T(8,128)}, f32[2,64,128]{2,1,0:T(8,128)S(1)}, u32[]{:S(2)}, u32[]{:S(2)}) %collective-permute-start.31) | collective-permute-done | bytes 65568 | tf_op jit(solution)/shard_map/ppermute | solution.py:489
  171.4 2.7 %collective-permute-start.20 = (bf16[2,64,1024]{2,1,0:T(8,128)(2,1)}, bf16[2,64,1024]{2,1,0:T(8,128)(2,1)S(1)}, u32[]{:S(2)}, u32[]{:S(2)}) collective-permute-start(bf16[2,64,1024]{2,1,0:T(8,128)(2,1)} %copy-done.42), channel_id=1, source_target_pairs={{0,32},{32,64},{64,96},{96,0},{1,33},{33,65},{65,97},{97,1},{2,34}... | collective-permute-start | bytes 786440 | tf_op jit(solution)/shard_map/ppermute | solution.py:489
  174.6 3.3 %collective-permute-start.25 = (f32[2,64,128]{2,1,0:T(8,128)}, f32[2,64,128]{2,1,0:T(8,128)S(1)}, u32[]{:S(2)}, u32[]{:S(2)}) collective-permute-start(f32[2,64,128]{2,1,0:T(8,128)} %get-tuple-element.94), channel_id=1, source_target_pairs={{0,64},{32,96},{64,0},{96,32},{1,65},{33,97},{65,1},{97,33},{2,66}... | collective-permute-start | bytes 196616 | tf_op jit(solution)/shard_map/ppermute | solution.py:489
  177.9 3.4 %collective-permute-done.25.refs_17_ = f32[2,64,128]{2,1,0:T(8,128)S(1)} collective-permute-done((f32[2,64,128]{2,1,0:T(8,128)}, f32[2,64,128]{2,1,0:T(8,128)S(1)}, u32[]{:S(2)}, u32[]{:S(2)}) %collective-permute-start.25) | collective-permute-done | bytes 65568 | tf_op jit(solution)/shard_map/ppermute | solution.py:489
  187.2 10.5 %backward.3 = (bf16[2,64,1024]{2,1,0:T(8,128)(2,1)S(1)}, bf16[2,64,1024]{2,1,0:T(8,128)(2,1)S(1)}, bf16[2,64,1024]{2,1,0:T(8,128)(2,1)}, bf16[2,64,1024]{2,1,0:T...) custom-call(s32[8]{0:T(128)S(1)} %copy-done.33, s32[8]{0:T(128)S(1)} %copy-done.35, ...), custom_call_target="tpu_custom_call" | custom-call | flops 402653184 | bytes 8388608 | tf_op jit(solution)/shard_map/backward/pallas_call | solution.py:296
  198.7 3.2 %collective-permute-start.10 = (bf16[2,64,1024]{2,1,0:T(8,128)(2,1)S(1)}, bf16[2,64,1024]{2,1,0:T(8,128)(2,1)S(1)}, u32[]{:S(2)}, u32[]{:S(2)}) collective-permute-start(bf16[2,64,1024]{2,1,0:T(8,128)(2,1)S(1)} %copy-done.44), channel_id=1, source_target_pairs={{0,64},{32,96},{64,0},{96,32},{1,65},{33,97},{65,1},{97,33},{2,66}... | collective-permute-start | bytes 786440 | tf_op jit(solution)/shard_map/ppermute | solution.py:489
  206.2 10.3 %backward.2 = (bf16[2,64,1024]{2,1,0:T(8,128)(2,1)S(1)}, bf16[2,64,1024]{2,1,0:T(8,128)(2,1)}, bf16[2,64,1024]{2,1,0:T(8,128)(2,1)}, bf16[2,64,1024]{2,1,0:T(8,1...) custom-call(s32[8]{0:T(128)S(1)} %copy-done.33, s32[8]{0:T(128)S(1)} %copy-done.35, ...), custom_call_target="tpu_custom_call" | custom-call | flops 402653184 | bytes 8388608 | tf_op jit(solution)/shard_map/backward/pallas_call | solution.py:296
  221.6 7.6 %terms.2 = (bf16[6,128,2048]{2,1,0:T(8,128)(2,1)}, bf16[6,128,2048]{2,1,0:T(8,128)(2,1)}) custom-call(s32[8]{0:T(128)} %get-tuple-element.61.pick.refs_0_, s32[8]{0:T(128)} %get-tuple-element.62.refs_1_, s32[8]{0:T(128)} %copy-done.38, s32[8]{0:T(128)} %copy-done.37, s32[8]{0:T(128)} %copy-done.36, bf16[3,64,1024]{2,1,0:T(8,128)(2,1)} %copy-done.7, ...), custom_call_target="tpu_custom_call" | custom-call | flops 268435456 | bytes 7340032 | tf_op jit(solution)/shard_map/terms/pallas_call | solution.py:353
  229.3 7.8 %terms.3 = (bf16[6,128,2048]{2,1,0:T(8,128)(2,1)}, bf16[6,128,2048]{2,1,0:T(8,128)(2,1)}) custom-call(s32[8]{0:T(128)} %get-tuple-element.61.pick.refs_0_, s32[8]{0:T(128)} %get-tuple-element.62.refs_1_, s32[8]{0:T(128)} %copy-done.38, s32[8]{0:T(128)} %copy-done.37, s32[8]{0:T(128)} %copy-done.36, ...), custom_call_target="tpu_custom_call", output_to_operand_aliasing={{0}: (15, {}), {1}: (16, {})} | custom-call | flops 268435456 | bytes 7340032 | tf_op jit(solution)/shard_map/terms/pallas_call | solution.py:353
  237.1 2.4 attend.2.refs_0_
  241.3 5.6 %grad.2.refs_0_ = f32[192,4096]{1,0:T(8,128)S(1)} custom-call(s32[8]{0:T(128)S(1)} %copy-done.34, bf16[2,64,1024]{2,1,0:T(8,128)(2,1)S(1)} %get-tuple-element.104.g0, bf16[2,64,1024]{2,1,0:T(8,128)(2,1)S(1)} %collective-permute-done.33.g1, bf16[2,64,1024]{2,1,0:T(8,128)(2,1)S(1)} %collective-permute-done.34.g2, ...), custom_call_target="tpu_custom_call" | custom-call | flops 1610612736 | bytes 11534336 | tf_op jit(solution)/shard_map/grad/pallas_call | solution.py:471
  247.0 6.4 %grad.3 = bf16[192,4096]{1,0:T(8,128)(2,1)} custom-call(s32[8]{0:T(128)S(1)} %copy-done.34, bf16[2,64,1024]{2,1,0:T(8,128)(2,1)S(1)} %get-tuple-element.96.g0, bf16[2,64,1024]{2,1,0:T(8,128)(2,1)S(1)} %collective-permute-done.27.g1, bf16[2,64,1024]{2,1,0:T(8,128)(2,1)S(1)} %collective-permute-done.28.g2, ...), custom_call_target="tpu_custom_call" | custom-call | flops 1610612736 | bytes 11534336 | tf_op jit(solution)/shard_map/grad/pallas_call | solution.py:471
  (171 shorter events, 60.9 us)
Async XLA Ops:
  7.2 77.9 %all-gather.2.cloned.1.call-start = ((), (), s32[]{:S(2)}) async-start(), calls=%async_computation | async-start | bytes 17301504 | tf_op jit(solution)/shard_map/all_gather | solution.py:506
  15.3 92.6 %collective-permute-start.6 = (bf16[2,64,2048]{2,1,0:T(8,128)(2,1)S(1)}, bf16[2,64,2048]{2,1,0:T(8,128)(2,1)S(1)}, u32[]{:S(2)}, u32[]{:S(2)}) collective-permute-start(bf16[2,64,2048]{2,1,0:T(8,128)(2,1)S(1)} %get-tuple-element.67), channel_id=1, source_target_pairs={{0,32},{32,64},{64,96},{96,0},{1,33},{33,65},{65,97},{97,1},{2,34}... | collective-permute-start | bytes 1572872 | tf_op jit(solution)/shard_map/ppermute | solution.py:489
  16.5 96.6 %collective-permute-start.7 = (bf16[2,64,2048]{2,1,0:T(8,128)(2,1)}, bf16[2,64,2048]{2,1,0:T(8,128)(2,1)S(1)}, u32[]{:S(2)}, u32[]{:S(2)}) collective-permute-start(bf16[2,64,2048]{2,1,0:T(8,128)(2,1)} %get-tuple-element.68), channel_id=1, source_target_pairs={{0,64},{32,96},{64,0},{96,32},{1,65},{33,97},{65,1},{97,33},{2,66}... | collective-permute-start | bytes 1572872 | tf_op jit(solution)/shard_map/ppermute | solution.py:489
  17.2 97.5 %collective-permute-start.8 = (bf16[2,64,2048]{2,1,0:T(8,128)(2,1)}, bf16[2,64,2048]{2,1,0:T(8,128)(2,1)S(1)}, u32[]{:S(2)}, u32[]{:S(2)}) collective-permute-start(bf16[2,64,2048]{2,1,0:T(8,128)(2,1)} %get-tuple-element.69), channel_id=1, source_target_pairs={{0,96},{32,0},{64,32},{96,64},{1,97},{33,1},{65,33},{97,65},{2,98}... | collective-permute-start | bytes 1572872 | tf_op jit(solution)/shard_map/ppermute | solution.py:489
  91.9 23.8 %collective-permute-start.15 = (bf16[2,64,1024]{2,1,0:T(8,128)(2,1)S(1)}, bf16[2,64,1024]{2,1,0:T(8,128)(2,1)S(1)}, u32[]{:S(2)}, u32[]{:S(2)}) collective-permute-start(bf16[2,64,1024]{2,1,0:T(8,128)(2,1)S(1)} %get-tuple-element.80), channel_id=1, source_target_pairs={{0,32},{32,64},{64,96},{96,0},{1,33},{33,65},{65,97},{97,1},{2,34}... | collective-permute-start | bytes 786440 | tf_op jit(solution)/shard_map/ppermute | solution.py:489
  113.2 24.4 %collective-permute-start.3 = (bf16[2,64,1024]{2,1,0:T(8,128)(2,1)S(1)}, bf16[2,64,1024]{2,1,0:T(8,128)(2,1)S(1)}, u32[]{:S(2)}, u32[]{:S(2)}) collective-permute-start(bf16[2,64,1024]{2,1,0:T(8,128)(2,1)S(1)} %get-tuple-element.64), channel_id=1, source_target_pairs={{0,32},{32,64},{64,96},{96,0},{1,33},{33,65},{65,97},{97,1},{2,34}... | collective-permute-start | bytes 786440 | tf_op jit(solution)/shard_map/ppermute | solution.py:489
  114.7 23.7 %collective-permute-start.4 = (bf16[2,64,1024]{2,1,0:T(8,128)(2,1)S(1)}, bf16[2,64,1024]{2,1,0:T(8,128)(2,1)S(1)}, u32[]{:S(2)}, u32[]{:S(2)}) collective-permute-start(bf16[2,64,1024]{2,1,0:T(8,128)(2,1)S(1)} %get-tuple-element.65), channel_id=1, source_target_pairs={{0,64},{32,96},{64,0},{96,32},{1,65},{33,97},{65,1},{97,33},{2,66}... | collective-permute-start | bytes 786440 | tf_op jit(solution)/shard_map/ppermute | solution.py:489
  115.7 22.8 %collective-permute-start.5 = (bf16[2,64,1024]{2,1,0:T(8,128)(2,1)S(1)}, bf16[2,64,1024]{2,1,0:T(8,128)(2,1)S(1)}, u32[]{:S(2)}, u32[]{:S(2)}) collective-permute-start(bf16[2,64,1024]{2,1,0:T(8,128)(2,1)S(1)} %get-tuple-element.66), channel_id=1, source_target_pairs={{0,96},{32,0},{64,32},{96,64},{1,97},{33,1},{65,33},{97,65},{2,98}... | collective-permute-start | bytes 786440 | tf_op jit(solution)/shard_map/ppermute | solution.py:489
  133.9 18.1 %collective-permute-start.21 = (f32[2,64,128]{2,1,0:T(8,128)S(1)}, f32[2,64,128]{2,1,0:T(8,128)S(1)}, u32[]{:S(2)}, u32[]{:S(2)}) collective-permute-start(f32[2,64,128]{2,1,0:T(8,128)S(1)} %get-tuple-element.88), channel_id=1, source_target_pairs={{0,96},{32,0},{64,32},{96,64},{1,97},{33,1},{65,33},{97,65},{2,98}... | collective-permute-start | bytes 196616 | tf_op jit(solution)/shard_map/ppermute | solution.py:489
  134.5 20.1 %collective-permute-start.22 = (f32[2,64,128]{2,1,0:T(8,128)S(1)}, f32[2,64,128]{2,1,0:T(8,128)S(1)}, u32[]{:S(2)}, u32[]{:S(2)}) collective-permute-start(f32[2,64,128]{2,1,0:T(8,128)S(1)} %get-tuple-element.89), channel_id=1, source_target_pairs={{0,64},{32,96},{64,0},{96,32},{1,65},{33,97},{65,1},{97,33},{2,66}... | collective-permute-start | bytes 196616 | tf_op jit(solution)/shard_map/ppermute | solution.py:489
  137.6 17.0 %collective-permute-start.23 = (f32[2,64,128]{2,1,0:T(8,128)S(1)}, f32[2,64,128]{2,1,0:T(8,128)S(1)}, u32[]{:S(2)}, u32[]{:S(2)}) collective-permute-start(f32[2,64,128]{2,1,0:T(8,128)S(1)} %get-tuple-element.90), channel_id=1, source_target_pairs={{0,32},{32,64},{64,96},{96,0},{1,33},{33,65},{65,97},{97,1},{2,34}... | collective-permute-start | bytes 196616 | tf_op jit(solution)/shard_map/ppermute | solution.py:489
  159.5 42.4 %collective-permute-start.18 = (bf16[2,64,1024]{2,1,0:T(8,128)(2,1)}, bf16[2,64,1024]{2,1,0:T(8,128)(2,1)}, u32[]{:S(2)}, u32[]{:S(2)}) collective-permute-start(bf16[2,64,1024]{2,1,0:T(8,128)(2,1)} %copy-done.46), channel_id=1, source_target_pairs={{0,96},{32,0},{64,32},{96,64},{1,97},{33,1},{65,33},{97,65},{2,98}... | collective-permute-start | bytes 786440 | tf_op jit(solution)/shard_map/ppermute | solution.py:489
  159.9 42.0 %collective-permute-start.19 = (bf16[2,64,1024]{2,1,0:T(8,128)(2,1)}, bf16[2,64,1024]{2,1,0:T(8,128)(2,1)}, u32[]{:S(2)}, u32[]{:S(2)}) collective-permute-start(bf16[2,64,1024]{2,1,0:T(8,128)(2,1)} %copy-done.45), channel_id=1, source_target_pairs={{0,64},{32,96},{64,0},{96,32},{1,65},{33,97},{65,1},{97,33},{2,66}... | collective-permute-start | bytes 786440 | tf_op jit(solution)/shard_map/ppermute | solution.py:489
  171.4 32.5 %collective-permute-start.20 = (bf16[2,64,1024]{2,1,0:T(8,128)(2,1)}, bf16[2,64,1024]{2,1,0:T(8,128)(2,1)S(1)}, u32[]{:S(2)}, u32[]{:S(2)}) collective-permute-start(bf16[2,64,1024]{2,1,0:T(8,128)(2,1)} %copy-done.42), channel_id=1, source_target_pairs={{0,32},{32,64},{64,96},{96,0},{1,33},{33,65},{65,97},{97,1},{2,34}... | collective-permute-start | bytes 786440 | tf_op jit(solution)/shard_map/ppermute | solution.py:489
  174.1 31.4 %collective-permute-start.9 = (bf16[2,64,1024]{2,1,0:T(8,128)(2,1)}, bf16[2,64,1024]{2,1,0:T(8,128)(2,1)S(1)}, u32[]{:S(2)}, u32[]{:S(2)}) collective-permute-start(bf16[2,64,1024]{2,1,0:T(8,128)(2,1)} %copy-done.47), channel_id=1, source_target_pairs={{0,96},{32,0},{64,32},{96,64},{1,97},{33,1},{65,33},{97,65},{2,98}... | collective-permute-start | bytes 786440 | tf_op jit(solution)/shard_map/ppermute | solution.py:489
  181.3 17.4 %collective-permute-start.26 = (f32[2,64,128]{2,1,0:T(8,128)}, f32[2,64,128]{2,1,0:T(8,128)S(1)}, u32[]{:S(2)}, u32[]{:S(2)}) collective-permute-start(f32[2,64,128]{2,1,0:T(8,128)} %get-tuple-element.95), channel_id=1, source_target_pairs={{0,96},{32,0},{64,32},{96,64},{1,97},{33,1},{65,33},{97,65},{2,98}... | collective-permute-start | bytes 196616 | tf_op jit(solution)/shard_map/ppermute | solution.py:489
  198.7 18.8 %collective-permute-start.10 = (bf16[2,64,1024]{2,1,0:T(8,128)(2,1)S(1)}, bf16[2,64,1024]{2,1,0:T(8,128)(2,1)S(1)}, u32[]{:S(2)}, u32[]{:S(2)}) collective-permute-start(bf16[2,64,1024]{2,1,0:T(8,128)(2,1)S(1)} %copy-done.44), channel_id=1, source_target_pairs={{0,64},{32,96},{64,0},{96,32},{1,65},{33,97},{65,1},{97,33},{2,66}... | collective-permute-start | bytes 786440 | tf_op jit(solution)/shard_map/ppermute | solution.py:489
  201.9 15.6 %collective-permute-start.11 = (bf16[2,64,1024]{2,1,0:T(8,128)(2,1)S(1)}, bf16[2,64,1024]{2,1,0:T(8,128)(2,1)S(1)}, u32[]{:S(2)}, u32[]{:S(2)}) collective-permute-start(bf16[2,64,1024]{2,1,0:T(8,128)(2,1)S(1)} %copy-done.41), channel_id=1, source_target_pairs={{0,32},{32,64},{64,96},{96,0},{1,33},{33,65},{65,97},{97,1},{2,34}... | collective-permute-start | bytes 786440 | tf_op jit(solution)/shard_map/ppermute | solution.py:489
  201.9 17.8 %collective-permute-start.33 = (bf16[2,64,1024]{2,1,0:T(8,128)(2,1)S(1)}, bf16[2,64,1024]{2,1,0:T(8,128)(2,1)S(1)}, u32[]{:S(2)}, u32[]{:S(2)}) collective-permute-start(bf16[2,64,1024]{2,1,0:T(8,128)(2,1)S(1)} %get-tuple-element.105), channel_id=1, source_target_pairs={{0,96},{32,0},{64,32},{96,64},{1,97},{33,1},{65,33},{97,65},{2,98}... | collective-permute-start | bytes 786440 | tf_op jit(solution)/shard_map/ppermute | solution.py:489
  203.9 37.4 %collective-permute-start.34 = (bf16[2,64,1024]{2,1,0:T(8,128)(2,1)}, bf16[2,64,1024]{2,1,0:T(8,128)(2,1)S(1)}, u32[]{:S(2)}, u32[]{:S(2)}) collective-permute-start(bf16[2,64,1024]{2,1,0:T(8,128)(2,1)} %get-tuple-element.106), channel_id=1, source_target_pairs={{0,64},{32,96},{64,0},{96,32},{1,65},{33,97},{65,1},{97,33},{2,66}... | collective-permute-start | bytes 786440 | tf_op jit(solution)/shard_map/ppermute | solution.py:489
  205.5 35.8 %collective-permute-start.35 = (bf16[2,64,1024]{2,1,0:T(8,128)(2,1)}, bf16[2,64,1024]{2,1,0:T(8,128)(2,1)S(1)}, u32[]{:S(2)}, u32[]{:S(2)}) collective-permute-start(bf16[2,64,1024]{2,1,0:T(8,128)(2,1)} %get-tuple-element.107), channel_id=1, source_target_pairs={{0,32},{32,64},{64,96},{96,0},{1,33},{33,65},{65,97},{97,1},{2,34}... | collective-permute-start | bytes 786440 | tf_op jit(solution)/shard_map/ppermute | solution.py:489
  217.5 29.5 %collective-permute-start.27 = (bf16[2,64,1024]{2,1,0:T(8,128)(2,1)}, bf16[2,64,1024]{2,1,0:T(8,128)(2,1)S(1)}, u32[]{:S(2)}, u32[]{:S(2)}) collective-permute-start(bf16[2,64,1024]{2,1,0:T(8,128)(2,1)} %get-tuple-element.97), channel_id=1, source_target_pairs={{0,96},{32,0},{64,32},{96,64},{1,97},{33,1},{65,33},{97,65},{2,98}... | collective-permute-start | bytes 786440 | tf_op jit(solution)/shard_map/ppermute | solution.py:489
  217.5 29.5 %collective-permute-start.28 = (bf16[2,64,1024]{2,1,0:T(8,128)(2,1)}, bf16[2,64,1024]{2,1,0:T(8,128)(2,1)S(1)}, u32[]{:S(2)}, u32[]{:S(2)}) collective-permute-start(bf16[2,64,1024]{2,1,0:T(8,128)(2,1)} %get-tuple-element.98), channel_id=1, source_target_pairs={{0,64},{32,96},{64,0},{96,32},{1,65},{33,97},{65,1},{97,33},{2,66}... | collective-permute-start | bytes 786440 | tf_op jit(solution)/shard_map/ppermute | solution.py:489
  219.7 27.3 %collective-permute-start.29 = (bf16[2,64,1024]{2,1,0:T(8,128)(2,1)}, bf16[2,64,1024]{2,1,0:T(8,128)(2,1)S(1)}, u32[]{:S(2)}, u32[]{:S(2)}) collective-permute-start(bf16[2,64,1024]{2,1,0:T(8,128)(2,1)} %get-tuple-element.99), channel_id=1, source_target_pairs={{0,32},{32,64},{64,96},{96,0},{1,33},{33,65},{65,97},{97,1},{2,34}... | collective-permute-start | bytes 786440 | tf_op jit(solution)/shard_map/ppermute | solution.py:489
  (64 other events, 1248.9 us)
Sparse Core Ops, SparseCore 0:
  10.3 74.7 all-gather.1

commit v2 on v1

v2 whole, which is shorter than its diff:
```python
import functools
import math

import jax
import jax.numpy as jnp
from jax import lax
from jax.experimental import pallas as pl
from jax.experimental.pallas import tpu as pltpu
from jax.sharding import PartitionSpec as P

HEAD = 128
LEN = 128
ROWS = 64
GROUPS = 3
STORED = 6
SLOTS = 8
WIDTH = 2048
SCALE = 1.0 / math.sqrt(HEAD)
F32 = jnp.float32
BF16 = jnp.bfloat16
ANY = pl.BlockSpec(memory_space=pltpu.HBM)
SMEM = pl.BlockSpec(memory_space=pltpu.SMEM)
VMEM = pl.BlockSpec(memory_space=pltpu.VMEM)


def whole(*dims):
    return pl.BlockSpec(dims, lambda i: (0,) * len(dims))


GANG = 8
HOME_GANG = 4
HEADS = 16
BIG = 58
STEP = 1024
GSTEP = 1024


def params(mib):
    return pltpu.CompilerParams(vmem_limit_bytes=mib << 20)


def cost(flops, data, exps=0):
    return pl.CostEstimate(flops=int(flops), bytes_accessed=int(data), transcendentals=int(exps))


def shape(dims, dtype):
    return jax.ShapeDtypeStruct(dims, dtype)


def dot(a, b, ca, cb):
    return lax.dot_general(a, b, (((ca,), (cb,)), ((), ())), preferred_element_type=F32)


def head(h):
    return slice(h * HEAD, (h + 1) * HEAD)


def route_kernel(me, owner, row, pick, want, place, count):
    for k in range(SLOTS):
        pick[k] = 0
        want[k] = -1
    for d in range(4):
        count[d] = 0
    for g in range(GROUPS):
        for j in range(2):
            d = (owner[g, j] - me[0] + 4) % 4
            k = d * 2 + jnp.minimum(count[d], 1)
            count[d] = count[d] + 1
            pick[k] = g
            want[k] = row[g, j]
            place[g * 2 + j] = k


def route(me, owner, row):
    return pl.pallas_call(
        route_kernel,
        out_shape=(shape((SLOTS,), jnp.int32), shape((SLOTS,), jnp.int32), shape((SLOTS,), jnp.int32)),
        in_specs=[SMEM] * 3,
        out_specs=(SMEM, SMEM, SMEM),
        scratch_shapes=[pltpu.SMEM((4,), jnp.int32)],
        name="route",
    )(me, owner, row)


def spread_kernel(pick, cot, *outs):
    for d in range(1, 4):
        for s in range(2):
            outs[d - 1][s] = cot[pick[2 * d + s]]


def spread(pick, cot):
    one = shape((2, ROWS, WIDTH), BF16)
    return pl.pallas_call(
        spread_kernel,
        out_shape=(one,) * 3,
        grid=(1,),
        in_specs=[SMEM, whole(GROUPS, ROWS, WIDTH)],
        out_specs=(whole(2, ROWS, WIDTH),) * 3,
        compiler_params=params(BIG),
        cost_estimate=cost(1, 20 * ROWS * WIDTH),
        name="spread",
    )(pick, cot)


def query_kernel(steps, pick, hid, w, q, s1, s2, s3, acc):
    i = pl.program_id(0)
    part = dot(hid[...], w[...], 1, 0)

    @pl.when(i == 0)
    def _():
        acc[...] = part

    @pl.when(i > 0)
    def _():
        acc[...] += part

    @pl.when(i == steps - 1)
    def _():
        for g in range(GROUPS):
            q[g] = acc[g * ROWS : (g + 1) * ROWS].astype(BF16)
        for d, out in ((1, s1), (2, s2), (3, s3)):
            for s in range(2):
                out[s] = q[pick[2 * d + s]]


def query(pick, hidden, weights, col, cw):
    depth = hidden.shape[1]
    step = STEP
    steps = depth // step
    c = col // cw
    const = lambda i: (0, 0, 0)
    piece = shape((2, ROWS, cw), BF16)
    return pl.pallas_call(
        functools.partial(query_kernel, steps),
        out_shape=(shape((GROUPS, ROWS, cw), BF16), piece, piece, piece),
        grid=(steps,),
        in_specs=[
            SMEM,
            pl.BlockSpec((GROUPS * ROWS, step), lambda i: (0, i)),
            pl.BlockSpec((step, cw), lambda i: (i, c)),
        ],
        out_specs=(pl.BlockSpec((GROUPS, ROWS, cw), const),) + (pl.BlockSpec((2, ROWS, cw), const),) * 3,
        scratch_shapes=[pltpu.VMEM((GROUPS * ROWS, cw), F32)],
        compiler_params=params(BIG),
        cost_estimate=cost(2 * 192 * depth * cw, 2 * depth * (192 + cw)),
        name="query",
    )(pick, hidden, weights)


def rows_of(k, asked):
    d, s = divmod(k, 2)
    return asked[d][2 * d + s]


def fill_rows(asked, rows):
    for k in range(SLOTS):
        rows[k] = rows_of(k, asked)


def wait_slot(k, bufs, sems):
    for n, buf in enumerate(bufs):
        pltpu.make_async_copy(buf.at[k], buf.at[k], sems.at[k, n]).wait()


def collect_kernel(*refs):
    asked, table, outs, buf, sems, osems = refs[:4], refs[4], refs[5:8], refs[8], refs[9], refs[10]
    loads, stores = [], []
    for k in range(2, SLOTS):
        d, s = divmod(k, 2)
        row = jnp.maximum(rows_of(k, asked), 0)
        loads.append(pltpu.make_async_copy(table.at[row], buf.at[k - 2], sems.at[k - 2]))
        stores.append(pltpu.make_async_copy(buf.at[k - 2], outs[d - 1].at[s], osems.at[k - 2]))
    for one in loads:
        one.start()
    for one, two in zip(loads, stores):
        one.wait()
        two.start()
    for one in stores:
        one.wait()


def collect(asked, table):
    one = shape((2, LEN, WIDTH), BF16)
    return pl.pallas_call(
        collect_kernel,
        out_shape=(one,) * 3,
        in_specs=[SMEM] * 4 + [ANY],
        out_specs=(ANY,) * 3,
        scratch_shapes=[
            pltpu.VMEM((SLOTS - 2, LEN, WIDTH), BF16),
            pltpu.SemaphoreType.DMA((SLOTS - 2,)),
            pltpu.SemaphoreType.DMA((SLOTS - 2,)),
        ],
        compiler_params=params(BIG),
        cost_estimate=cost(1, 24 * LEN * WIDTH),
        name="collect",
    )(*asked, table)


def home_kernel(*refs):
    pick, place, want, q, c, keys, values = refs[:7]
    ks, vs = (keys,) + refs[7:10], (values,) + refs[10:13]
    att, gq, backs = refs[13], refs[14], refs[15:19]
    qb, cb, kb, vb, res, sems, gsems = refs[19:]
    for g in range(GROUPS):
        pltpu.make_async_copy(q.at[g], qb.at[g], gsems.at[g, 0]).start()
        pltpu.make_async_copy(c.at[g], cb.at[g], gsems.at[g, 1]).start()
        for r in (2 * g, 2 * g + 1):
            at = place[r]
            for d in range(4):

                @pl.when(at // 2 == d)
                def _(r=r, d=d, at=at):
                    s = jnp.maximum(want[at], 0) if d == 0 else at - 2 * d
                    pltpu.make_async_copy(ks[d].at[s], kb.at[r], sems.at[r, 0]).start()
                    pltpu.make_async_copy(vs[d].at[s], vb.at[r], sems.at[r, 1]).start()

    lane = lax.broadcasted_iota(jnp.int32, (ROWS, HEAD), 1)

    @pl.loop(0, GROUPS)
    def _(g):
        wait_slot(g, (qb, cb), gsems)
        for j in range(2):
            wait_slot(2 * g + j, (kb, vb), sems)
        stats = jnp.zeros((ROWS, HEAD), F32)
        out = pl.ds(pl.multiple_of(g * ROWS, ROWS), ROWS)
        for base in range(0, HEADS, HOME_GANG):
            span = [(h, j) for h in range(base, base + HOME_GANG) for j in range(2)]
            key = {(h, j): kb[2 * g + j, :, head(h)] for h, j in span}
            value = {(h, j): vb[2 * g + j, :, head(h)] for h, j in span}
            score = {(h, j): dot(qb[g, :, head(h)], key[h, j], 1, 1) * SCALE for h, j in span}
            slope = {(h, j): dot(cb[g, :, head(h)], value[h, j], 1, 1) for h, j in span}
            peak = {x: jnp.max(score[x], axis=1, keepdims=True) for x in span}
            e = {x: jnp.exp(score[x] - peak[x]) for x in span}
            total = {x: jnp.sum(e[x], axis=1, keepdims=True) for x in span}
            part = {x: dot(e[x].astype(BF16), value[x], 1, 0) for x in span}
            for h in range(base, base + HOME_GANG):
                top = jnp.maximum(peak[h, 0], peak[h, 1])
                scale = [jnp.exp(peak[h, j] - top) for j in range(2)]
                below = scale[0] * total[h, 0] + scale[1] * total[h, 1]
                scale = [x / below for x in scale]
                mix = part[h, 0] * scale[0] + part[h, 1] * scale[1]
                att[out, head(h)] = mix.astype(BF16)
                delta = jnp.sum(cb[g, :, head(h)].astype(F32) * mix, axis=1, keepdims=True)
                stats = jnp.where(lane == h, top + jnp.log(below), stats)
                stats = jnp.where(lane == HEADS + h, delta, stats)
                both = None
                for j in range(2):
                    gs = (e[h, j] * scale[j] * (slope[h, j] - delta) * SCALE).astype(BF16)
                    one = dot(gs, key[h, j], 1, 0)
                    both = one if both is None else both + one
                gq[out, head(h)] = both.astype(BF16)
        res[g] = stats

    for d in range(4):
        for s in range(2):
            backs[d][s] = res[pick[2 * d + s]]


def home(pick, place, want, q, c, keys, values, ks, vs):
    rows = shape((GROUPS * ROWS, WIDTH), BF16)
    small = shape((2, ROWS, HEAD), F32)
    return pl.pallas_call(
        home_kernel,
        out_shape=(rows,) * 2 + (small,) * 4,
        grid=(1,),
        in_specs=[SMEM] * 3 + [ANY] * 10,
        out_specs=(whole(GROUPS * ROWS, WIDTH),) * 2 + (whole(2, ROWS, HEAD),) * 4,
        scratch_shapes=[
            pltpu.VMEM((GROUPS, ROWS, WIDTH), BF16),
            pltpu.VMEM((GROUPS, ROWS, WIDTH), BF16),
            pltpu.VMEM((2 * GROUPS, LEN, WIDTH), BF16),
            pltpu.VMEM((2 * GROUPS, LEN, WIDTH), BF16),
            pltpu.VMEM((GROUPS, ROWS, HEAD), F32),
            pltpu.SemaphoreType.DMA((2 * GROUPS, 2)),
            pltpu.SemaphoreType.DMA((GROUPS, 2)),
        ],
        compiler_params=params(BIG),
        cost_estimate=cost(6 * 8 * ROWS * LEN * WIDTH, 30 * LEN * WIDTH, 6 * ROWS * WIDTH),
        name="home",
    )(pick, place, want, q, c, keys, values, *ks, *vs)


def terms_kernel(*refs):
    pick, asked, refs = refs[0], refs[1:5], refs[5:]
    q, c, keys, values, back = refs[:4], refs[4:8], refs[8], refs[9], refs[10:14]
    dk, dv, rows, seen, qb, cb, kb, vb, bb, sems = refs[14:]
    fill_rows(asked, rows)
    bufs = (qb, cb, kb, vb, bb)
    for b in range(STORED):
        seen[b] = 0
    for k in range(SLOTS):
        d, s = divmod(k, 2)
        at = pick[k] if d == 0 else s
        row = jnp.maximum(rows[k], 0)
        pltpu.make_async_copy(q[d].at[at], qb.at[k], sems.at[k, 0]).start()
        pltpu.make_async_copy(c[d].at[at], cb.at[k], sems.at[k, 1]).start()
        pltpu.make_async_copy(keys.at[row], kb.at[k], sems.at[k, 2]).start()
        pltpu.make_async_copy(values.at[row], vb.at[k], sems.at[k, 3]).start()
        pltpu.make_async_copy(back[d].at[s], bb.at[k], sems.at[k, 4]).start()

    def one_slot(k, row, add):
        stats = bb[k]
        for base in range(0, HEADS, GANG):
            span = range(base, base + GANG)
            scores = [dot(qb[k, :, head(h)], kb[k, :, head(h)], 1, 1) * SCALE for h in span]
            slopes = [dot(cb[k, :, head(h)], vb[k, :, head(h)], 1, 1) for h in span]
            probs = [jnp.exp(x - stats[:, h : h + 1]) for h, x in zip(span, scores)]
            gs = [
                (x * (y - stats[:, HEADS + h : HEADS + h + 1]) * SCALE).astype(BF16)
                for h, x, y in zip(span, probs, slopes)
            ]
            kts = [dot(x, qb[k, :, head(h)], 0, 0) for h, x in zip(span, gs)]
            vts = [dot(x.astype(BF16), cb[k, :, head(h)], 0, 0) for h, x in zip(span, probs)]
            for h, kt, vt in zip(span, kts, vts):
                if add:
                    kt = kt.astype(BF16).astype(F32) + dk[row, :, head(h)].astype(F32)
                    vt = vt.astype(BF16).astype(F32) + dv[row, :, head(h)].astype(F32)
                dk[row, :, head(h)] = kt.astype(BF16)
                dv[row, :, head(h)] = vt.astype(BF16)

    @pl.loop(0, SLOTS)
    def _(k):
        wait_slot(k, bufs, sems)
        row = jnp.maximum(rows[k], 0)
        valid = rows[k] >= 0

        @pl.when(valid & (seen[row] == 0))
        def _():
            one_slot(k, row, False)

        @pl.when(valid & (seen[row] > 0))
        def _():
            one_slot(k, row, True)

        seen[row] = seen[row] + valid.astype(jnp.int32)

    for b in range(STORED):

        @pl.when(seen[b] == 0)
        def _(b=b):
            dk[b] = jnp.zeros((LEN, WIDTH), BF16)
            dv[b] = jnp.zeros((LEN, WIDTH), BF16)


def terms(pick, asked, q, c, keys, values, back):
    full = shape((STORED, LEN, WIDTH), BF16)
    return pl.pallas_call(
        terms_kernel,
        out_shape=(full,) * 2,
        grid=(1,),
        in_specs=[SMEM] * 5 + [ANY] * 14,
        out_specs=(whole(STORED, LEN, WIDTH),) * 2,
        scratch_shapes=[
            pltpu.SMEM((SLOTS,), jnp.int32),
            pltpu.SMEM((STORED,), jnp.int32),
            pltpu.VMEM((SLOTS, ROWS, WIDTH), BF16),
            pltpu.VMEM((SLOTS, ROWS, WIDTH), BF16),
            pltpu.VMEM((SLOTS, LEN, WIDTH), BF16),
            pltpu.VMEM((SLOTS, LEN, WIDTH), BF16),
            pltpu.VMEM((SLOTS, ROWS, HEAD), F32),
            pltpu.SemaphoreType.DMA((SLOTS, 5)),
        ],
        compiler_params=params(BIG),
        cost_estimate=cost(SLOTS * 8 * ROWS * LEN * WIDTH, 44 * LEN * WIDTH, SLOTS * ROWS * WIDTH),
        name="terms",
    )(pick, *asked, *q, *c, keys, values, *back)


def grad_kernel(gq, w, out):
    out[...] = dot(gq[...], w[...], 1, 1).astype(BF16)


def grad(gq, weights):
    depth, step = weights.shape[0], GSTEP
    return pl.pallas_call(
        grad_kernel,
        out_shape=shape((GROUPS * ROWS, depth), BF16),
        grid=(depth // step,),
        in_specs=[whole(GROUPS * ROWS, WIDTH), pl.BlockSpec((step, WIDTH), lambda i: (i, 0))],
        out_specs=pl.BlockSpec((GROUPS * ROWS, step), lambda i: (0, i)),
        compiler_params=params(BIG),
        cost_estimate=cost(2 * 192 * depth * WIDTH, 2 * depth * (192 + WIDTH)),
        name="grad",
    )(gq, weights)


def shift(x, d):
    return lax.ppermute(x, "enc", [(i, (i + d) % 4) for i in range(4)])


def to_owner(pieces):
    return [shift(x, d + 1) for d, x in enumerate(pieces)]


def to_home(pieces):
    return [shift(x, -(d + 1)) for d, x in enumerate(pieces)]


def per_device(hidden, query_weight, keys, values, owner, row, cotangent):
    me = lax.axis_index("enc").astype(jnp.int32).reshape(1)
    weights = lax.all_gather(query_weight, "fsdp", axis=0, tiled=True)
    pick, want, place = route(me, owner, row)
    asked = [want] + to_owner([want] * 3)
    ks = to_home(collect(asked, keys))
    vs = to_home(collect(asked, values))
    cot = cotangent.reshape(GROUPS, ROWS, WIDTH)
    c = [cot] + to_owner(spread(pick, cot))
    q, *sends = query(pick, hidden, weights, 0, WIDTH)
    qs = [q] + to_owner(sends)
    attended, gq, *back = home(pick, place, want, q, cot, keys, values, ks, vs)
    back = [back[0]] + to_owner(back[1:])
    grad_hidden = grad(gq, weights)
    grad_keys, grad_values = terms(pick, asked, qs, c, keys, values, back)
    return attended, grad_hidden, grad_keys, grad_values


def solution(mesh):
    rows = P(("enc", "fsdp"), None)
    blocks = P(("enc", "fsdp"), None, None)
    return jax.shard_map(
        per_device,
        mesh=mesh,
        in_specs=(rows, P("fsdp", None), blocks, blocks, rows, rows, rows),
        out_specs=(rows, rows, blocks, blocks),
        check_vma=False,
    )
```

time: 262 us -> 204 us (0.78)
  the two profiles are of different devices: /device:TPU:16 before, /device:TPU:106 now
where the time goes in v2:
time: 204 us; the launch traced here: 200 us
  waiting for transfers between devices  77.9 us (38%)
  Pallas kernels  57.3 us (28%)
  starting transfers between devices  46.2 us (23%)
  between operations  14.2 us (7%)
  local copies, waits for them, and re-layouts  4.87 us (2%)
    ppermute x18, waiting for transfers between devices, shift(): return lax.ppermute(x, 'enc', [(i, (i + d) % 4) for i in range(4)])  77.2 us
    ppermute x18, starting transfers between devices, shift(): return lax.ppermute(x, 'enc', [(i, (i + d) % 4) for i in range(4)])  46.2 us
    pallas_call x1, Pallas kernels, home(): pl.pallas_call(home_kernel, out_shape=(rows,) * 2 + (small,) * 4, grid=(1...  12.3 us
    pallas_call x1, Pallas kernels, terms(): pl.pallas_call(terms_kernel, out_shape=(full,) * 2, grid=(1,), in_specs=[...  12.2 us
    pallas_call x1, Pallas kernels, grad(): pl.pallas_call(grad_kernel, out_shape=shape((GROUPS * ROWS, depth), BF16)...  10.3 us
    pallas_call x1, Pallas kernels, query(): pl.pallas_call(functools.partial(query_kernel, steps), out_shape=(shape((...  10.1 us
    pallas_call x2, Pallas kernels, collect(): pl.pallas_call(collect_kernel, out_shape=(one,) * 3, in_specs=[SMEM] * 4...  8.62 us
    unnamed x28, local copies, waits for them, and re-layouts  4.87 us
  transfers between devices with their start and end apart: 19, of which 8 were waited for; matrix products, arithmetic and copies ran while one was open for 1% of the time, Pallas kernels for 22%

profile of v2, /device:TPU:106, one launch (start us, length us, event | category | flops | bytes accessed | tf_op | source)
XLA Modules:
  0.0 200.4 jit_solution(9197040736785321248)
XLA Ops:
  14.5 2.4 %collective-permute-start.2 = (s32[8]{0:T(128)}, s32[8]{0:T(128)S(1)}, u32[]{:S(2)}, u32[]{:S(2)}) collective-permute-start(s32[8]{0:T(128)} %get-tuple-element.30.refs_0_.refs_2_.refs_1_), channel_id=1, source_target_pairs={{0,96},{32,0},{64,32},{96,64},{1,97},{33,1},{65,33},{97,65},{2,98}... | collective-permute-start | bytes 104 | tf_op jit(solution)/shard_map/ppermute | solution.py:389
  16.9 1.7 collective-permute-done.1.refs_2_.refs_3_
  19.7 4.3 %collect.2 = (bf16[2,128,2048]{2,1,0:T(8,128)(2,1)}, bf16[2,128,2048]{2,1,0:T(8,128)(2,1)}, bf16[2,128,2048]{2,1,0:T(8,128)(2,1)}) custom-call(s32[8]{0:T(128)} %get-tuple-element.30.refs_0_.refs_2_.refs_1_, s32[8]{0:T(128)} %copy-done.10, s32[8]{0:T(128)} %copy-done.11, s32[8]{0:T(128)} %copy-done.12, bf16[6,128,2048]{2,1,0:T(8,128)(2,1)} %refs_13_.1), custom_call_target="tpu_custom_call" | custom-call | flops 1 | bytes 6291456 | tf_op jit(solution)/shard_map/collect/pallas_call | solution.py:184
  25.1 2.4 %spread.1 = (bf16[2,64,2048]{2,1,0:T(8,128)(2,1)}, bf16[2,64,2048]{2,1,0:T(8,128)(2,1)}, bf16[2,64,2048]{2,1,0:T(8,128)(2,1)}) custom-call(s32[8]{0:T(128)} %get-tuple-element.28.pick.refs_0_, bf16[3,64,2048]{2,1,0:T(8,128)(2,1)} %bitcast.2), custom_call_target="tpu_custom_call" | custom-call | flops 1 | bytes 2621440 | tf_op jit(solution)/shard_map/spread/pallas_call | solution.py:93
  28.5 3.8 %collective-permute-start.4 = (bf16[2,128,2048]{2,1,0:T(8,128)(2,1)}, bf16[2,128,2048]{2,1,0:T(8,128)(2,1)S(1)}, u32[]{:S(2)}, u32[]{:S(2)}) collective-permute-start(bf16[2,128,2048]{2,1,0:T(8,128)(2,1)} %get-tuple-element.33), channel_id=1, source_target_pairs={{0,64},{32,96},{64,0},{96,32},{1,65},{33,97},{65,1},{97,33},{2,66}... | collective-permute-start | bytes 3145736 | tf_op jit(solution)/shard_map/ppermute | solution.py:389
  32.3 4.3 %collect.3 = (bf16[2,128,2048]{2,1,0:T(8,128)(2,1)}, bf16[2,128,2048]{2,1,0:T(8,128)(2,1)}, bf16[2,128,2048]{2,1,0:T(8,128)(2,1)}) custom-call(s32[8]{0:T(128)} %get-tuple-element.30.refs_0_.refs_2_.refs_1_, s32[8]{0:T(128)} %copy-done.10, s32[8]{0:T(128)} %copy-done.11, s32[8]{0:T(128)} %copy-done.12, bf16[6,128,2048]{2,1,0:T(8,128)(2,1)} %refs_14_.1), custom_call_target="tpu_custom_call" | custom-call | flops 1 | bytes 6291456 | tf_op jit(solution)/shard_map/collect/pallas_call | solution.py:184
  36.6 2.0 collective-permute-start.6
  38.6 23.3 %collective-permute-done.12.refs_10_ = bf16[2,64,2048]{2,1,0:T(8,128)(2,1)S(1)} collective-permute-done((bf16[2,64,2048]{2,1,0:T(8,128)(2,1)}, bf16[2,64,2048]{2,1,0:T(8,128)(2,1)S(1)}, u32[]{:S(2)}, u32[]{:S(2)}) %collective-permute-start.12) | collective-permute-done | bytes 524320 | tf_op jit(solution)/shard_map/ppermute | solution.py:389
  61.9 5.5 %collective-permute-start.7 = (bf16[2,128,2048]{2,1,0:T(8,128)(2,1)}, bf16[2,128,2048]{2,1,0:T(8,128)(2,1)}, u32[]{:S(2)}, u32[]{:S(2)}) collective-permute-start(bf16[2,128,2048]{2,1,0:T(8,128)(2,1)} %get-tuple-element.36), channel_id=1, source_target_pairs={{0,64},{32,96},{64,0},{96,32},{1,65},{33,97},{65,1},{97,33},{2,66}... | collective-permute-start | bytes 3145736 | tf_op jit(solution)/shard_map/ppermute | solution.py:389
  67.5 4.7 %collective-permute-done.3.refs_7_ = bf16[2,128,2048]{2,1,0:T(8,128)(2,1)S(1)} collective-permute-done((bf16[2,128,2048]{2,1,0:T(8,128)(2,1)}, bf16[2,128,2048]{2,1,0:T(8,128)(2,1)S(1)}, u32[]{:S(2)}, u32[]{:S(2)}) %collective-permute-start.3) | collective-permute-done | bytes 1048608 | tf_op jit(solution)/shard_map/ppermute | solution.py:389
  73.5 3.2 %collective-permute-start.13 = (bf16[2,64,2048]{2,1,0:T(8,128)(2,1)}, bf16[2,64,2048]{2,1,0:T(8,128)(2,1)}, u32[]{:S(2)}, u32[]{:S(2)}) collective-permute-start(bf16[2,64,2048]{2,1,0:T(8,128)(2,1)} %get-tuple-element.44), channel_id=1, source_target_pairs={{0,64},{32,96},{64,0},{96,32},{1,65},{33,97},{65,1},{97,33},{2,66}... | collective-permute-start | bytes 1572872 | tf_op jit(solution)/shard_map/ppermute | solution.py:389
  76.7 30.1 %collective-permute-done.5.refs_9_ = bf16[2,128,2048]{2,1,0:T(8,128)(2,1)S(1)} collective-permute-done((bf16[2,128,2048]{2,1,0:T(8,128)(2,1)}, bf16[2,128,2048]{2,1,0:T(8,128)(2,1)S(1)}, u32[]{:S(2)}, u32[]{:S(2)}) %collective-permute-start.5) | collective-permute-done | bytes 1048608 | tf_op jit(solution)/shard_map/ppermute | solution.py:389
  106.8 7.1 %collective-permute-start.14 = (bf16[2,64,2048]{2,1,0:T(8,128)(2,1)}, bf16[2,64,2048]{2,1,0:T(8,128)(2,1)}, u32[]{:S(2)}, u32[]{:S(2)}) collective-permute-start(bf16[2,64,2048]{2,1,0:T(8,128)(2,1)} %get-tuple-element.45), channel_id=1, source_target_pairs={{0,96},{32,0},{64,32},{96,64},{1,97},{33,1},{65,33},{97,65},{2,98}... | collective-permute-start | bytes 1572872 | tf_op jit(solution)/shard_map/ppermute | solution.py:389
  113.9 10.1 %query.1 = (bf16[3,64,2048]{2,1,0:T(8,128)(2,1)}, bf16[2,64,2048]{2,1,0:T(8,128)(2,1)}, bf16[2,64,2048]{2,1,0:T(8,128)(2,1)}, bf16[2,64,2048]{2,1,0:T(8,128)(2,1)}) custom-call(s32[8]{0:T(128)} %get-tuple-element.28.pick.refs_0_, bf16[192,4096]{1,0:T(8,128)(2,1)} %hid.1, bf16[4096,2048]{1,0:T(8,128)(2,1)} %all-gather.2.cloned.1.call-done.w), custom_call_target="tpu_custom_call" | custom-call | flops 3221225472 | bytes 18350080 | tf_op jit(solution)/shard_map/query/pallas_call | solution.py:133
  124.1 4.3 %collective-permute-done.6.refs_10_ = bf16[2,128,2048]{2,1,0:T(8,128)(2,1)} collective-permute-done((bf16[2,128,2048]{2,1,0:T(8,128)(2,1)}, bf16[2,128,2048]{2,1,0:T(8,128)(2,1)}, u32[]{:S(2)}, u32[]{:S(2)}) %collective-permute-start.6) | collective-permute-done | bytes 1048608 | tf_op jit(solution)/shard_map/ppermute | solution.py:389
  128.4 4.5 %collective-permute-start.10 = (bf16[2,64,2048]{2,1,0:T(8,128)(2,1)}, bf16[2,64,2048]{2,1,0:T(8,128)(2,1)S(1)}, u32[]{:S(2)}, u32[]{:S(2)}) collective-permute-start(bf16[2,64,2048]{2,1,0:T(8,128)(2,1)} %get-tuple-element.41), channel_id=1, source_target_pairs={{0,64},{32,96},{64,0},{96,32},{1,65},{33,97},{65,1},{97,33},{2,66}... | collective-permute-start | bytes 1572872 | tf_op jit(solution)/shard_map/ppermute | solution.py:389
  132.9 7.6 %collective-permute-done.8.refs_12_ = bf16[2,128,2048]{2,1,0:T(8,128)(2,1)} collective-permute-done((bf16[2,128,2048]{2,1,0:T(8,128)(2,1)}, bf16[2,128,2048]{2,1,0:T(8,128)(2,1)}, u32[]{:S(2)}, u32[]{:S(2)}) %collective-permute-start.8) | collective-permute-done | bytes 1048608 | tf_op jit(solution)/shard_map/ppermute | solution.py:389
  140.5 7.3 %collective-permute-start.11 = (bf16[2,64,2048]{2,1,0:T(8,128)(2,1)}, bf16[2,64,2048]{2,1,0:T(8,128)(2,1)S(1)}, u32[]{:S(2)}, u32[]{:S(2)}) collective-permute-start(bf16[2,64,2048]{2,1,0:T(8,128)(2,1)} %get-tuple-element.42), channel_id=1, source_target_pairs={{0,96},{32,0},{64,32},{96,64},{1,97},{33,1},{65,33},{97,65},{2,98}... | collective-permute-start | bytes 1572872 | tf_op jit(solution)/shard_map/ppermute | solution.py:389
  147.8 12.3 %home.1 = (bf16[192,2048]{1,0:T(8,128)(2,1)}, bf16[192,2048]{1,0:T(8,128)(2,1)}, f32[2,64,128]{2,1,0:T(8,128)}, f32[2,64,128]{2,1,0:T(8,128)}, f32[2,64,128]{2,1,0:T(8,128)}, /*index=5*/f32[2,64,128]{2,1,0:T(8,128)}) custom-call(s32[8]{0:T(128)} %get-tuple-element.28.pick.refs_0_, s32[8]{0:T(128)} %get-tuple-element.29.refs_1_, ...), custom_call_target="tpu_custom_call" | custom-call | flops 805306368 | bytes 7864320 | tf_op jit(solution)/shard_map/home/pallas_call | solution.py:263
  160.2 2.0 %collective-permute-start.16 = (f32[2,64,128]{2,1,0:T(8,128)}, f32[2,64,128]{2,1,0:T(8,128)S(1)}, u32[]{:S(2)}, u32[]{:S(2)}) collective-permute-start(f32[2,64,128]{2,1,0:T(8,128)} %get-tuple-element.48), channel_id=1, source_target_pairs={{0,64},{32,96},{64,0},{96,32},{1,65},{33,97},{65,1},{97,33},{2,66}... | collective-permute-start | bytes 196616 | tf_op jit(solution)/shard_map/ppermute | solution.py:389
  162.2 4.1 %collective-permute-done.15.refs_16_ = f32[2,64,128]{2,1,0:T(8,128)S(1)} collective-permute-done((f32[2,64,128]{2,1,0:T(8,128)}, f32[2,64,128]{2,1,0:T(8,128)S(1)}, u32[]{:S(2)}, u32[]{:S(2)}) %collective-permute-start.15) | collective-permute-done | bytes 65568 | tf_op jit(solution)/shard_map/ppermute | solution.py:389
  166.3 3.5 %collective-permute-start.17 = (f32[2,64,128]{2,1,0:T(8,128)}, f32[2,64,128]{2,1,0:T(8,128)S(1)}, u32[]{:S(2)}, u32[]{:S(2)}) collective-permute-start(f32[2,64,128]{2,1,0:T(8,128)} %get-tuple-element.49), channel_id=1, source_target_pairs={{0,96},{32,0},{64,32},{96,64},{1,97},{33,1},{65,33},{97,65},{2,98}... | collective-permute-start | bytes 196616 | tf_op jit(solution)/shard_map/ppermute | solution.py:389
  169.8 10.3 %grad.1 = bf16[192,4096]{1,0:T(8,128)(2,1)} custom-call(bf16[192,2048]{1,0:T(8,128)(2,1)} %get-tuple-element.39.gq, bf16[4096,2048]{1,0:T(8,128)(2,1)} %all-gather.2.cloned.1.call-done.w), custom_call_target="tpu_custom_call" | custom-call | flops 3221225472 | bytes 18350080 | tf_op jit(solution)/shard_map/grad/pallas_call | solution.py:376
  181.3 12.2 %terms.1 = (bf16[6,128,2048]{2,1,0:T(8,128)(2,1)}, bf16[6,128,2048]{2,1,0:T(8,128)(2,1)}) custom-call(s32[8]{0:T(128)} %get-tuple-element.28.pick.refs_0_, s32[8]{0:T(128)} %get-tuple-element.30.refs_0_.refs_2_.refs_1_, s32[8]{0:T(128)} %copy-done.10, s32[8]{0:T(128)} %copy-done.11, s32[8]{0:T(128)} %copy-done.12, ...), custom_call_target="tpu_custom_call" | custom-call | flops 1073741824 | bytes 11534336 | tf_op jit(solution)/shard_map/terms/pallas_call | solution.py:348
  (51 shorter events, 13.0 us)
Async XLA Ops:
  7.2 106.8 %all-gather.2.cloned.1.call-start = ((), (), s32[]{:S(2)}) async-start(), calls=%async_computation | async-start | bytes 17301504 | tf_op jit(solution)/shard_map/all_gather | solution.py:402
  11.9 5.0 %collective-permute-start = (s32[8]{0:T(128)}, s32[8]{0:T(128)S(1)}, u32[]{:S(2)}, u32[]{:S(2)}) collective-permute-start(s32[8]{0:T(128)} %get-tuple-element.30.refs_0_.refs_2_.refs_1_), channel_id=1, source_target_pairs={{0,32},{32,64},{64,96},{96,0},{1,33},{33,65},{65,97},{97,1},{2,34}... | collective-permute-start | bytes 104 | tf_op jit(solution)/shard_map/ppermute | solution.py:389
  13.5 5.1 %collective-permute-start.1 = (s32[8]{0:T(128)}, s32[8]{0:T(128)S(1)}, u32[]{:S(2)}, u32[]{:S(2)}) collective-permute-start(s32[8]{0:T(128)} %get-tuple-element.30.refs_0_.refs_2_.refs_1_), channel_id=1, source_target_pairs={{0,64},{32,96},{64,0},{96,32},{1,65},{33,97},{65,1},{97,33},{2,66}... | collective-permute-start | bytes 104 | tf_op jit(solution)/shard_map/ppermute | solution.py:389
  14.5 4.2 %collective-permute-start.2 = (s32[8]{0:T(128)}, s32[8]{0:T(128)S(1)}, u32[]{:S(2)}, u32[]{:S(2)}) collective-permute-start(s32[8]{0:T(128)} %get-tuple-element.30.refs_0_.refs_2_.refs_1_), channel_id=1, source_target_pairs={{0,96},{32,0},{64,32},{96,64},{1,97},{33,1},{65,33},{97,65},{2,98}... | collective-permute-start | bytes 104 | tf_op jit(solution)/shard_map/ppermute | solution.py:389
  24.0 48.2 %collective-permute-start.3 = (bf16[2,128,2048]{2,1,0:T(8,128)(2,1)}, bf16[2,128,2048]{2,1,0:T(8,128)(2,1)S(1)}, u32[]{:S(2)}, u32[]{:S(2)}) collective-permute-start(bf16[2,128,2048]{2,1,0:T(8,128)(2,1)} %get-tuple-element.32), channel_id=1, source_target_pairs={{0,96},{32,0},{64,32},{96,64},{1,97},{33,1},{65,33},{97,65},{2,98}... | collective-permute-start | bytes 3145736 | tf_op jit(solution)/shard_map/ppermute | solution.py:389
  27.5 34.4 %collective-permute-start.12 = (bf16[2,64,2048]{2,1,0:T(8,128)(2,1)}, bf16[2,64,2048]{2,1,0:T(8,128)(2,1)S(1)}, u32[]{:S(2)}, u32[]{:S(2)}) collective-permute-start(bf16[2,64,2048]{2,1,0:T(8,128)(2,1)} %get-tuple-element.43), channel_id=1, source_target_pairs={{0,32},{32,64},{64,96},{96,0},{1,33},{33,65},{65,97},{97,1},{2,34}... | collective-permute-start | bytes 1572872 | tf_op jit(solution)/shard_map/ppermute | solution.py:389
  28.5 45.0 %collective-permute-start.4 = (bf16[2,128,2048]{2,1,0:T(8,128)(2,1)}, bf16[2,128,2048]{2,1,0:T(8,128)(2,1)S(1)}, u32[]{:S(2)}, u32[]{:S(2)}) collective-permute-start(bf16[2,128,2048]{2,1,0:T(8,128)(2,1)} %get-tuple-element.33), channel_id=1, source_target_pairs={{0,64},{32,96},{64,0},{96,32},{1,65},{33,97},{65,1},{97,33},{2,66}... | collective-permute-start | bytes 3145736 | tf_op jit(solution)/shard_map/ppermute | solution.py:389
  32.3 74.5 %collective-permute-start.5 = (bf16[2,128,2048]{2,1,0:T(8,128)(2,1)}, bf16[2,128,2048]{2,1,0:T(8,128)(2,1)S(1)}, u32[]{:S(2)}, u32[]{:S(2)}) collective-permute-start(bf16[2,128,2048]{2,1,0:T(8,128)(2,1)} %get-tuple-element.34), channel_id=1, source_target_pairs={{0,32},{32,64},{64,96},{96,0},{1,33},{33,65},{65,97},{97,1},{2,34}... | collective-permute-start | bytes 3145736 | tf_op jit(solution)/shard_map/ppermute | solution.py:389
  36.6 91.8 %collective-permute-start.6 = (bf16[2,128,2048]{2,1,0:T(8,128)(2,1)}, bf16[2,128,2048]{2,1,0:T(8,128)(2,1)}, u32[]{:S(2)}, u32[]{:S(2)}) collective-permute-start(bf16[2,128,2048]{2,1,0:T(8,128)(2,1)} %get-tuple-element.35), channel_id=1, source_target_pairs={{0,96},{32,0},{64,32},{96,64},{1,97},{33,1},{65,33},{97,65},{2,98}... | collective-permute-start | bytes 3145736 | tf_op jit(solution)/shard_map/ppermute | solution.py:389
  61.9 44.9 %copy-start.3 = (bf16[2,64,2048]{2,1,0:T(8,128)(2,1)}, bf16[2,64,2048]{2,1,0:T(8,128)(2,1)S(1)}, u32[]{:S(2)}) copy-start(bf16[2,64,2048]{2,1,0:T(8,128)(2,1)S(1)} %collective-permute-done.12.refs_10_) | copy-start | bytes 1572868
  61.9 66.5 %collective-permute-start.7 = (bf16[2,128,2048]{2,1,0:T(8,128)(2,1)}, bf16[2,128,2048]{2,1,0:T(8,128)(2,1)}, u32[]{:S(2)}, u32[]{:S(2)}) collective-permute-start(bf16[2,128,2048]{2,1,0:T(8,128)(2,1)} %get-tuple-element.36), channel_id=1, source_target_pairs={{0,64},{32,96},{64,0},{96,32},{1,65},{33,97},{65,1},{97,33},{2,66}... | collective-permute-start | bytes 3145736 | tf_op jit(solution)/shard_map/ppermute | solution.py:389
  72.2 51.9 %copy-start = (bf16[2,128,2048]{2,1,0:T(8,128)(2,1)}, bf16[2,128,2048]{2,1,0:T(8,128)(2,1)S(1)}, u32[]{:S(2)}) copy-start(bf16[2,128,2048]{2,1,0:T(8,128)(2,1)S(1)} %collective-permute-done.3.refs_7_) | copy-start | bytes 3145732
  72.2 68.3 %collective-permute-start.8 = (bf16[2,128,2048]{2,1,0:T(8,128)(2,1)}, bf16[2,128,2048]{2,1,0:T(8,128)(2,1)}, u32[]{:S(2)}, u32[]{:S(2)}) collective-permute-start(bf16[2,128,2048]{2,1,0:T(8,128)(2,1)} %get-tuple-element.37), channel_id=1, source_target_pairs={{0,32},{32,64},{64,96},{96,0},{1,33},{33,65},{65,97},{97,1},{2,34}... | collective-permute-start | bytes 3145736 | tf_op jit(solution)/shard_map/ppermute | solution.py:389
  73.5 50.6 %copy-start.1 = (bf16[2,128,2048]{2,1,0:T(8,128)(2,1)}, bf16[2,128,2048]{2,1,0:T(8,128)(2,1)S(1)}, u32[]{:S(2)}) copy-start(bf16[2,128,2048]{2,1,0:T(8,128)(2,1)S(1)} %collective-permute-done.4.refs_8_) | copy-start | bytes 3145732
  73.5 86.6 %collective-permute-start.13 = (bf16[2,64,2048]{2,1,0:T(8,128)(2,1)}, bf16[2,64,2048]{2,1,0:T(8,128)(2,1)}, u32[]{:S(2)}, u32[]{:S(2)}) collective-permute-start(bf16[2,64,2048]{2,1,0:T(8,128)(2,1)} %get-tuple-element.44), channel_id=1, source_target_pairs={{0,64},{32,96},{64,0},{96,32},{1,65},{33,97},{65,1},{97,33},{2,66}... | collective-permute-start | bytes 1572872 | tf_op jit(solution)/shard_map/ppermute | solution.py:389
  106.8 17.3 %copy-start.2 = (bf16[2,128,2048]{2,1,0:T(8,128)(2,1)}, bf16[2,128,2048]{2,1,0:T(8,128)(2,1)S(1)}, u32[]{:S(2)}) copy-start(bf16[2,128,2048]{2,1,0:T(8,128)(2,1)S(1)} %collective-permute-done.5.refs_9_) | copy-start | bytes 3145732
  106.8 53.3 %collective-permute-start.14 = (bf16[2,64,2048]{2,1,0:T(8,128)(2,1)}, bf16[2,64,2048]{2,1,0:T(8,128)(2,1)}, u32[]{:S(2)}, u32[]{:S(2)}) collective-permute-start(bf16[2,64,2048]{2,1,0:T(8,128)(2,1)} %get-tuple-element.45), channel_id=1, source_target_pairs={{0,96},{32,0},{64,32},{96,64},{1,97},{33,1},{65,33},{97,65},{2,98}... | collective-permute-start | bytes 1572872 | tf_op jit(solution)/shard_map/ppermute | solution.py:389
  128.4 51.7 %collective-permute-start.9 = (bf16[2,64,2048]{2,1,0:T(8,128)(2,1)}, bf16[2,64,2048]{2,1,0:T(8,128)(2,1)S(1)}, u32[]{:S(2)}, u32[]{:S(2)}) collective-permute-start(bf16[2,64,2048]{2,1,0:T(8,128)(2,1)} %get-tuple-element.40), channel_id=1, source_target_pairs={{0,32},{32,64},{64,96},{96,0},{1,33},{33,65},{65,97},{97,1},{2,34}... | collective-permute-start | bytes 1572872 | tf_op jit(solution)/shard_map/ppermute | solution.py:389
  128.4 51.7 %collective-permute-start.10 = (bf16[2,64,2048]{2,1,0:T(8,128)(2,1)}, bf16[2,64,2048]{2,1,0:T(8,128)(2,1)S(1)}, u32[]{:S(2)}, u32[]{:S(2)}) collective-permute-start(bf16[2,64,2048]{2,1,0:T(8,128)(2,1)} %get-tuple-element.41), channel_id=1, source_target_pairs={{0,64},{32,96},{64,0},{96,32},{1,65},{33,97},{65,1},{97,33},{2,66}... | collective-permute-start | bytes 1572872 | tf_op jit(solution)/shard_map/ppermute | solution.py:389
  140.5 39.7 %collective-permute-start.11 = (bf16[2,64,2048]{2,1,0:T(8,128)(2,1)}, bf16[2,64,2048]{2,1,0:T(8,128)(2,1)S(1)}, u32[]{:S(2)}, u32[]{:S(2)}) collective-permute-start(bf16[2,64,2048]{2,1,0:T(8,128)(2,1)} %get-tuple-element.42), channel_id=1, source_target_pairs={{0,96},{32,0},{64,32},{96,64},{1,97},{33,1},{65,33},{97,65},{2,98}... | collective-permute-start | bytes 1572872 | tf_op jit(solution)/shard_map/ppermute | solution.py:389
  160.1 6.2 %collective-permute-start.15 = (f32[2,64,128]{2,1,0:T(8,128)}, f32[2,64,128]{2,1,0:T(8,128)S(1)}, u32[]{:S(2)}, u32[]{:S(2)}) collective-permute-start(f32[2,64,128]{2,1,0:T(8,128)} %get-tuple-element.47), channel_id=1, source_target_pairs={{0,32},{32,64},{64,96},{96,0},{1,33},{33,65},{65,97},{97,1},{2,34}... | collective-permute-start | bytes 196616 | tf_op jit(solution)/shard_map/ppermute | solution.py:389
  160.2 19.9 %collective-permute-start.16 = (f32[2,64,128]{2,1,0:T(8,128)}, f32[2,64,128]{2,1,0:T(8,128)S(1)}, u32[]{:S(2)}, u32[]{:S(2)}) collective-permute-start(f32[2,64,128]{2,1,0:T(8,128)} %get-tuple-element.48), channel_id=1, source_target_pairs={{0,64},{32,96},{64,0},{96,32},{1,65},{33,97},{65,1},{97,33},{2,66}... | collective-permute-start | bytes 196616 | tf_op jit(solution)/shard_map/ppermute | solution.py:389
  166.3 13.8 %copy-start.7 = (f32[2,64,128]{2,1,0:T(8,128)}, f32[2,64,128]{2,1,0:T(8,128)S(1)}, u32[]{:S(2)}) copy-start(f32[2,64,128]{2,1,0:T(8,128)S(1)} %collective-permute-done.15.refs_16_) | copy-start | bytes 196612
  166.3 13.8 %collective-permute-start.17 = (f32[2,64,128]{2,1,0:T(8,128)}, f32[2,64,128]{2,1,0:T(8,128)S(1)}, u32[]{:S(2)}, u32[]{:S(2)}) collective-permute-start(f32[2,64,128]{2,1,0:T(8,128)} %get-tuple-element.49), channel_id=1, source_target_pairs={{0,96},{32,0},{64,32},{96,64},{1,97},{33,1},{65,33},{97,65},{2,98}... | collective-permute-start | bytes 196616 | tf_op jit(solution)/shard_map/ppermute | solution.py:389
  (8 other events, 7.0 us)
Sparse Core Ops, SparseCore 0:
  10.3 71.7 all-gather.1

commit v3 on v2

v3 whole, which is shorter than its diff:
```python
import functools
import math

import jax
import jax.numpy as jnp
from jax import lax
from jax.experimental import pallas as pl
from jax.experimental.pallas import tpu as pltpu
from jax.sharding import PartitionSpec as P

HEAD = 128
LEN = 128
ROWS = 64
GROUPS = 3
STORED = 6
SLOTS = 8
WIDTH = 2048
SCALE = 1.0 / math.sqrt(HEAD)
F32 = jnp.float32
BF16 = jnp.bfloat16
ANY = pl.BlockSpec(memory_space=pltpu.HBM)
SMEM = pl.BlockSpec(memory_space=pltpu.SMEM)
VMEM = pl.BlockSpec(memory_space=pltpu.VMEM)


def whole(*dims):
    return pl.BlockSpec(dims, lambda i: (0,) * len(dims))


TWIDTH = 1024
GANG = 8
HOME_GANG = 4
PARTS = ((0, 1536), (1536, 512))
HEADS = 16
BIG = 58
QSTEP = 512
GSTEP = 1024


def params(mib):
    return pltpu.CompilerParams(vmem_limit_bytes=mib << 20)


def cost(flops, data, exps=0):
    return pl.CostEstimate(flops=int(flops), bytes_accessed=int(data), transcendentals=int(exps))


def shape(dims, dtype):
    return jax.ShapeDtypeStruct(dims, dtype)


def dot(a, b, ca, cb):
    return lax.dot_general(a, b, (((ca,), (cb,)), ((), ())), preferred_element_type=F32)


def head(h):
    return slice(h * HEAD, (h + 1) * HEAD)


def route_kernel(me, table, pick, want, place, count):
    for k in range(SLOTS):
        pick[k] = 0
        want[k] = -1
    for d in range(4):
        count[d] = 0
    for g in range(GROUPS):
        for j in range(2):
            d = (table[g, j] - me[0] + 4) % 4
            k = d * 2 + jnp.minimum(count[d], 1)
            count[d] = count[d] + 1
            pick[k] = g
            want[k] = table[g, 2 + j]
            place[g * 2 + j] = k


def route(me, table):
    return pl.pallas_call(
        route_kernel,
        out_shape=(shape((SLOTS,), jnp.int32), shape((SLOTS,), jnp.int32), shape((SLOTS,), jnp.int32)),
        in_specs=[SMEM] * 2,
        out_specs=(SMEM, SMEM, SMEM),
        scratch_shapes=[pltpu.SMEM((4,), jnp.int32)],
        name="route",
    )(me, table)


def spread_kernel(pick, cot, *outs):
    for d in range(1, 4):
        for s in range(2):
            outs[d - 1][s] = cot[pick[2 * d + s]]


def spread(pick, cot):
    one = shape((2, ROWS, WIDTH), BF16)
    return pl.pallas_call(
        spread_kernel,
        out_shape=(one,) * 3,
        grid=(1,),
        in_specs=[SMEM, whole(GROUPS, ROWS, WIDTH)],
        out_specs=(whole(2, ROWS, WIDTH),) * 3,
        compiler_params=params(BIG),
        cost_estimate=cost(1, 20 * ROWS * WIDTH),
        name="spread",
    )(pick, cot)


def query_kernel(pick, hid, w, q, s1, s2, s3):
    part = dot(hid[...], w[...], 1, 0)
    for g in range(GROUPS):
        q[g] = part[g * ROWS : (g + 1) * ROWS].astype(BF16)
    for d, out in ((1, s1), (2, s2), (3, s3)):
        for s in range(2):
            out[s] = q[pick[2 * d + s]]


def query(pick, hidden, weights):
    depth = hidden.shape[1]
    piece = shape((2, ROWS, WIDTH), BF16)
    block = pl.BlockSpec((2, ROWS, QSTEP), lambda i: (0, 0, i))
    return pl.pallas_call(
        query_kernel,
        out_shape=(shape((GROUPS, ROWS, WIDTH), BF16), piece, piece, piece),
        grid=(WIDTH // QSTEP,),
        in_specs=[
            SMEM,
            whole(GROUPS * ROWS, depth),
            pl.BlockSpec((depth, QSTEP), lambda i: (0, i)),
        ],
        out_specs=(pl.BlockSpec((GROUPS, ROWS, QSTEP), lambda i: (0, 0, i)), block, block, block),
        compiler_params=params(BIG),
        cost_estimate=cost(2 * 192 * depth * WIDTH, 2 * depth * (192 + WIDTH)),
        name="query",
    )(pick, hidden, weights)


def rows_of(k, asked):
    d, s = divmod(k, 2)
    return asked[d][2 * d + s]


def fill_rows(asked, rows):
    for k in range(SLOTS):
        rows[k] = rows_of(k, asked)


def wait_slot(k, bufs, sems):
    for n, buf in enumerate(bufs):
        pltpu.make_async_copy(buf.at[k], buf.at[k], sems.at[k, n]).wait()


def collect_kernel(col, cw, *refs):
    asked, tables, outs, buf, sems, osems = refs[:4], refs[4:6], refs[6:9], refs[9], refs[10], refs[11]
    loads, stores = [], []
    for k in range(2, SLOTS):
        d, s = divmod(k, 2)
        row = jnp.maximum(rows_of(k, asked), 0)
        for n in range(2):
            here = buf.at[k - 2, n]
            loads.append(pltpu.make_async_copy(tables[n].at[row, :, pl.ds(col, cw)], here, sems.at[k - 2, n]))
            stores.append(pltpu.make_async_copy(here, outs[d - 1].at[s, n], osems.at[k - 2, n]))
    for one in loads:
        one.start()
    for one, two in zip(loads, stores):
        one.wait()
        two.start()
    for one in stores:
        one.wait()


def collect(asked, keys, values, col, cw):
    one = shape((2, 2, LEN, cw), BF16)
    return pl.pallas_call(
        functools.partial(collect_kernel, col, cw),
        out_shape=(one,) * 3,
        in_specs=[SMEM] * 4 + [ANY] * 2,
        out_specs=(ANY,) * 3,
        scratch_shapes=[
            pltpu.VMEM((SLOTS - 2, 2, LEN, cw), BF16),
            pltpu.SemaphoreType.DMA((SLOTS - 2, 2)),
            pltpu.SemaphoreType.DMA((SLOTS - 2, 2)),
        ],
        compiler_params=params(BIG),
        cost_estimate=cost(1, 48 * LEN * cw),
        name="collect",
    )(*asked, keys, values)


def home_kernel(col, cw, first, last, *refs):
    pick, place, want, q, c, keys, values = refs[:7]
    pairs, refs = refs[7:10], refs[10:]
    if not first:
        before, refs = refs[0], refs[2:]
    att, gq, refs = refs[0], refs[1], refs[2:]
    if last:
        backs, refs = refs[:4], refs[4:]
    qb, cb, kb, vb, res, sems, gsems = refs
    cols = pl.ds(col, cw)
    for g in range(GROUPS):
        pltpu.make_async_copy(q.at[g, :, cols], qb.at[g], gsems.at[g, 0]).start()
        pltpu.make_async_copy(c.at[g, :, cols], cb.at[g], gsems.at[g, 1]).start()
        for r in (2 * g, 2 * g + 1):
            at = place[r]
            for d in range(4):

                @pl.when(at // 2 == d)
                def _(r=r, d=d, at=at):
                    if d == 0:
                        s = jnp.maximum(want[at], 0)
                        ends = keys.at[s, :, cols], values.at[s, :, cols]
                    else:
                        ends = pairs[d - 1].at[at - 2 * d, 0], pairs[d - 1].at[at - 2 * d, 1]
                    pltpu.make_async_copy(ends[0], kb.at[r], sems.at[r, 0]).start()
                    pltpu.make_async_copy(ends[1], vb.at[r], sems.at[r, 1]).start()

    lane = lax.broadcasted_iota(jnp.int32, (ROWS, HEAD), 1)

    @pl.loop(0, GROUPS)
    def _(g):
        wait_slot(g, (qb, cb), gsems)
        for j in range(2):
            wait_slot(2 * g + j, (kb, vb), sems)
        stats = jnp.zeros((ROWS, HEAD), F32) if first else before[g]
        out = pl.ds(pl.multiple_of(g * ROWS, ROWS), ROWS)
        for base in range(0, cw // HEAD, HOME_GANG):
            span = [(h, j) for h in range(base, base + HOME_GANG) for j in range(2)]
            key = {(h, j): kb[2 * g + j, :, head(h)] for h, j in span}
            value = {(h, j): vb[2 * g + j, :, head(h)] for h, j in span}
            score = {(h, j): dot(qb[g, :, head(h)], key[h, j], 1, 1) * SCALE for h, j in span}
            slope = {(h, j): dot(cb[g, :, head(h)], value[h, j], 1, 1) for h, j in span}
            peak = {x: jnp.max(score[x], axis=1, keepdims=True) for x in span}
            e = {x: jnp.exp(score[x] - peak[x]) for x in span}
            total = {x: jnp.sum(e[x], axis=1, keepdims=True) for x in span}
            part = {x: dot(e[x].astype(BF16), value[x], 1, 0) for x in span}
            for h in range(base, base + HOME_GANG):
                top = jnp.maximum(peak[h, 0], peak[h, 1])
                scale = [jnp.exp(peak[h, j] - top) for j in range(2)]
                below = scale[0] * total[h, 0] + scale[1] * total[h, 1]
                scale = [x / below for x in scale]
                mix = part[h, 0] * scale[0] + part[h, 1] * scale[1]
                att[out, head(h)] = mix.astype(BF16)
                delta = jnp.sum(cb[g, :, head(h)].astype(F32) * mix, axis=1, keepdims=True)
                where = col // HEAD + h
                stats = jnp.where(lane == where, top + jnp.log(below), stats)
                stats = jnp.where(lane == HEADS + where, delta, stats)
                both = None
                for j in range(2):
                    gs = (e[h, j] * scale[j] * (slope[h, j] - delta) * SCALE).astype(BF16)
                    one = dot(gs, key[h, j], 1, 0)
                    both = one if both is None else both + one
                gq[out, head(h)] = both.astype(BF16)
        res[g] = stats

    if last:
        for d in range(4):
            for s in range(2):
                backs[d][s] = res[pick[2 * d + s]]


def home(pick, place, want, q, c, keys, values, pairs, before, last, col, cw):
    tokens = GROUPS * ROWS
    small = shape((2, ROWS, HEAD), F32)
    every = shape((GROUPS, ROWS, HEAD), F32)
    first = before is None
    extra = [] if first else [whole(GROUPS, ROWS, HEAD), ANY]
    out_shape = (shape((tokens, WIDTH), BF16), shape((tokens, cw), BF16))
    out_specs = (pl.BlockSpec((tokens, cw), lambda i: (0, col // cw)), whole(tokens, cw))
    keep = [pltpu.VMEM((GROUPS, ROWS, HEAD), F32)]
    if last:
        out_shape += (small,) * 4
        out_specs += (whole(2, ROWS, HEAD),) * 4
    else:
        out_shape += (every,)
        out_specs += (whole(GROUPS, ROWS, HEAD),)
        keep = []
    body = functools.partial(home_kernel, col, cw, first, last)
    if not last:
        inner = body

        def body(*refs):
            n = 10 + len(extra)
            ins, att, gq, res, rest = refs[:n], refs[n], refs[n + 1], refs[n + 2], refs[n + 3 :]
            inner(*ins, att, gq, *rest[:4], res, *rest[4:])

    return pl.pallas_call(
        body,
        out_shape=out_shape,
        grid=(1,),
        in_specs=[SMEM] * 3 + [ANY] * 7 + extra,
        out_specs=out_specs,
        scratch_shapes=[
            pltpu.VMEM((GROUPS, ROWS, cw), BF16),
            pltpu.VMEM((GROUPS, ROWS, cw), BF16),
            pltpu.VMEM((2 * GROUPS, LEN, cw), BF16),
            pltpu.VMEM((2 * GROUPS, LEN, cw), BF16),
            *keep,
            pltpu.SemaphoreType.DMA((2 * GROUPS, 2)),
            pltpu.SemaphoreType.DMA((GROUPS, 2)),
        ],
        input_output_aliases={} if first else {11: 0},
        compiler_params=params(BIG),
        cost_estimate=cost(6 * 8 * ROWS * LEN * cw, 30 * LEN * cw, 6 * ROWS * cw),
        name="home",
    )(pick, place, want, q, c, keys, values, *pairs, *(() if first else before))


def terms_kernel(tw, *refs):
    pick, asked, refs = refs[0], refs[1:5], refs[5:]
    q, c, keys, values, back = refs[:4], refs[4:8], refs[8], refs[9], refs[10:14]
    dk, dv, rows, seen, qb, cb, bb = refs[14:]
    fill_rows(asked, rows)
    for b in range(STORED):
        seen[b] = 0
    base = pl.program_id(0) * (tw // HEAD)
    for k in range(SLOTS):
        d, s = divmod(k, 2)
        at = pick[k] if d == 0 else s
        qb[k] = q[d][at]
        cb[k] = c[d][at]
        bb[k] = jnp.transpose(pltpu.roll(back[d][s], (HEAD - base) % HEAD, 1))

    def one_slot(k, row, add):
        for first in range(0, tw // HEAD, GANG):
            span = range(first, first + GANG)
            qs = [qb[k, :, head(h)] for h in span]
            cs = [cb[k, :, head(h)] for h in span]
            scores = [dot(keys[row, :, head(h)], x, 1, 1) * SCALE for h, x in zip(span, qs)]
            slopes = [dot(values[row, :, head(h)], x, 1, 1) for h, x in zip(span, cs)]
            probs = [jnp.exp(x - bb[k, h : h + 1, :]) for h, x in zip(span, scores)]
            gs = [
                (x * (y - bb[k, HEADS + h : HEADS + h + 1, :]) * SCALE).astype(BF16)
                for h, x, y in zip(span, probs, slopes)
            ]
            kts = [dot(x, y, 1, 0) for x, y in zip(gs, qs)]
            vts = [dot(x.astype(BF16), y, 1, 0) for x, y in zip(probs, cs)]
            for h, kt, vt in zip(span, kts, vts):
                if add:
                    kt = kt.astype(BF16).astype(F32) + dk[row, :, head(h)].astype(F32)
                    vt = vt.astype(BF16).astype(F32) + dv[row, :, head(h)].astype(F32)
                dk[row, :, head(h)] = kt.astype(BF16)
                dv[row, :, head(h)] = vt.astype(BF16)

    @pl.loop(0, SLOTS)
    def _(k):
        row = jnp.maximum(rows[k], 0)
        valid = rows[k] >= 0

        @pl.when(valid & (seen[row] == 0))
        def _():
            one_slot(k, row, False)

        @pl.when(valid & (seen[row] > 0))
        def _():
            one_slot(k, row, True)

        seen[row] = seen[row] + valid.astype(jnp.int32)

    for b in range(STORED):

        @pl.when(seen[b] == 0)
        def _(b=b):
            dk[b] = jnp.zeros((LEN, tw), BF16)
            dv[b] = jnp.zeros((LEN, tw), BF16)


def terms(pick, asked, q, c, keys, values, back):
    full = shape((STORED, LEN, WIDTH), BF16)
    tw = TWIDTH

    def part(x):
        return pl.BlockSpec((x.shape[0], x.shape[1], tw), lambda i: (0, 0, i))

    return pl.pallas_call(
        functools.partial(terms_kernel, tw),
        out_shape=(full,) * 2,
        grid=(WIDTH // tw,),
        in_specs=[SMEM] * 5 + [part(x) for x in (*q, *c, keys, values)] + [whole(2, ROWS, HEAD)] * 4,
        out_specs=(part(keys),) * 2,
        scratch_shapes=[
            pltpu.SMEM((SLOTS,), jnp.int32),
            pltpu.SMEM((STORED,), jnp.int32),
            pltpu.VMEM((SLOTS, ROWS, tw), BF16),
            pltpu.VMEM((SLOTS, ROWS, tw), BF16),
            pltpu.VMEM((SLOTS, HEAD, ROWS), F32),
        ],
        compiler_params=params(BIG),
        cost_estimate=cost(SLOTS * 8 * ROWS * LEN * WIDTH, 44 * LEN * WIDTH, SLOTS * ROWS * WIDTH),
        name="terms",
    )(pick, *asked, *q, *c, keys, values, *back)


def grad_kernel(gq, w, *refs):
    part = dot(gq[...], w[...], 1, 1)
    if len(refs) == 2:
        part = part + refs[0][...]
    refs[-1][...] = part.astype(refs[-1].dtype)


def grad(gq, weights, before, last, col, cw):
    depth, step = weights.shape[0], GSTEP
    first = before is None
    block = pl.BlockSpec((GROUPS * ROWS, step), lambda i: (0, i))
    return pl.pallas_call(
        grad_kernel,
        out_shape=shape((GROUPS * ROWS, depth), BF16 if last else F32),
        grid=(depth // step,),
        in_specs=[whole(GROUPS * ROWS, cw), pl.BlockSpec((step, cw), lambda i: (i, col // cw))]
        + ([] if first else [block]),
        out_specs=block,
        compiler_params=params(BIG),
        cost_estimate=cost(2 * 192 * depth * cw, 2 * depth * (384 + cw)),
        name="grad",
    )(gq, weights, *(() if first else (before,)))


def shift(x, d):
    return lax.ppermute(x, "enc", [(i, (i + d) % 4) for i in range(4)])


def to_owner(pieces):
    return [shift(x, d + 1) for d, x in enumerate(pieces)]


def to_home(pieces):
    return [shift(x, -(d + 1)) for d, x in enumerate(pieces)]


def after(values, *done):
    return lax.optimization_barrier((values, done))[0]


def per_device(hidden, query_weight, keys, values, owner, row, cotangent):
    me = lax.axis_index("enc").astype(jnp.int32).reshape(1)
    weights = lax.all_gather(query_weight, "fsdp", axis=0, tiled=True)
    pick, want, place = route(me, jnp.concatenate([owner, row], axis=1))
    cot = cotangent.reshape(GROUPS, ROWS, WIDTH)
    asked = [want] + to_owner([want] * 3)
    c = [cot] + to_owner(after(spread(pick, cot), asked[1]))
    sent = [collect(asked, keys, values, col, cw) for col, cw in PARTS]
    pairs = [to_home(after(pieces, c)) for pieces in sent]
    q, *sends = query(pick, hidden, weights)
    before, grad_hidden = None, None
    for (col, cw), pair in zip(PARTS, pairs):
        last = col + cw == WIDTH
        attended, gq, *back = home(pick, place, want, q, cot, keys, values, pair, before, last, col, cw)
        if before is None:
            qs = [q] + to_owner(after(sends, gq))
        before = (back[0], attended)
        grad_hidden = grad(gq, weights, grad_hidden, last, col, cw)
    back = [back[0]] + to_owner(back[1:])
    grad_keys, grad_values = terms(pick, asked, qs, c, keys, values, back)
    return attended, grad_hidden, grad_keys, grad_values


def solution(mesh):
    rows = P(("enc", "fsdp"), None)
    blocks = P(("enc", "fsdp"), None, None)
    return jax.shard_map(
        per_device,
        mesh=mesh,
        in_specs=(rows, P("fsdp", None), blocks, blocks, rows, rows, rows),
        out_specs=(rows, rows, blocks, blocks),
        check_vma=False,
    )
```

time: 204 us -> 199 us (0.975); the launches traced: 200 us -> 198 us
  starting transfers between devices: 46.2 us -> 28.5 us
  Pallas kernels: 57.3 us -> 67.1 us
  waiting for transfers between devices: 77.9 us -> 82.5 us
    ppermute x18, starting transfers between devices: 46.2 us -> 28.5 us  [shift(): return lax.ppermute(x, 'enc', [(i, (i + d) % 4) for i in range(4)])]
    pallas_call x6 -> x8, Pallas kernels: 53.6 us -> 63.4 us  [the longest x2 15.5 us: home(): pl.pallas_call(body, out_shape=out_shape, grid=(1,), in_specs=[SMEM] * 3...]
    ppermute x18, waiting for transfers between devices: 77.2 us -> 81.8 us  [shift(): return lax.ppermute(x, 'enc', [(i, (i + d) % 4) for i in range(4)])]
    unnamed x28 -> x38, local copies, waits for them, and re-layouts: 4.87 us -> 4.99 us
  transfers between devices with their start and end apart: 19 -> 19, of which waited for: 8 -> 2; matrix products, arithmetic and copies ran while one was open for 1% -> 1% of each run, Pallas kernels for 22% -> 27%
where the time goes in v3:
time: 199 us; the launch traced here: 198 us
  waiting for transfers between devices  82.5 us (41%)
  Pallas kernels  67.1 us (34%)
  starting transfers between devices  28.5 us (14%)
  between operations  14.3 us (7%)
  local copies, waits for them, and re-layouts  4.99 us (3%)
    ppermute x18, waiting for transfers between devices, shift(): return lax.ppermute(x, 'enc', [(i, (i + d) % 4) for i in range(4)])  81.8 us
    ppermute x18, starting transfers between devices, shift(): return lax.ppermute(x, 'enc', [(i, (i + d) % 4) for i in range(4)])  28.5 us
    pallas_call x2, Pallas kernels, home(): pl.pallas_call(body, out_shape=out_shape, grid=(1,), in_specs=[SMEM] * 3...  15.5 us
    pallas_call x2, Pallas kernels, grad(): pl.pallas_call(grad_kernel, out_shape=shape((GROUPS * ROWS, depth), BF16...  14.9 us
    pallas_call x1, Pallas kernels, terms(): pl.pallas_call(functools.partial(terms_kernel, tw), out_shape=(full,) * 2...  14.2 us
    pallas_call x1, Pallas kernels, query(): pl.pallas_call(query_kernel, out_shape=(shape((GROUPS, ROWS, WIDTH), BF16...  10.2 us
    pallas_call x2, Pallas kernels, collect(): pl.pallas_call(functools.partial(collect_kernel, col, cw), out_shape=(one...  8.63 us
    unnamed x38, local copies, waits for them, and re-layouts  4.99 us
  transfers between devices with their start and end apart: 19, of which 2 were waited for; matrix products, arithmetic and copies ran while one was open for 1% of the time, Pallas kernels for 27%

profile of v3, /device:TPU:106, one launch (start us, length us, event | category | flops | bytes accessed | tf_op | source)
XLA Modules:
  0.0 198.0 jit_solution(1342910461708563220)
XLA Ops:
  10.1 1.3 route.1
  11.4 1.6 collective-permute-start
  13.0 2.4 %spread.1 = (bf16[2,64,2048]{2,1,0:T(8,128)(2,1)}, bf16[2,64,2048]{2,1,0:T(8,128)(2,1)}, bf16[2,64,2048]{2,1,0:T(8,128)(2,1)}) custom-call(s32[8]{0:T(128)} %get-tuple-element.43.pick.refs_0_, bf16[3,64,2048]{2,1,0:T(8,128)(2,1)} %bitcast.2), custom_call_target="tpu_custom_call" | custom-call | flops 1 | bytes 2621440 | tf_op jit(solution)/shard_map/spread/pallas_call | solution.py:95
  15.4 1.3 collective-permute-start.3
  16.7 2.1 %collective-permute-start.4 = (bf16[2,64,2048]{2,1,0:T(8,128)(2,1)}, bf16[2,64,2048]{2,1,0:T(8,128)(2,1)S(1)}, u32[]{:S(2)}, u32[]{:S(2)}) collective-permute-start(bf16[2,64,2048]{2,1,0:T(8,128)(2,1)} %get-tuple-element.54), channel_id=1, source_target_pairs={{0,64},{32,96},{64,0},{96,32},{1,65},{33,97},{65,1},{97,33},{2,66}... | collective-permute-start | bytes 1572872 | tf_op jit(solution)/shard_map/ppermute | solution.py:416
  18.8 1.2 collective-permute-start.5
  20.4 2.5 %collective-permute-start.2 = (s32[8]{0:T(128)}, s32[8]{0:T(128)S(1)}, u32[]{:S(2)}, u32[]{:S(2)}) collective-permute-start(s32[8]{0:T(128)} %get-tuple-element.45.refs_0_.refs_2_.refs_1_), channel_id=1, source_target_pairs={{0,96},{32,0},{64,32},{96,64},{1,97},{33,1},{65,33},{97,65},{2,98}... | collective-permute-start | bytes 104 | tf_op jit(solution)/shard_map/ppermute | solution.py:416
  22.9 19.9 %collective-permute-done.1.refs_2_.refs_3_ = s32[8]{0:T(128)S(1)} collective-permute-done((s32[8]{0:T(128)}, s32[8]{0:T(128)S(1)}, u32[]{:S(2)}, u32[]{:S(2)}) %collective-permute-start.1) | collective-permute-done | bytes 64 | tf_op jit(solution)/shard_map/ppermute | solution.py:416
  43.9 5.4 %collect.3 = (bf16[2,2,128,1536]{3,2,1,0:T(8,128)(2,1)}, bf16[2,2,128,1536]{3,2,1,0:T(8,128)(2,1)}, bf16[2,2,128,1536]{3,2,1,0:T(8,128)(2,1)}) custom-call(s32[8]{0:T(128)} %get-tuple-element.45.refs_0_.refs_2_.refs_1_, s32[8]{0:T(128)} %copy-done.11, s32[8]{0:T(128)} %copy-done.12, s32[8]{0:T(128)} %copy-done.13, bf16[6,128,2048]{2,1,0:T(8,128)(2,1)} %refs_13_.1, ...), custom_call_target="tpu_custom_call" | custom-call | flops 1 | bytes 9437184 | tf_op jit(solution)/shard_map/collect/pallas_call | solution.py:172
  49.5 1.9 collective-permute-start.10
  51.4 2.5 %collective-permute-start.11 = (bf16[2,2,128,1536]{3,2,1,0:T(8,128)(2,1)}, bf16[2,2,128,1536]{3,2,1,0:T(8,128)(2,1)}, u32[]{:S(2)}, u32[]{:S(2)}) collective-permute-start(bf16[2,2,128,1536]{3,2,1,0:T(8,128)(2,1)} %get-tuple-element.64), channel_id=1, source_target_pairs={{0,32},{32,64},{64,96},{96,0},{1,33},{33,65},{65,97},{97,1},{2,34}... | collective-permute-start | bytes 4718600 | tf_op jit(solution)/shard_map/ppermute | solution.py:416
  54.0 3.2 %collect.2 = (bf16[2,2,128,512]{3,2,1,0:T(8,128)(2,1)}, bf16[2,2,128,512]{3,2,1,0:T(8,128)(2,1)}, bf16[2,2,128,512]{3,2,1,0:T(8,128)(2,1)}) custom-call(s32[8]{0:T(128)} %get-tuple-element.45.refs_0_.refs_2_.refs_1_, s32[8]{0:T(128)} %copy-done.11, s32[8]{0:T(128)} %copy-done.12, s32[8]{0:T(128)} %copy-done.13, bf16[6,128,2048]{2,1,0:T(8,128)(2,1)} %refs_13_.1, ...), custom_call_target="tpu_custom_call" | custom-call | flops 1 | bytes 3145728 | tf_op jit(solution)/shard_map/collect/pallas_call | solution.py:172
  57.3 1.7 collective-permute-start.7
  59.0 61.8 %collective-permute-done.9.refs_7_ = bf16[2,2,128,1536]{3,2,1,0:T(8,128)(2,1)S(1)} collective-permute-done((bf16[2,2,128,1536]{3,2,1,0:T(8,128)(2,1)}, bf16[2,2,128,1536]{3,2,1,0:T(8,128)(2,1)S(1)}, u32[]{:S(2)}, u32[]{:S(2)}) %collective-permute-start.9) | collective-permute-done | bytes 1572896 | tf_op jit(solution)/shard_map/ppermute | solution.py:416
  120.8 10.2 %query.1 = (bf16[3,64,2048]{2,1,0:T(8,128)(2,1)}, bf16[2,64,2048]{2,1,0:T(8,128)(2,1)}, bf16[2,64,2048]{2,1,0:T(8,128)(2,1)}, bf16[2,64,2048]{2,1,0:T(8,128)(2,1)}) custom-call(s32[8]{0:T(128)} %get-tuple-element.43.pick.refs_0_, bf16[192,4096]{1,0:T(8,128)(2,1)} %hid.1, bf16[4096,2048]{1,0:T(8,128)(2,1)} %all-gather.2.cloned.1.call-done.w), custom_call_target="tpu_custom_call" | custom-call | flops 3221225472 | bytes 18350080 | tf_op jit(solution)/shard_map/query/pallas_call | solution.py:120
  131.0 1.1 copy-done.1
  132.1 10.0 %home.2 = (bf16[192,2048]{1,0:T(8,128)(2,1)}, bf16[192,1536]{1,0:T(8,128)(2,1)}, f32[3,64,128]{2,1,0:T(8,128)}) custom-call(s32[8]{0:T(128)} %get-tuple-element.43.pick.refs_0_, s32[8]{0:T(128)} %get-tuple-element.44.refs_1_, s32[8]{0:T(128)} %get-tuple-element.45.refs_0_.refs_2_.refs_1_, bf16[3,64,2048]{2,1,0:T(8,128)(2,1)} %get-tuple-element.46.refs_3_.refs_5_, ...), custom_call_target="tpu_custom_call" | custom-call | flops 603979776 | bytes 5898240 | tf_op jit(solution)/shard_map/home/pallas_call | solution.py:284
  142.1 3.0 %collective-permute-start.12 = (bf16[2,64,2048]{2,1,0:T(8,128)(2,1)S(1)}, bf16[2,64,2048]{2,1,0:T(8,128)(2,1)S(1)}, u32[]{:S(2)}, u32[]{:S(2)}) collective-permute-start(bf16[2,64,2048]{2,1,0:T(8,128)(2,1)S(1)} %copy-done.16), channel_id=1, source_target_pairs={{0,32},{32,64},{64,96},{96,0},{1,33},{33,65},{65,97},{97,1},{2,34}... | collective-permute-start | bytes 1572872 | tf_op jit(solution)/shard_map/ppermute | solution.py:416
  145.6 2.9 %collective-permute-start.14 = (bf16[2,64,2048]{2,1,0:T(8,128)(2,1)S(1)}, bf16[2,64,2048]{2,1,0:T(8,128)(2,1)S(1)}, u32[]{:S(2)}, u32[]{:S(2)}) collective-permute-start(bf16[2,64,2048]{2,1,0:T(8,128)(2,1)S(1)} %copy-done.14), channel_id=1, source_target_pairs={{0,96},{32,0},{64,32},{96,64},{1,97},{33,1},{65,33},{97,65},{2,98}... | collective-permute-start | bytes 1572872 | tf_op jit(solution)/shard_map/ppermute | solution.py:416
  148.6 5.5 %home.3 = (bf16[192,2048]{1,0:T(8,128)(2,1)}, bf16[192,512]{1,0:T(8,128)(2,1)}, f32[2,64,128]{2,1,0:T(8,128)}, f32[2,64,128]{2,1,0:T(8,128)}, f32[2,64,128]{2,1,0:T(8,128)}, /*index=5*/f32[2,64,128]{2,1,0:T(8,128)}) custom-call(s32[8]{0:T(128)} %get-tuple-element.43.pick.refs_0_, s32[8]{0:T(128)} %get-tuple-element.44.refs_1_, ...), custom_call_target="tpu_custom_call", output_to_operand_aliasing={{0}: (11, {})} | custom-call | flops 201326592 | bytes 1966080 | tf_op jit(solution)/shard_map/home/pallas_call | solution.py:284
  154.2 6.2 %collective-permute-start.16 = (f32[2,64,128]{2,1,0:T(8,128)}, f32[2,64,128]{2,1,0:T(8,128)S(1)}, u32[]{:S(2)}, u32[]{:S(2)}) collective-permute-start(f32[2,64,128]{2,1,0:T(8,128)} %get-tuple-element.78), channel_id=1, source_target_pairs={{0,64},{32,96},{64,0},{96,32},{1,65},{33,97},{65,1},{97,33},{2,66}... | collective-permute-start | bytes 196616 | tf_op jit(solution)/shard_map/ppermute | solution.py:416
  160.4 8.9 %grad.2.refs_0_ = f32[192,4096]{1,0:T(8,128)} custom-call(bf16[192,1536]{1,0:T(8,128)(2,1)} %get-tuple-element.69.gq, bf16[4096,2048]{1,0:T(8,128)(2,1)} %all-gather.2.cloned.1.call-done.w), custom_call_target="tpu_custom_call" | custom-call | flops 2415919104 | bytes 15728640 | tf_op jit(solution)/shard_map/grad/pallas_call | solution.py:402
  169.7 6.0 %grad.3 = bf16[192,4096]{1,0:T(8,128)(2,1)} custom-call(bf16[192,512]{1,0:T(8,128)(2,1)} %get-tuple-element.68.gq, bf16[4096,2048]{1,0:T(8,128)(2,1)} %all-gather.2.cloned.1.call-done.w, f32[192,4096]{1,0:T(8,128)} %grad.2.refs_0_), custom_call_target="tpu_custom_call" | custom-call | flops 805306368 | bytes 7340032 | tf_op jit(solution)/shard_map/grad/pallas_call | solution.py:402
  177.0 14.2 %terms.1 = (bf16[6,128,2048]{2,1,0:T(8,128)(2,1)}, bf16[6,128,2048]{2,1,0:T(8,128)(2,1)}) custom-call(s32[8]{0:T(128)} %get-tuple-element.43.pick.refs_0_, s32[8]{0:T(128)} %get-tuple-element.45.refs_0_.refs_2_.refs_1_, s32[8]{0:T(128)} %copy-done.11, s32[8]{0:T(128)} %copy-done.12, s32[8]{0:T(128)} %copy-done.13, ...), custom_call_target="tpu_custom_call" | custom-call | flops 1073741824 | bytes 11534336 | tf_op jit(solution)/shard_map/terms/pallas_call | solution.py:372
  (64 shorter events, 6.9 us)
Async XLA Ops:
  7.2 113.6 %all-gather.2.cloned.1.call-start = ((), (), s32[]{:S(2)}) async-start(), calls=%async_computation | async-start | bytes 17301504 | tf_op jit(solution)/shard_map/all_gather | solution.py:433
  11.4 4.0 %collective-permute-start = (s32[8]{0:T(128)}, s32[8]{0:T(128)S(1)}, u32[]{:S(2)}, u32[]{:S(2)}) collective-permute-start(s32[8]{0:T(128)} %get-tuple-element.45.refs_0_.refs_2_.refs_1_), channel_id=1, source_target_pairs={{0,32},{32,64},{64,96},{96,0},{1,33},{33,65},{65,97},{97,1},{2,34}... | collective-permute-start | bytes 104 | tf_op jit(solution)/shard_map/ppermute | solution.py:416
  15.4 27.4 %copy-start.11 = (s32[8]{0:T(128)}, s32[8]{0:T(128)S(1)}, u32[]{:S(2)}) copy-start(s32[8]{0:T(128)S(1)} %collective-permute-done.refs_1_.refs_2_) | copy-start | bytes 100
  15.4 34.0 %collective-permute-start.3 = (bf16[2,64,2048]{2,1,0:T(8,128)(2,1)}, bf16[2,64,2048]{2,1,0:T(8,128)(2,1)S(1)}, u32[]{:S(2)}, u32[]{:S(2)}) collective-permute-start(bf16[2,64,2048]{2,1,0:T(8,128)(2,1)} %get-tuple-element.53), channel_id=1, source_target_pairs={{0,32},{32,64},{64,96},{96,0},{1,33},{33,65},{65,97},{97,1},{2,34}... | collective-permute-start | bytes 1572872 | tf_op jit(solution)/shard_map/ppermute | solution.py:416
  16.7 32.7 %collective-permute-start.4 = (bf16[2,64,2048]{2,1,0:T(8,128)(2,1)}, bf16[2,64,2048]{2,1,0:T(8,128)(2,1)S(1)}, u32[]{:S(2)}, u32[]{:S(2)}) collective-permute-start(bf16[2,64,2048]{2,1,0:T(8,128)(2,1)} %get-tuple-element.54), channel_id=1, source_target_pairs={{0,64},{32,96},{64,0},{96,32},{1,65},{33,97},{65,1},{97,33},{2,66}... | collective-permute-start | bytes 1572872 | tf_op jit(solution)/shard_map/ppermute | solution.py:416
  18.8 30.7 %collective-permute-start.5 = (bf16[2,64,2048]{2,1,0:T(8,128)(2,1)}, bf16[2,64,2048]{2,1,0:T(8,128)(2,1)S(1)}, u32[]{:S(2)}, u32[]{:S(2)}) collective-permute-start(bf16[2,64,2048]{2,1,0:T(8,128)(2,1)} %get-tuple-element.55), channel_id=1, source_target_pairs={{0,96},{32,0},{64,32},{96,64},{1,97},{33,1},{65,33},{97,65},{2,98}... | collective-permute-start | bytes 1572872 | tf_op jit(solution)/shard_map/ppermute | solution.py:416
  20.0 22.8 %collective-permute-start.1 = (s32[8]{0:T(128)}, s32[8]{0:T(128)S(1)}, u32[]{:S(2)}, u32[]{:S(2)}) collective-permute-start(s32[8]{0:T(128)} %get-tuple-element.45.refs_0_.refs_2_.refs_1_), channel_id=1, source_target_pairs={{0,64},{32,96},{64,0},{96,32},{1,65},{33,97},{65,1},{97,33},{2,66}... | collective-permute-start | bytes 104 | tf_op jit(solution)/shard_map/ppermute | solution.py:416
  20.4 22.4 %collective-permute-start.2 = (s32[8]{0:T(128)}, s32[8]{0:T(128)S(1)}, u32[]{:S(2)}, u32[]{:S(2)}) collective-permute-start(s32[8]{0:T(128)} %get-tuple-element.45.refs_0_.refs_2_.refs_1_), channel_id=1, source_target_pairs={{0,96},{32,0},{64,32},{96,64},{1,97},{33,1},{65,33},{97,65},{2,98}... | collective-permute-start | bytes 104 | tf_op jit(solution)/shard_map/ppermute | solution.py:416
  49.5 71.3 %collective-permute-start.9 = (bf16[2,2,128,1536]{3,2,1,0:T(8,128)(2,1)}, bf16[2,2,128,1536]{3,2,1,0:T(8,128)(2,1)S(1)}, u32[]{:S(2)}, u32[]{:S(2)}) collective-permute-start(bf16[2,2,128,1536]{3,2,1,0:T(8,128)(2,1)} %get-tuple-element.62), channel_id=1, source_target_pairs={{0,96},{32,0},{64,32},{96,64},{1,97},{33,1},{65,33},{97,65},{2,98}... | collective-permute-start | bytes 4718600 | tf_op jit(solution)/shard_map/ppermute | solution.py:416
  49.5 81.5 %collective-permute-start.10 = (bf16[2,2,128,1536]{3,2,1,0:T(8,128)(2,1)}, bf16[2,2,128,1536]{3,2,1,0:T(8,128)(2,1)S(1)}, u32[]{:S(2)}, u32[]{:S(2)}) collective-permute-start(bf16[2,2,128,1536]{3,2,1,0:T(8,128)(2,1)} %get-tuple-element.63), channel_id=1, source_target_pairs={{0,64},{32,96},{64,0},{96,32},{1,65},{33,97},{65,1},{97,33},{2,66}... | collective-permute-start | bytes 4718600 | tf_op jit(solution)/shard_map/ppermute | solution.py:416
  51.4 79.6 %collective-permute-start.11 = (bf16[2,2,128,1536]{3,2,1,0:T(8,128)(2,1)}, bf16[2,2,128,1536]{3,2,1,0:T(8,128)(2,1)}, u32[]{:S(2)}, u32[]{:S(2)}) collective-permute-start(bf16[2,2,128,1536]{3,2,1,0:T(8,128)(2,1)} %get-tuple-element.64), channel_id=1, source_target_pairs={{0,32},{32,64},{64,96},{96,0},{1,33},{33,65},{65,97},{97,1},{2,34}... | collective-permute-start | bytes 4718600 | tf_op jit(solution)/shard_map/ppermute | solution.py:416
  57.2 88.5 %collective-permute-start.6 = (bf16[2,2,128,512]{3,2,1,0:T(8,128)(2,1)}, bf16[2,2,128,512]{3,2,1,0:T(8,128)(2,1)}, u32[]{:S(2)}, u32[]{:S(2)}) collective-permute-start(bf16[2,2,128,512]{3,2,1,0:T(8,128)(2,1)} %get-tuple-element.56), channel_id=1, source_target_pairs={{0,96},{32,0},{64,32},{96,64},{1,97},{33,1},{65,33},{97,65},{2,98}... | collective-permute-start | bytes 1572872 | tf_op jit(solution)/shard_map/ppermute | solution.py:416
  57.3 91.3 %collective-permute-start.7 = (bf16[2,2,128,512]{3,2,1,0:T(8,128)(2,1)}, bf16[2,2,128,512]{3,2,1,0:T(8,128)(2,1)}, u32[]{:S(2)}, u32[]{:S(2)}) collective-permute-start(bf16[2,2,128,512]{3,2,1,0:T(8,128)(2,1)} %get-tuple-element.57), channel_id=1, source_target_pairs={{0,64},{32,96},{64,0},{96,32},{1,65},{33,97},{65,1},{97,33},{2,66}... | collective-permute-start | bytes 1572872 | tf_op jit(solution)/shard_map/ppermute | solution.py:416
  120.8 10.2 %copy-start = (bf16[2,2,128,1536]{3,2,1,0:T(8,128)(2,1)}, bf16[2,2,128,1536]{3,2,1,0:T(8,128)(2,1)S(1)}, u32[]{:S(2)}) copy-start(bf16[2,2,128,1536]{3,2,1,0:T(8,128)(2,1)S(1)} %collective-permute-done.9.refs_7_) | copy-start | bytes 4718596
  120.8 27.8 %collective-permute-start.8 = (bf16[2,2,128,512]{3,2,1,0:T(8,128)(2,1)}, bf16[2,2,128,512]{3,2,1,0:T(8,128)(2,1)}, u32[]{:S(2)}, u32[]{:S(2)}) collective-permute-start(bf16[2,2,128,512]{3,2,1,0:T(8,128)(2,1)} %get-tuple-element.58), channel_id=1, source_target_pairs={{0,32},{32,64},{64,96},{96,0},{1,33},{33,65},{65,97},{97,1},{2,34}... | collective-permute-start | bytes 1572872 | tf_op jit(solution)/shard_map/ppermute | solution.py:416
  132.1 13.0 %copy-start.15 = (bf16[2,64,2048]{2,1,0:T(8,128)(2,1)S(1)}, bf16[2,64,2048]{2,1,0:T(8,128)(2,1)}, u32[]{:S(2)}) copy-start(bf16[2,64,2048]{2,1,0:T(8,128)(2,1)} %get-tuple-element.74) | copy-start | bytes 1572868
  132.1 13.5 %copy-start.14 = (bf16[2,64,2048]{2,1,0:T(8,128)(2,1)S(1)}, bf16[2,64,2048]{2,1,0:T(8,128)(2,1)}, u32[]{:S(2)}) copy-start(bf16[2,64,2048]{2,1,0:T(8,128)(2,1)} %get-tuple-element.75) | copy-start | bytes 1572868
  142.1 33.6 %collective-permute-start.12 = (bf16[2,64,2048]{2,1,0:T(8,128)(2,1)S(1)}, bf16[2,64,2048]{2,1,0:T(8,128)(2,1)S(1)}, u32[]{:S(2)}, u32[]{:S(2)}) collective-permute-start(bf16[2,64,2048]{2,1,0:T(8,128)(2,1)S(1)} %copy-done.16), channel_id=1, source_target_pairs={{0,32},{32,64},{64,96},{96,0},{1,33},{33,65},{65,97},{97,1},{2,34}... | collective-permute-start | bytes 1572872 | tf_op jit(solution)/shard_map/ppermute | solution.py:416
  145.1 30.7 %collective-permute-start.13 = (bf16[2,64,2048]{2,1,0:T(8,128)(2,1)S(1)}, bf16[2,64,2048]{2,1,0:T(8,128)(2,1)S(1)}, u32[]{:S(2)}, u32[]{:S(2)}) collective-permute-start(bf16[2,64,2048]{2,1,0:T(8,128)(2,1)S(1)} %copy-done.15), channel_id=1, source_target_pairs={{0,64},{32,96},{64,0},{96,32},{1,65},{33,97},{65,1},{97,33},{2,66}... | collective-permute-start | bytes 1572872 | tf_op jit(solution)/shard_map/ppermute | solution.py:416
  145.6 30.2 %collective-permute-start.14 = (bf16[2,64,2048]{2,1,0:T(8,128)(2,1)S(1)}, bf16[2,64,2048]{2,1,0:T(8,128)(2,1)S(1)}, u32[]{:S(2)}, u32[]{:S(2)}) collective-permute-start(bf16[2,64,2048]{2,1,0:T(8,128)(2,1)S(1)} %copy-done.14), channel_id=1, source_target_pairs={{0,96},{32,0},{64,32},{96,64},{1,97},{33,1},{65,33},{97,65},{2,98}... | collective-permute-start | bytes 1572872 | tf_op jit(solution)/shard_map/ppermute | solution.py:416
  154.1 15.1 %collective-permute-start.15 = (f32[2,64,128]{2,1,0:T(8,128)}, f32[2,64,128]{2,1,0:T(8,128)S(1)}, u32[]{:S(2)}, u32[]{:S(2)}) collective-permute-start(f32[2,64,128]{2,1,0:T(8,128)} %get-tuple-element.77), channel_id=1, source_target_pairs={{0,32},{32,64},{64,96},{96,0},{1,33},{33,65},{65,97},{97,1},{2,34}... | collective-permute-start | bytes 196616 | tf_op jit(solution)/shard_map/ppermute | solution.py:416
  154.2 15.0 %copy-start.17 = (f32[2,64,128]{2,1,0:T(8,128)S(1)}, f32[2,64,128]{2,1,0:T(8,128)}, u32[]{:S(2)}) copy-start(f32[2,64,128]{2,1,0:T(8,128)} %get-tuple-element.79) | copy-start | bytes 196612
  154.2 21.5 %collective-permute-start.16 = (f32[2,64,128]{2,1,0:T(8,128)}, f32[2,64,128]{2,1,0:T(8,128)S(1)}, u32[]{:S(2)}, u32[]{:S(2)}) collective-permute-start(f32[2,64,128]{2,1,0:T(8,128)} %get-tuple-element.78), channel_id=1, source_target_pairs={{0,64},{32,96},{64,0},{96,32},{1,65},{33,97},{65,1},{97,33},{2,66}... | collective-permute-start | bytes 196616 | tf_op jit(solution)/shard_map/ppermute | solution.py:416
  169.2 6.5 %collective-permute-start.17 = (f32[2,64,128]{2,1,0:T(8,128)S(1)}, f32[2,64,128]{2,1,0:T(8,128)S(1)}, u32[]{:S(2)}, u32[]{:S(2)}) collective-permute-start(f32[2,64,128]{2,1,0:T(8,128)S(1)} %copy-done.17), channel_id=1, source_target_pairs={{0,96},{32,0},{64,32},{96,64},{1,97},{33,1},{65,33},{97,65},{2,98}... | collective-permute-start | bytes 196616 | tf_op jit(solution)/shard_map/ppermute | solution.py:416
  (13 other events, 46.2 us)
Sparse Core Ops, SparseCore 0:
  10.3 71.7 all-gather.1

commit v4 on v3

--- a/solution.py
+++ b/solution.py
@@ -436,8 +436,8 @@
     asked = [want] + to_owner([want] * 3)
     c = [cot] + to_owner(after(spread(pick, cot), asked[1]))
     sent = [collect(asked, keys, values, col, cw) for col, cw in PARTS]
-    pairs = [to_home(after(pieces, c)) for pieces in sent]
     q, *sends = query(pick, hidden, weights)
+    pairs = [to_home(after(sent[0], c)), to_home([*after(sent[1][:2], c), after(sent[1][2], c, q)])]
     before, grad_hidden = None, None
     for (col, cw), pair in zip(PARTS, pairs):
         last = col + cw == WIDTH

time: 199 us -> 205 us (1.030)
  starting transfers between devices: 28.5 us -> 42.7 us
  waiting for transfers between devices: 82.5 us -> 74.9 us
    ppermute x18, waiting for transfers between devices: 81.8 us -> 51 us  [shift(): return lax.ppermute(x, 'enc', [(i, (i + d) % 4) for i in range(4)])]
    all_gather x1, waiting for transfers between devices: 0.01 us -> 23.2 us  [per_device(): weights = lax.all_gather(query_weight, 'fsdp', axis=0, tiled=True)]
    ppermute x18, starting transfers between devices: 28.5 us -> 42.7 us  [shift(): return lax.ppermute(x, 'enc', [(i, (i + d) % 4) for i in range(4)])]
    unnamed x38 -> x34, local copies, waits for them, and re-layouts: 4.99 us -> 4.41 us
  transfers between devices with their start and end apart: 19 -> 19, of which waited for: 2 -> 4; matrix products, arithmetic and copies ran while one was open for 1% -> 1% of each run, Pallas kernels for 27% -> 26%
where the time goes in v4:
time: 205 us; the launch traced here: 204 us
  waiting for transfers between devices  74.9 us (37%)
  Pallas kernels  66.6 us (32%)
  starting transfers between devices  42.7 us (21%)
  between operations  14.3 us (7%)
  local copies, waits for them, and re-layouts  4.41 us (2%)
    ppermute x18, waiting for transfers between devices, shift(): return lax.ppermute(x, 'enc', [(i, (i + d) % 4) for i in range(4)])  51 us
    ppermute x18, starting transfers between devices, shift(): return lax.ppermute(x, 'enc', [(i, (i + d) % 4) for i in range(4)])  42.7 us
    all_gather x1, waiting for transfers between devices, per_device(): weights = lax.all_gather(query_weight, 'fsdp', axis=0, tiled=True)  23.2 us
    pallas_call x2, Pallas kernels, home(): pl.pallas_call(body, out_shape=out_shape, grid=(1,), in_specs=[SMEM] * 3...  15.4 us
    pallas_call x2, Pallas kernels, grad(): pl.pallas_call(grad_kernel, out_shape=shape((GROUPS * ROWS, depth), BF16...  15.1 us
    pallas_call x1, Pallas kernels, terms(): pl.pallas_call(functools.partial(terms_kernel, tw), out_shape=(full,) * 2...  14.3 us
    pallas_call x1, Pallas kernels, query(): pl.pallas_call(query_kernel, out_shape=(shape((GROUPS, ROWS, WIDTH), BF16...  9.56 us
    pallas_call x2, Pallas kernels, collect(): pl.pallas_call(functools.partial(collect_kernel, col, cw), out_shape=(one...  8.6 us
  transfers between devices with their start and end apart: 19, of which 4 were waited for; matrix products, arithmetic and copies ran while one was open for 1% of the time, Pallas kernels for 26%

profile of v4, /device:TPU:106, one launch (start us, length us, event | category | flops | bytes accessed | tf_op | source)
XLA Modules:
  0.0 203.6 jit_solution(6233457388406498594)
XLA Ops:
  11.4 1.6 collective-permute-start
  13.0 2.4 %spread.1 = (bf16[2,64,2048]{2,1,0:T(8,128)(2,1)}, bf16[2,64,2048]{2,1,0:T(8,128)(2,1)}, bf16[2,64,2048]{2,1,0:T(8,128)(2,1)}) custom-call(s32[8]{0:T(128)} %get-tuple-element.43.pick.refs_0_, bf16[3,64,2048]{2,1,0:T(8,128)(2,1)} %bitcast.2), custom_call_target="tpu_custom_call" | custom-call | flops 1 | bytes 2621440 | tf_op jit(solution)/shard_map/spread/pallas_call | solution.py:95
  15.4 1.4 collective-permute-start.3
  16.8 2.2 %collective-permute-start.4 = (bf16[2,64,2048]{2,1,0:T(8,128)(2,1)}, bf16[2,64,2048]{2,1,0:T(8,128)(2,1)S(1)}, u32[]{:S(2)}, u32[]{:S(2)}) collective-permute-start(bf16[2,64,2048]{2,1,0:T(8,128)(2,1)} %get-tuple-element.53), channel_id=1, source_target_pairs={{0,64},{32,96},{64,0},{96,32},{1,65},{33,97},{65,1},{97,33},{2,66}... | collective-permute-start | bytes 1572872 | tf_op jit(solution)/shard_map/ppermute | solution.py:416
  20.4 2.7 %collective-permute-start.2 = (s32[8]{0:T(128)}, s32[8]{0:T(128)S(1)}, u32[]{:S(2)}, u32[]{:S(2)}) collective-permute-start(s32[8]{0:T(128)} %get-tuple-element.45.refs_0_.refs_2_.refs_1_), channel_id=1, source_target_pairs={{0,96},{32,0},{64,32},{96,64},{1,97},{33,1},{65,33},{97,65},{2,98}... | collective-permute-start | bytes 104 | tf_op jit(solution)/shard_map/ppermute | solution.py:416
  23.0 19.8 %collective-permute-done.1.refs_2_.refs_3_ = s32[8]{0:T(128)S(1)} collective-permute-done((s32[8]{0:T(128)}, s32[8]{0:T(128)S(1)}, u32[]{:S(2)}, u32[]{:S(2)}) %collective-permute-start.1) | collective-permute-done | bytes 64 | tf_op jit(solution)/shard_map/ppermute | solution.py:416
  43.8 5.5 %collect.3 = (bf16[2,2,128,1536]{3,2,1,0:T(8,128)(2,1)}, bf16[2,2,128,1536]{3,2,1,0:T(8,128)(2,1)}, bf16[2,2,128,1536]{3,2,1,0:T(8,128)(2,1)}) custom-call(s32[8]{0:T(128)} %get-tuple-element.45.refs_0_.refs_2_.refs_1_, s32[8]{0:T(128)} %copy-done.12, s32[8]{0:T(128)} %copy-done.13, s32[8]{0:T(128)} %copy-done.14, bf16[6,128,2048]{2,1,0:T(8,128)(2,1)} %refs_13_.1, ...), custom_call_target="tpu_custom_call" | custom-call | flops 1 | bytes 9437184 | tf_op jit(solution)/shard_map/collect/pallas_call | solution.py:172
  49.4 1.6 collective-permute-start.10
  51.0 2.5 %collective-permute-start.11 = (bf16[2,2,128,1536]{3,2,1,0:T(8,128)(2,1)}, bf16[2,2,128,1536]{3,2,1,0:T(8,128)(2,1)}, u32[]{:S(2)}, u32[]{:S(2)}) collective-permute-start(bf16[2,2,128,1536]{3,2,1,0:T(8,128)(2,1)} %get-tuple-element.64), channel_id=1, source_target_pairs={{0,32},{32,64},{64,96},{96,0},{1,33},{33,65},{65,97},{97,1},{2,34}... | collective-permute-start | bytes 4718600 | tf_op jit(solution)/shard_map/ppermute | solution.py:416
  53.6 3.1 %collect.2 = (bf16[2,2,128,512]{3,2,1,0:T(8,128)(2,1)}, bf16[2,2,128,512]{3,2,1,0:T(8,128)(2,1)}, bf16[2,2,128,512]{3,2,1,0:T(8,128)(2,1)}) custom-call(s32[8]{0:T(128)} %get-tuple-element.45.refs_0_.refs_2_.refs_1_, s32[8]{0:T(128)} %copy-done.12, s32[8]{0:T(128)} %copy-done.13, s32[8]{0:T(128)} %copy-done.14, bf16[6,128,2048]{2,1,0:T(8,128)(2,1)} %refs_13_.1, ...), custom_call_target="tpu_custom_call" | custom-call | flops 1 | bytes 3145728 | tf_op jit(solution)/shard_map/collect/pallas_call | solution.py:172
  56.8 2.0 collective-permute-start.7
  58.8 23.2 %all-gather.2.cloned.1.call-done.w = bf16[4096,2048]{1,0:T(8,128)(2,1)} async-done(((bf16[128,2048]{1,0:T(8,128)(2,1)}), bf16[4096,2048]{1,0:T(8,128)(2,1)}) %all-gather.2.cloned.1.call-update) | async-done | bytes 16777232 | tf_op jit(solution)/shard_map/all_gather | solution.py:433
  82.1 9.6 %query.1 = (bf16[3,64,2048]{2,1,0:T(8,128)(2,1)}, bf16[2,64,2048]{2,1,0:T(8,128)(2,1)}, bf16[2,64,2048]{2,1,0:T(8,128)(2,1)}, bf16[2,64,2048]{2,1,0:T(8,128)(2,1)}) custom-call(s32[8]{0:T(128)} %get-tuple-element.43.pick.refs_0_, bf16[192,4096]{1,0:T(8,128)(2,1)} %hid.1, bf16[4096,2048]{1,0:T(8,128)(2,1)} %all-gather.2.cloned.1.call-done.w), custom_call_target="tpu_custom_call" | custom-call | flops 3221225472 | bytes 18350080 | tf_op jit(solution)/shard_map/query/pallas_call | solution.py:120
  91.6 29.0 %collective-permute-done.9.refs_7_ = bf16[2,2,128,1536]{3,2,1,0:T(8,128)(2,1)S(1)} collective-permute-done((bf16[2,2,128,1536]{3,2,1,0:T(8,128)(2,1)}, bf16[2,2,128,1536]{3,2,1,0:T(8,128)(2,1)S(1)}, u32[]{:S(2)}, u32[]{:S(2)}) %collective-permute-start.9) | collective-permute-done | bytes 1572896 | tf_op jit(solution)/shard_map/ppermute | solution.py:416
  120.7 2.1 %collective-permute-done.11.refs_9_ = bf16[2,2,128,1536]{3,2,1,0:T(8,128)(2,1)} collective-permute-done((bf16[2,2,128,1536]{3,2,1,0:T(8,128)(2,1)}, bf16[2,2,128,1536]{3,2,1,0:T(8,128)(2,1)}, u32[]{:S(2)}, u32[]{:S(2)}) %collective-permute-start.11) | collective-permute-done | bytes 1572896 | tf_op jit(solution)/shard_map/ppermute | solution.py:416
  122.9 9.9 %home.2 = (bf16[192,2048]{1,0:T(8,128)(2,1)}, bf16[192,1536]{1,0:T(8,128)(2,1)}, f32[3,64,128]{2,1,0:T(8,128)}) custom-call(s32[8]{0:T(128)} %get-tuple-element.43.pick.refs_0_, s32[8]{0:T(128)} %get-tuple-element.44.refs_1_, s32[8]{0:T(128)} %get-tuple-element.45.refs_0_.refs_2_.refs_1_, bf16[3,64,2048]{2,1,0:T(8,128)(2,1)} %get-tuple-element.46.refs_3_.refs_5_, ...), custom_call_target="tpu_custom_call" | custom-call | flops 603979776 | bytes 5898240 | tf_op jit(solution)/shard_map/home/pallas_call | solution.py:284
  132.7 2.3 %collective-permute-start.12 = (bf16[2,64,2048]{2,1,0:T(8,128)(2,1)}, bf16[2,64,2048]{2,1,0:T(8,128)(2,1)S(1)}, u32[]{:S(2)}, u32[]{:S(2)}) collective-permute-start(bf16[2,64,2048]{2,1,0:T(8,128)(2,1)} %get-tuple-element.73), channel_id=1, source_target_pairs={{0,32},{32,64},{64,96},{96,0},{1,33},{33,65},{65,97},{97,1},{2,34}... | collective-permute-start | bytes 1572872 | tf_op jit(solution)/shard_map/ppermute | solution.py:416
  135.1 2.0 collective-permute-start.13
  137.1 17.0 %collective-permute-start.14 = (bf16[2,64,2048]{2,1,0:T(8,128)(2,1)S(1)}, bf16[2,64,2048]{2,1,0:T(8,128)(2,1)S(1)}, u32[]{:S(2)}, u32[]{:S(2)}) collective-permute-start(bf16[2,64,2048]{2,1,0:T(8,128)(2,1)S(1)} %copy-done.15), channel_id=1, source_target_pairs={{0,96},{32,0},{64,32},{96,64},{1,97},{33,1},{65,33},{97,65},{2,98}... | collective-permute-start | bytes 1572872 | tf_op jit(solution)/shard_map/ppermute | solution.py:416
  154.0 8.9 %grad.2.refs_0_ = f32[192,4096]{1,0:T(8,128)} custom-call(bf16[192,1536]{1,0:T(8,128)(2,1)} %get-tuple-element.69.gq, bf16[4096,2048]{1,0:T(8,128)(2,1)} %all-gather.2.cloned.1.call-done.w), custom_call_target="tpu_custom_call" | custom-call | flops 2415919104 | bytes 15728640 | tf_op jit(solution)/shard_map/grad/pallas_call | solution.py:402
  163.7 5.5 %home.3 = (bf16[192,2048]{1,0:T(8,128)(2,1)}, bf16[192,512]{1,0:T(8,128)(2,1)}, f32[2,64,128]{2,1,0:T(8,128)}, f32[2,64,128]{2,1,0:T(8,128)}, f32[2,64,128]{2,1,0:T(8,128)}, /*index=5*/f32[2,64,128]{2,1,0:T(8,128)}) custom-call(s32[8]{0:T(128)} %get-tuple-element.43.pick.refs_0_, s32[8]{0:T(128)} %get-tuple-element.44.refs_1_, ...), custom_call_target="tpu_custom_call", output_to_operand_aliasing={{0}: (11, {})} | custom-call | flops 201326592 | bytes 1966080 | tf_op jit(solution)/shard_map/home/pallas_call | solution.py:284
  169.3 5.8 %collective-permute-start.16 = (f32[2,64,128]{2,1,0:T(8,128)}, f32[2,64,128]{2,1,0:T(8,128)S(1)}, u32[]{:S(2)}, u32[]{:S(2)}) collective-permute-start(f32[2,64,128]{2,1,0:T(8,128)} %get-tuple-element.78), channel_id=1, source_target_pairs={{0,64},{32,96},{64,0},{96,32},{1,65},{33,97},{65,1},{97,33},{2,66}... | collective-permute-start | bytes 196616 | tf_op jit(solution)/shard_map/ppermute | solution.py:416
  175.1 6.2 %grad.3 = bf16[192,4096]{1,0:T(8,128)(2,1)} custom-call(bf16[192,512]{1,0:T(8,128)(2,1)} %get-tuple-element.68.gq, bf16[4096,2048]{1,0:T(8,128)(2,1)} %all-gather.2.cloned.1.call-done.w, f32[192,4096]{1,0:T(8,128)} %grad.2.refs_0_), custom_call_target="tpu_custom_call" | custom-call | flops 805306368 | bytes 7340032 | tf_op jit(solution)/shard_map/grad/pallas_call | solution.py:402
  182.4 14.3 %terms.1 = (bf16[6,128,2048]{2,1,0:T(8,128)(2,1)}, bf16[6,128,2048]{2,1,0:T(8,128)(2,1)}) custom-call(s32[8]{0:T(128)} %get-tuple-element.43.pick.refs_0_, s32[8]{0:T(128)} %get-tuple-element.45.refs_0_.refs_2_.refs_1_, s32[8]{0:T(128)} %copy-done.12, s32[8]{0:T(128)} %copy-done.13, s32[8]{0:T(128)} %copy-done.14, ...), custom_call_target="tpu_custom_call" | custom-call | flops 1073741824 | bytes 11534336 | tf_op jit(solution)/shard_map/terms/pallas_call | solution.py:372
  (60 shorter events, 8.8 us)
Async XLA Ops:
  7.2 74.9 %all-gather.2.cloned.1.call-start = ((), (), s32[]{:S(2)}) async-start(), calls=%async_computation | async-start | bytes 17301504 | tf_op jit(solution)/shard_map/all_gather | solution.py:433
  11.4 4.0 %collective-permute-start = (s32[8]{0:T(128)}, s32[8]{0:T(128)S(1)}, u32[]{:S(2)}, u32[]{:S(2)}) collective-permute-start(s32[8]{0:T(128)} %get-tuple-element.45.refs_0_.refs_2_.refs_1_), channel_id=1, source_target_pairs={{0,32},{32,64},{64,96},{96,0},{1,33},{33,65},{65,97},{97,1},{2,34}... | collective-permute-start | bytes 104 | tf_op jit(solution)/shard_map/ppermute | solution.py:416
  15.4 27.4 %copy-start.12 = (s32[8]{0:T(128)}, s32[8]{0:T(128)S(1)}, u32[]{:S(2)}) copy-start(s32[8]{0:T(128)S(1)} %collective-permute-done.refs_1_.refs_2_) | copy-start | bytes 100
  15.4 33.9 %collective-permute-start.3 = (bf16[2,64,2048]{2,1,0:T(8,128)(2,1)}, bf16[2,64,2048]{2,1,0:T(8,128)(2,1)S(1)}, u32[]{:S(2)}, u32[]{:S(2)}) collective-permute-start(bf16[2,64,2048]{2,1,0:T(8,128)(2,1)} %get-tuple-element.52), channel_id=1, source_target_pairs={{0,32},{32,64},{64,96},{96,0},{1,33},{33,65},{65,97},{97,1},{2,34}... | collective-permute-start | bytes 1572872 | tf_op jit(solution)/shard_map/ppermute | solution.py:416
  16.8 32.6 %collective-permute-start.4 = (bf16[2,64,2048]{2,1,0:T(8,128)(2,1)}, bf16[2,64,2048]{2,1,0:T(8,128)(2,1)S(1)}, u32[]{:S(2)}, u32[]{:S(2)}) collective-permute-start(bf16[2,64,2048]{2,1,0:T(8,128)(2,1)} %get-tuple-element.53), channel_id=1, source_target_pairs={{0,64},{32,96},{64,0},{96,32},{1,65},{33,97},{65,1},{97,33},{2,66}... | collective-permute-start | bytes 1572872 | tf_op jit(solution)/shard_map/ppermute | solution.py:416
  18.9 30.4 %collective-permute-start.5 = (bf16[2,64,2048]{2,1,0:T(8,128)(2,1)}, bf16[2,64,2048]{2,1,0:T(8,128)(2,1)S(1)}, u32[]{:S(2)}, u32[]{:S(2)}) collective-permute-start(bf16[2,64,2048]{2,1,0:T(8,128)(2,1)} %get-tuple-element.54), channel_id=1, source_target_pairs={{0,96},{32,0},{64,32},{96,64},{1,97},{33,1},{65,33},{97,65},{2,98}... | collective-permute-start | bytes 1572872 | tf_op jit(solution)/shard_map/ppermute | solution.py:416
  20.1 22.6 %collective-permute-start.1 = (s32[8]{0:T(128)}, s32[8]{0:T(128)S(1)}, u32[]{:S(2)}, u32[]{:S(2)}) collective-permute-start(s32[8]{0:T(128)} %get-tuple-element.45.refs_0_.refs_2_.refs_1_), channel_id=1, source_target_pairs={{0,64},{32,96},{64,0},{96,32},{1,65},{33,97},{65,1},{97,33},{2,66}... | collective-permute-start | bytes 104 | tf_op jit(solution)/shard_map/ppermute | solution.py:416
  20.4 22.4 %collective-permute-start.2 = (s32[8]{0:T(128)}, s32[8]{0:T(128)S(1)}, u32[]{:S(2)}, u32[]{:S(2)}) collective-permute-start(s32[8]{0:T(128)} %get-tuple-element.45.refs_0_.refs_2_.refs_1_), channel_id=1, source_target_pairs={{0,96},{32,0},{64,32},{96,64},{1,97},{33,1},{65,33},{97,65},{2,98}... | collective-permute-start | bytes 104 | tf_op jit(solution)/shard_map/ppermute | solution.py:416
  49.3 7.4 %copy-start.2 = (bf16[2,64,2048]{2,1,0:T(8,128)(2,1)}, bf16[2,64,2048]{2,1,0:T(8,128)(2,1)S(1)}, u32[]{:S(2)}) copy-start(bf16[2,64,2048]{2,1,0:T(8,128)(2,1)S(1)} %collective-permute-done.3.refs_10_) | copy-start | bytes 1572868
  49.3 7.4 %copy-start.3 = (bf16[2,64,2048]{2,1,0:T(8,128)(2,1)}, bf16[2,64,2048]{2,1,0:T(8,128)(2,1)S(1)}, u32[]{:S(2)}) copy-start(bf16[2,64,2048]{2,1,0:T(8,128)(2,1)S(1)} %collective-permute-done.4.refs_11_) | copy-start | bytes 1572868
  49.3 7.4 %copy-start.4 = (bf16[2,64,2048]{2,1,0:T(8,128)(2,1)}, bf16[2,64,2048]{2,1,0:T(8,128)(2,1)S(1)}, u32[]{:S(2)}) copy-start(bf16[2,64,2048]{2,1,0:T(8,128)(2,1)S(1)} %collective-permute-done.5.refs_12_) | copy-start | bytes 1572868
  49.4 71.3 %collective-permute-start.9 = (bf16[2,2,128,1536]{3,2,1,0:T(8,128)(2,1)}, bf16[2,2,128,1536]{3,2,1,0:T(8,128)(2,1)S(1)}, u32[]{:S(2)}, u32[]{:S(2)}) collective-permute-start(bf16[2,2,128,1536]{3,2,1,0:T(8,128)(2,1)} %get-tuple-element.62), channel_id=1, source_target_pairs={{0,96},{32,0},{64,32},{96,64},{1,97},{33,1},{65,33},{97,65},{2,98}... | collective-permute-start | bytes 4718600 | tf_op jit(solution)/shard_map/ppermute | solution.py:416
  49.4 71.2 %collective-permute-start.10 = (bf16[2,2,128,1536]{3,2,1,0:T(8,128)(2,1)}, bf16[2,2,128,1536]{3,2,1,0:T(8,128)(2,1)S(1)}, u32[]{:S(2)}, u32[]{:S(2)}) collective-permute-start(bf16[2,2,128,1536]{3,2,1,0:T(8,128)(2,1)} %get-tuple-element.63), channel_id=1, source_target_pairs={{0,64},{32,96},{64,0},{96,32},{1,65},{33,97},{65,1},{97,33},{2,66}... | collective-permute-start | bytes 4718600 | tf_op jit(solution)/shard_map/ppermute | solution.py:416
  51.0 71.8 %collective-permute-start.11 = (bf16[2,2,128,1536]{3,2,1,0:T(8,128)(2,1)}, bf16[2,2,128,1536]{3,2,1,0:T(8,128)(2,1)}, u32[]{:S(2)}, u32[]{:S(2)}) collective-permute-start(bf16[2,2,128,1536]{3,2,1,0:T(8,128)(2,1)} %get-tuple-element.64), channel_id=1, source_target_pairs={{0,32},{32,64},{64,96},{96,0},{1,33},{33,65},{65,97},{97,1},{2,34}... | collective-permute-start | bytes 4718600 | tf_op jit(solution)/shard_map/ppermute | solution.py:416
  56.7 80.3 %collective-permute-start.6 = (bf16[2,2,128,512]{3,2,1,0:T(8,128)(2,1)}, bf16[2,2,128,512]{3,2,1,0:T(8,128)(2,1)}, u32[]{:S(2)}, u32[]{:S(2)}) collective-permute-start(bf16[2,2,128,512]{3,2,1,0:T(8,128)(2,1)} %get-tuple-element.55), channel_id=1, source_target_pairs={{0,96},{32,0},{64,32},{96,64},{1,97},{33,1},{65,33},{97,65},{2,98}... | collective-permute-start | bytes 1572872 | tf_op jit(solution)/shard_map/ppermute | solution.py:416
  56.8 106.1 %collective-permute-start.7 = (bf16[2,2,128,512]{3,2,1,0:T(8,128)(2,1)}, bf16[2,2,128,512]{3,2,1,0:T(8,128)(2,1)}, u32[]{:S(2)}, u32[]{:S(2)}) collective-permute-start(bf16[2,2,128,512]{3,2,1,0:T(8,128)(2,1)} %get-tuple-element.56), channel_id=1, source_target_pairs={{0,64},{32,96},{64,0},{96,32},{1,65},{33,97},{65,1},{97,33},{2,66}... | collective-permute-start | bytes 1572872 | tf_op jit(solution)/shard_map/ppermute | solution.py:416
  120.7 42.2 %collective-permute-start.8 = (bf16[2,2,128,512]{3,2,1,0:T(8,128)(2,1)}, bf16[2,2,128,512]{3,2,1,0:T(8,128)(2,1)S(1)}, u32[]{:S(2)}, u32[]{:S(2)}) collective-permute-start(bf16[2,2,128,512]{3,2,1,0:T(8,128)(2,1)} %get-tuple-element.58), channel_id=1, source_target_pairs={{0,32},{32,64},{64,96},{96,0},{1,33},{33,65},{65,97},{97,1},{2,34}... | collective-permute-start | bytes 1572872 | tf_op jit(solution)/shard_map/ppermute | solution.py:416
  122.8 14.2 %copy-start.15 = (bf16[2,64,2048]{2,1,0:T(8,128)(2,1)S(1)}, bf16[2,64,2048]{2,1,0:T(8,128)(2,1)}, u32[]{:S(2)}) copy-start(bf16[2,64,2048]{2,1,0:T(8,128)(2,1)} %get-tuple-element.75) | copy-start | bytes 1572868
  132.7 42.4 %collective-permute-start.12 = (bf16[2,64,2048]{2,1,0:T(8,128)(2,1)}, bf16[2,64,2048]{2,1,0:T(8,128)(2,1)S(1)}, u32[]{:S(2)}, u32[]{:S(2)}) collective-permute-start(bf16[2,64,2048]{2,1,0:T(8,128)(2,1)} %get-tuple-element.73), channel_id=1, source_target_pairs={{0,32},{32,64},{64,96},{96,0},{1,33},{33,65},{65,97},{97,1},{2,34}... | collective-permute-start | bytes 1572872 | tf_op jit(solution)/shard_map/ppermute | solution.py:416
  135.1 46.2 %collective-permute-start.13 = (bf16[2,64,2048]{2,1,0:T(8,128)(2,1)}, bf16[2,64,2048]{2,1,0:T(8,128)(2,1)S(1)}, u32[]{:S(2)}, u32[]{:S(2)}) collective-permute-start(bf16[2,64,2048]{2,1,0:T(8,128)(2,1)} %get-tuple-element.74), channel_id=1, source_target_pairs={{0,64},{32,96},{64,0},{96,32},{1,65},{33,97},{65,1},{97,33},{2,66}... | collective-permute-start | bytes 1572872 | tf_op jit(solution)/shard_map/ppermute | solution.py:416
  137.1 44.3 %collective-permute-start.14 = (bf16[2,64,2048]{2,1,0:T(8,128)(2,1)S(1)}, bf16[2,64,2048]{2,1,0:T(8,128)(2,1)S(1)}, u32[]{:S(2)}, u32[]{:S(2)}) collective-permute-start(bf16[2,64,2048]{2,1,0:T(8,128)(2,1)S(1)} %copy-done.15), channel_id=1, source_target_pairs={{0,96},{32,0},{64,32},{96,64},{1,97},{33,1},{65,33},{97,65},{2,98}... | collective-permute-start | bytes 1572872 | tf_op jit(solution)/shard_map/ppermute | solution.py:416
  169.3 12.1 %collective-permute-start.15 = (f32[2,64,128]{2,1,0:T(8,128)}, f32[2,64,128]{2,1,0:T(8,128)S(1)}, u32[]{:S(2)}, u32[]{:S(2)}) collective-permute-start(f32[2,64,128]{2,1,0:T(8,128)} %get-tuple-element.77), channel_id=1, source_target_pairs={{0,32},{32,64},{64,96},{96,0},{1,33},{33,65},{65,97},{97,1},{2,34}... | collective-permute-start | bytes 196616 | tf_op jit(solution)/shard_map/ppermute | solution.py:416
  169.3 12.0 %collective-permute-start.16 = (f32[2,64,128]{2,1,0:T(8,128)}, f32[2,64,128]{2,1,0:T(8,128)S(1)}, u32[]{:S(2)}, u32[]{:S(2)}) collective-permute-start(f32[2,64,128]{2,1,0:T(8,128)} %get-tuple-element.78), channel_id=1, source_target_pairs={{0,64},{32,96},{64,0},{96,32},{1,65},{33,97},{65,1},{97,33},{2,66}... | collective-permute-start | bytes 196616 | tf_op jit(solution)/shard_map/ppermute | solution.py:416
  175.1 6.3 %collective-permute-start.17 = (f32[2,64,128]{2,1,0:T(8,128)}, f32[2,64,128]{2,1,0:T(8,128)S(1)}, u32[]{:S(2)}, u32[]{:S(2)}) collective-permute-start(f32[2,64,128]{2,1,0:T(8,128)} %get-tuple-element.79), channel_id=1, source_target_pairs={{0,96},{32,0},{64,32},{96,64},{1,97},{33,1},{65,33},{97,65},{2,98}... | collective-permute-start | bytes 196616 | tf_op jit(solution)/shard_map/ppermute | solution.py:416
  (11 other events, 17.2 us)
Sparse Core Ops, SparseCore 0:
  10.3 71.7 all-gather.1

commit v5 on v4

--- a/solution.py
+++ b/solution.py
@@ -186,13 +186,13 @@
 
 
 def home_kernel(col, cw, first, last, *refs):
-    pick, place, want, q, c, keys, values = refs[:7]
-    pairs, refs = refs[7:10], refs[10:]
+    pick, place, want, me, q, c, keys, values = refs[:8]
+    pairs, refs = refs[8:11], refs[11:]
     if not first:
         before, refs = refs[0], refs[2:]
     att, gq, refs = refs[0], refs[1], refs[2:]
     if last:
-        backs, refs = refs[:4], refs[4:]
+        backs, refs = refs[0], refs[1:]
     qb, cb, kb, vb, res, sems, gsems = refs
     cols = pl.ds(col, cw)
     for g in range(GROUPS):
@@ -253,12 +253,12 @@
     if last:
         for d in range(4):
             for s in range(2):
-                backs[d][s] = res[pick[2 * d + s]]
-
-
-def home(pick, place, want, q, c, keys, values, pairs, before, last, col, cw):
+                backs[(me[0] + d) % 4, s] = res[pick[2 * d + s]]
+
+
+def home(pick, place, want, me, q, c, keys, values, pairs, before, last, col, cw):
     tokens = GROUPS * ROWS
-    small = shape((2, ROWS, HEAD), F32)
+    small = shape((4, 2, ROWS, HEAD), F32)
     every = shape((GROUPS, ROWS, HEAD), F32)
     first = before is None
     extra = [] if first else [whole(GROUPS, ROWS, HEAD), ANY]
@@ -266,8 +266,8 @@
     out_specs = (pl.BlockSpec((tokens, cw), lambda i: (0, col // cw)), whole(tokens, cw))
     keep = [pltpu.VMEM((GROUPS, ROWS, HEAD), F32)]
     if last:
-        out_shape += (small,) * 4
-        out_specs += (whole(2, ROWS, HEAD),) * 4
+        out_shape += (small,)
+        out_specs += (whole(4, 2, ROWS, HEAD),)
     else:
         out_shape += (every,)
         out_specs += (whole(GROUPS, ROWS, HEAD),)
@@ -277,7 +277,7 @@
         inner = body
 
         def body(*refs):
-            n = 10 + len(extra)
+            n = 11 + len(extra)
             ins, att, gq, res, rest = refs[:n], refs[n], refs[n + 1], refs[n + 2], refs[n + 3 :]
             inner(*ins, att, gq, *rest[:4], res, *rest[4:])
 
@@ -285,7 +285,7 @@
         body,
         out_shape=out_shape,
         grid=(1,),
-        in_specs=[SMEM] * 3 + [ANY] * 7 + extra,
+        in_specs=[SMEM] * 4 + [ANY] * 7 + extra,
         out_specs=out_specs,
         scratch_shapes=[
             pltpu.VMEM((GROUPS, ROWS, cw), BF16),
@@ -296,17 +296,17 @@
             pltpu.SemaphoreType.DMA((2 * GROUPS, 2)),
             pltpu.SemaphoreType.DMA((GROUPS, 2)),
         ],
-        input_output_aliases={} if first else {11: 0},
+        input_output_aliases={} if first else {12: 0},
         compiler_params=params(BIG),
         cost_estimate=cost(6 * 8 * ROWS * LEN * cw, 30 * LEN * cw, 6 * ROWS * cw),
         name="home",
-    )(pick, place, want, q, c, keys, values, *pairs, *(() if first else before))
+    )(pick, place, want, me, q, c, keys, values, *pairs, *(() if first else before))
 
 
 def terms_kernel(tw, *refs):
-    pick, asked, refs = refs[0], refs[1:5], refs[5:]
-    q, c, keys, values, back = refs[:4], refs[4:8], refs[8], refs[9], refs[10:14]
-    dk, dv, rows, seen, qb, cb, bb = refs[14:]
+    me, pick, asked, refs = refs[0], refs[1], refs[2:6], refs[6:]
+    q, c, keys, values, back = refs[:4], refs[4:8], refs[8], refs[9], refs[10]
+    dk, dv, rows, seen, qb, cb, bb = refs[11:]
     fill_rows(asked, rows)
     for b in range(STORED):
         seen[b] = 0
@@ -316,7 +316,7 @@
         at = pick[k] if d == 0 else s
         qb[k] = q[d][at]
         cb[k] = c[d][at]
-        bb[k] = jnp.transpose(pltpu.roll(back[d][s], (HEAD - base) % HEAD, 1))
+        bb[k] = jnp.transpose(pltpu.roll(back[(me[0] + 4 - d) % 4, s], (HEAD - base) % HEAD, 1))
 
     def one_slot(k, row, add):
         for first in range(0, tw // HEAD, GANG):
@@ -362,7 +362,7 @@
             dv[b] = jnp.zeros((LEN, tw), BF16)
 
 
-def terms(pick, asked, q, c, keys, values, back):
+def terms(me, pick, asked, q, c, keys, values, back):
     full = shape((STORED, LEN, WIDTH), BF16)
     tw = TWIDTH
 
@@ -373,7 +373,7 @@
         functools.partial(terms_kernel, tw),
         out_shape=(full,) * 2,
         grid=(WIDTH // tw,),
-        in_specs=[SMEM] * 5 + [part(x) for x in (*q, *c, keys, values)] + [whole(2, ROWS, HEAD)] * 4,
+        in_specs=[SMEM] * 6 + [part(x) for x in (*q, *c, keys, values)] + [whole(4, 2, ROWS, HEAD)],
         out_specs=(part(keys),) * 2,
         scratch_shapes=[
             pltpu.SMEM((SLOTS,), jnp.int32),
@@ -385,7 +385,7 @@
         compiler_params=params(BIG),
         cost_estimate=cost(SLOTS * 8 * ROWS * LEN * WIDTH, 44 * LEN * WIDTH, SLOTS * ROWS * WIDTH),
         name="terms",
-    )(pick, *asked, *q, *c, keys, values, *back)
+    )(me, pick, *asked, *q, *c, keys, values, back)
 
 
 def grad_kernel(gq, w, *refs):
@@ -441,13 +441,14 @@
     before, grad_hidden = None, None
     for (col, cw), pair in zip(PARTS, pairs):
         last = col + cw == WIDTH
-        attended, gq, *back = home(pick, place, want, q, cot, keys, values, pair, before, last, col, cw)
+        attended, gq, *back = home(pick, place, want, me, q, cot, keys, values, pair, before, last, col, cw)
+        partial = grad_hidden
+        grad_hidden = grad(gq, weights, partial, last, col, cw)
         if before is None:
-            qs = [q] + to_owner(after(sends, gq))
-        before = (back[0], attended)
-        grad_hidden = grad(gq, weights, grad_hidden, last, col, cw)
-    back = [back[0]] + to_owner(back[1:])
-    grad_keys, grad_values = terms(pick, asked, qs, c, keys, values, back)
+            qs = [q] + to_owner(after(sends, pairs[1], grad_hidden))
+            before = after((back[0], attended), grad_hidden)
+    back = lax.all_to_all(back[0], "enc", split_axis=0, concat_axis=0, tiled=True)
+    grad_keys, grad_values = terms(me, pick, asked, qs, c, keys, values, back)
     return attended, grad_hidden, grad_keys, grad_values
 
 

time: 205 us -> 200 us (0.976)
  the two profiles are of different devices: /device:TPU:106 before, /device:TPU:100 now
where the time goes in v5:
time: 200 us; the launch traced here: 199 us
  waiting for transfers between devices  87 us (44%)
  Pallas kernels  66.9 us (33%)
  starting transfers between devices  26 us (13%)
  between operations  14.3 us (7%)
  local copies, waits for them, and re-layouts  4.55 us (2%)
    ppermute x15, waiting for transfers between devices, shift(): return lax.ppermute(x, 'enc', [(i, (i + d) % 4) for i in range(4)])  60.1 us
    ppermute x15, starting transfers between devices, shift(): return lax.ppermute(x, 'enc', [(i, (i + d) % 4) for i in range(4)])  21.9 us
    all_gather x1, waiting for transfers between devices, per_device(): weights = lax.all_gather(query_weight, 'fsdp', axis=0, tiled=True)  21.3 us
    pallas_call x2, Pallas kernels, home(): pl.pallas_call(body, out_shape=out_shape, grid=(1,), in_specs=[SMEM] * 4...  15.4 us
    pallas_call x2, Pallas kernels, grad(): pl.pallas_call(grad_kernel, out_shape=shape((GROUPS * ROWS, depth), BF16...  15 us
    pallas_call x1, Pallas kernels, terms(): pl.pallas_call(functools.partial(terms_kernel, tw), out_shape=(full,) * 2...  14.4 us
    pallas_call x1, Pallas kernels, query(): pl.pallas_call(query_kernel, out_shape=(shape((GROUPS, ROWS, WIDTH), BF16...  9.68 us
    pallas_call x2, Pallas kernels, collect(): pl.pallas_call(functools.partial(collect_kernel, col, cw), out_shape=(one...  8.83 us
  transfers between devices with their start and end apart: 17, of which 6 were waited for; matrix products, arithmetic and copies ran while one was open for 1% of the time, Pallas kernels for 26%

profile of v5, /device:TPU:100, one launch (start us, length us, event | category | flops | bytes accessed | tf_op | source)
XLA Modules:
  0.0 199.4 jit_solution(13625302127063028151)
XLA Ops:
  10.1 1.3 route.1
  11.4 1.6 collective-permute-start
  13.0 2.4 %spread.1 = (bf16[2,64,2048]{2,1,0:T(8,128)(2,1)}, bf16[2,64,2048]{2,1,0:T(8,128)(2,1)}, bf16[2,64,2048]{2,1,0:T(8,128)(2,1)}) custom-call(s32[8]{0:T(128)} %get-tuple-element.42.pick.refs_0_.refs_1_, bf16[3,64,2048]{2,1,0:T(8,128)(2,1)} %bitcast.2), custom_call_target="tpu_custom_call" | custom-call | flops 1 | bytes 2621440 | tf_op jit(solution)/shard_map/spread/pallas_call | solution.py:95
  17.0 2.7 %collective-permute-start.4 = (bf16[2,64,2048]{2,1,0:T(8,128)(2,1)}, bf16[2,64,2048]{2,1,0:T(8,128)(2,1)S(1)}, u32[]{:S(2)}, u32[]{:S(2)}) collective-permute-start(bf16[2,64,2048]{2,1,0:T(8,128)(2,1)} %get-tuple-element.52), channel_id=1, source_target_pairs={{0,64},{32,96},{64,0},{96,32},{1,65},{33,97},{65,1},{97,33},{2,66}... | collective-permute-start | bytes 1572872 | tf_op jit(solution)/shard_map/ppermute | solution.py:416
  19.7 1.3 collective-permute-start.5
  21.1 2.7 %collective-permute-start.1 = (s32[8]{0:T(128)}, s32[8]{0:T(128)S(1)}, u32[]{:S(2)}, u32[]{:S(2)}) collective-permute-start(s32[8]{0:T(128)} %get-tuple-element.44.refs_0_.refs_2_), channel_id=1, source_target_pairs={{0,64},{32,96},{64,0},{96,32},{1,65},{33,97},{65,1},{97,33},{2,66}... | collective-permute-start | bytes 104 | tf_op jit(solution)/shard_map/ppermute | solution.py:416
  23.8 18.4 %collective-permute-done.2.refs_3_.refs_5_ = s32[8]{0:T(128)S(1)} collective-permute-done((s32[8]{0:T(128)}, s32[8]{0:T(128)S(1)}, u32[]{:S(2)}, u32[]{:S(2)}) %collective-permute-start.2) | collective-permute-done | bytes 64 | tf_op jit(solution)/shard_map/ppermute | solution.py:416
  43.3 5.8 %collect.3 = (bf16[2,2,128,1536]{3,2,1,0:T(8,128)(2,1)}, bf16[2,2,128,1536]{3,2,1,0:T(8,128)(2,1)}, bf16[2,2,128,1536]{3,2,1,0:T(8,128)(2,1)}) custom-call(s32[8]{0:T(128)} %get-tuple-element.44.refs_0_.refs_2_, s32[8]{0:T(128)} %copy-done.10, s32[8]{0:T(128)} %copy-done.12, s32[8]{0:T(128)} %copy-done.11, bf16[6,128,2048]{2,1,0:T(8,128)(2,1)} %refs_14_.1, ...), custom_call_target="tpu_custom_call" | custom-call | flops 1 | bytes 9437184 | tf_op jit(solution)/shard_map/collect/pallas_call | solution.py:172
  49.2 2.7 %collective-permute-start.9 = (bf16[2,2,128,1536]{3,2,1,0:T(8,128)(2,1)}, bf16[2,2,128,1536]{3,2,1,0:T(8,128)(2,1)S(1)}, u32[]{:S(2)}, u32[]{:S(2)}) collective-permute-start(bf16[2,2,128,1536]{3,2,1,0:T(8,128)(2,1)} %get-tuple-element.61), channel_id=1, source_target_pairs={{0,96},{32,0},{64,32},{96,64},{1,97},{33,1},{65,33},{97,65},{2,98}... | collective-permute-start | bytes 4718600 | tf_op jit(solution)/shard_map/ppermute | solution.py:416
  51.8 1.2 collective-permute-start.10
  53.5 3.0 %collect.2 = (bf16[2,2,128,512]{3,2,1,0:T(8,128)(2,1)}, bf16[2,2,128,512]{3,2,1,0:T(8,128)(2,1)}, bf16[2,2,128,512]{3,2,1,0:T(8,128)(2,1)}) custom-call(s32[8]{0:T(128)} %get-tuple-element.44.refs_0_.refs_2_, s32[8]{0:T(128)} %copy-done.10, s32[8]{0:T(128)} %copy-done.12, s32[8]{0:T(128)} %copy-done.11, bf16[6,128,2048]{2,1,0:T(8,128)(2,1)} %refs_14_.1, ...), custom_call_target="tpu_custom_call" | custom-call | flops 1 | bytes 3145728 | tf_op jit(solution)/shard_map/collect/pallas_call | solution.py:172
  56.5 3.1 %collective-permute-start.6 = (bf16[2,2,128,512]{3,2,1,0:T(8,128)(2,1)}, bf16[2,2,128,512]{3,2,1,0:T(8,128)(2,1)}, u32[]{:S(2)}, u32[]{:S(2)}) collective-permute-start(bf16[2,2,128,512]{3,2,1,0:T(8,128)(2,1)} %get-tuple-element.54), channel_id=1, source_target_pairs={{0,96},{32,0},{64,32},{96,64},{1,97},{33,1},{65,33},{97,65},{2,98}... | collective-permute-start | bytes 1572872 | tf_op jit(solution)/shard_map/ppermute | solution.py:416
  60.6 21.3 %all-gather.2.cloned.1.call-done.w = bf16[4096,2048]{1,0:T(8,128)(2,1)} async-done(((bf16[128,2048]{1,0:T(8,128)(2,1)}), bf16[4096,2048]{1,0:T(8,128)(2,1)}) %all-gather.2.cloned.1.call-update) | async-done | bytes 16777232 | tf_op jit(solution)/shard_map/all_gather | solution.py:433
  82.0 9.7 %query.1 = (bf16[3,64,2048]{2,1,0:T(8,128)(2,1)}, bf16[2,64,2048]{2,1,0:T(8,128)(2,1)}, bf16[2,64,2048]{2,1,0:T(8,128)(2,1)}, bf16[2,64,2048]{2,1,0:T(8,128)(2,1)}) custom-call(s32[8]{0:T(128)} %get-tuple-element.42.pick.refs_0_.refs_1_, bf16[192,4096]{1,0:T(8,128)(2,1)} %hid.1, bf16[4096,2048]{1,0:T(8,128)(2,1)} %all-gather.2.cloned.1.call-done.w), custom_call_target="tpu_custom_call" | custom-call | flops 3221225472 | bytes 18350080 | tf_op jit(solution)/shard_map/query/pallas_call | solution.py:120
  91.6 28.9 %collective-permute-done.9.refs_8_ = bf16[2,2,128,1536]{3,2,1,0:T(8,128)(2,1)S(1)} collective-permute-done((bf16[2,2,128,1536]{3,2,1,0:T(8,128)(2,1)}, bf16[2,2,128,1536]{3,2,1,0:T(8,128)(2,1)S(1)}, u32[]{:S(2)}, u32[]{:S(2)}) %collective-permute-start.9) | collective-permute-done | bytes 1572896 | tf_op jit(solution)/shard_map/ppermute | solution.py:416
  121.6 11.7 %collective-permute-done.11.refs_10_ = bf16[2,2,128,1536]{3,2,1,0:T(8,128)(2,1)} collective-permute-done((bf16[2,2,128,1536]{3,2,1,0:T(8,128)(2,1)}, bf16[2,2,128,1536]{3,2,1,0:T(8,128)(2,1)}, u32[]{:S(2)}, u32[]{:S(2)}) %collective-permute-start.11) | collective-permute-done | bytes 1572896 | tf_op jit(solution)/shard_map/ppermute | solution.py:416
  133.4 9.7 %home.2 = (bf16[192,2048]{1,0:T(8,128)(2,1)}, bf16[192,1536]{1,0:T(8,128)(2,1)}, f32[3,64,128]{2,1,0:T(8,128)}) custom-call(s32[8]{0:T(128)} %get-tuple-element.42.pick.refs_0_.refs_1_, s32[8]{0:T(128)} %get-tuple-element.43.refs_1_, s32[8]{0:T(128)} %get-tuple-element.44.refs_0_.refs_2_, s32[1]{0:T(128)} %bitcast.me.refs_3_.refs_0_, ...), custom_call_target="tpu_custom_call" | custom-call | flops 603979776 | bytes 5898240 | tf_op jit(solution)/shard_map/home/pallas_call | solution.py:284
  143.2 9.0 %grad.2.refs_0_ = f32[192,4096]{1,0:T(8,128)} custom-call(bf16[192,1536]{1,0:T(8,128)(2,1)} %get-tuple-element.66.gq, bf16[4096,2048]{1,0:T(8,128)(2,1)} %all-gather.2.cloned.1.call-done.w), custom_call_target="tpu_custom_call" | custom-call | flops 2415919104 | bytes 15728640 | tf_op jit(solution)/shard_map/grad/pallas_call | solution.py:402
  152.4 3.2 %collective-permute-start.14 = (bf16[2,64,2048]{2,1,0:T(8,128)(2,1)S(1)}, bf16[2,64,2048]{2,1,0:T(8,128)(2,1)S(1)}, u32[]{:S(2)}, u32[]{:S(2)}) collective-permute-start(bf16[2,64,2048]{2,1,0:T(8,128)(2,1)S(1)} %copy-done.13), channel_id=1, source_target_pairs={{0,96},{32,0},{64,32},{96,64},{1,97},{33,1},{65,33},{97,65},{2,98}... | collective-permute-start | bytes 1572872 | tf_op jit(solution)/shard_map/ppermute | solution.py:416
  155.6 5.6 %home.3 = (bf16[192,2048]{1,0:T(8,128)(2,1)}, bf16[192,512]{1,0:T(8,128)(2,1)}, f32[4,2,64,128]{3,2,1,0:T(8,128)}) custom-call(s32[8]{0:T(128)} %get-tuple-element.42.pick.refs_0_.refs_1_, s32[8]{0:T(128)} %get-tuple-element.43.refs_1_, s32[8]{0:T(128)} %get-tuple-element.44.refs_0_.refs_2_, ...), custom_call_target="tpu_custom_call", output_to_operand_aliasing={{0}: (12, {})} | custom-call | flops 201326592 | bytes 1966080 | tf_op jit(solution)/shard_map/home/pallas_call | solution.py:284
  161.2 4.1 %all-to-all-start = ((f32[4,2,64,128]{3,2,1,0:T(8,128)}), f32[4,2,64,128]{3,2,1,0:T(8,128)S(1)}, u32[]{:S(2)}, u32[]{:S(2)}) async-start(f32[4,2,64,128]{3,2,1,0:T(8,128)} %get-tuple-element.77), calls=%async_computation | async-start | bytes 524288 | tf_op jit(solution)/shard_map/all_to_all | solution.py:450
  165.3 6.0 %grad.3 = bf16[192,4096]{1,0:T(8,128)(2,1)} custom-call(bf16[192,512]{1,0:T(8,128)(2,1)} %get-tuple-element.70.gq, bf16[4096,2048]{1,0:T(8,128)(2,1)} %all-gather.2.cloned.1.call-done.w, f32[192,4096]{1,0:T(8,128)} %grad.2.refs_0_), custom_call_target="tpu_custom_call" | custom-call | flops 805306368 | bytes 7340032 | tf_op jit(solution)/shard_map/grad/pallas_call | solution.py:402
  171.3 5.0 %all-to-all-done.refs_16_ = f32[4,2,64,128]{3,2,1,0:T(8,128)S(1)} async-done(((f32[4,2,64,128]{3,2,1,0:T(8,128)}), f32[4,2,64,128]{3,2,1,0:T(8,128)S(1)}, u32[]{:S(2)}, u32[]{:S(2)}) %all-to-all-start) | async-done | bytes 262176 | tf_op jit(solution)/shard_map/all_to_all | solution.py:450
  178.2 14.4 %terms.1 = (bf16[6,128,2048]{2,1,0:T(8,128)(2,1)}, bf16[6,128,2048]{2,1,0:T(8,128)(2,1)}) custom-call(s32[1]{0:T(128)} %bitcast.me.refs_3_.refs_0_, s32[8]{0:T(128)} %get-tuple-element.42.pick.refs_0_.refs_1_, s32[8]{0:T(128)} %get-tuple-element.44.refs_0_.refs_2_, s32[8]{0:T(128)} %copy-done.10, s32[8]{0:T(128)} %copy-done.12, s32[8]{0:T(128)} %copy-done.11, ...), custom_call_target="tpu_custom_call" | custom-call | flops 1073741824 | bytes 11534336 | tf_op jit(solution)/shard_map/terms/pallas_call | solution.py:372
  (58 shorter events, 10.4 us)
Async XLA Ops:
  7.2 74.8 %all-gather.2.cloned.1.call-start = ((), (), s32[]{:S(2)}) async-start(), calls=%async_computation.1 | async-start | bytes 17301504 | tf_op jit(solution)/shard_map/all_gather | solution.py:433
  11.4 5.0 %collective-permute-start = (s32[8]{0:T(128)}, s32[8]{0:T(128)S(1)}, u32[]{:S(2)}, u32[]{:S(2)}) collective-permute-start(s32[8]{0:T(128)} %get-tuple-element.44.refs_0_.refs_2_), channel_id=1, source_target_pairs={{0,32},{32,64},{64,96},{96,0},{1,33},{33,65},{65,97},{97,1},{2,34}... | collective-permute-start | bytes 104 | tf_op jit(solution)/shard_map/ppermute | solution.py:416
  16.4 25.8 %copy-start.10 = (s32[8]{0:T(128)}, s32[8]{0:T(128)S(1)}, u32[]{:S(2)}) copy-start(s32[8]{0:T(128)S(1)} %collective-permute-done.refs_1_.refs_3_) | copy-start | bytes 100
  16.4 32.7 %collective-permute-start.3 = (bf16[2,64,2048]{2,1,0:T(8,128)(2,1)}, bf16[2,64,2048]{2,1,0:T(8,128)(2,1)S(1)}, u32[]{:S(2)}, u32[]{:S(2)}) collective-permute-start(bf16[2,64,2048]{2,1,0:T(8,128)(2,1)} %get-tuple-element.51), channel_id=1, source_target_pairs={{0,32},{32,64},{64,96},{96,0},{1,33},{33,65},{65,97},{97,1},{2,34}... | collective-permute-start | bytes 1572872 | tf_op jit(solution)/shard_map/ppermute | solution.py:416
  17.0 32.2 %collective-permute-start.4 = (bf16[2,64,2048]{2,1,0:T(8,128)(2,1)}, bf16[2,64,2048]{2,1,0:T(8,128)(2,1)S(1)}, u32[]{:S(2)}, u32[]{:S(2)}) collective-permute-start(bf16[2,64,2048]{2,1,0:T(8,128)(2,1)} %get-tuple-element.52), channel_id=1, source_target_pairs={{0,64},{32,96},{64,0},{96,32},{1,65},{33,97},{65,1},{97,33},{2,66}... | collective-permute-start | bytes 1572872 | tf_op jit(solution)/shard_map/ppermute | solution.py:416
  19.7 29.5 %collective-permute-start.5 = (bf16[2,64,2048]{2,1,0:T(8,128)(2,1)}, bf16[2,64,2048]{2,1,0:T(8,128)(2,1)S(1)}, u32[]{:S(2)}, u32[]{:S(2)}) collective-permute-start(bf16[2,64,2048]{2,1,0:T(8,128)(2,1)} %get-tuple-element.53), channel_id=1, source_target_pairs={{0,96},{32,0},{64,32},{96,64},{1,97},{33,1},{65,33},{97,65},{2,98}... | collective-permute-start | bytes 1572872 | tf_op jit(solution)/shard_map/ppermute | solution.py:416
  21.0 21.2 %collective-permute-start.2 = (s32[8]{0:T(128)}, s32[8]{0:T(128)S(1)}, u32[]{:S(2)}, u32[]{:S(2)}) collective-permute-start(s32[8]{0:T(128)} %get-tuple-element.44.refs_0_.refs_2_), channel_id=1, source_target_pairs={{0,96},{32,0},{64,32},{96,64},{1,97},{33,1},{65,33},{97,65},{2,98}... | collective-permute-start | bytes 104 | tf_op jit(solution)/shard_map/ppermute | solution.py:416
  21.1 21.1 %collective-permute-start.1 = (s32[8]{0:T(128)}, s32[8]{0:T(128)S(1)}, u32[]{:S(2)}, u32[]{:S(2)}) collective-permute-start(s32[8]{0:T(128)} %get-tuple-element.44.refs_0_.refs_2_), channel_id=1, source_target_pairs={{0,64},{32,96},{64,0},{96,32},{1,65},{33,97},{65,1},{97,33},{2,66}... | collective-permute-start | bytes 104 | tf_op jit(solution)/shard_map/ppermute | solution.py:416
  49.2 71.3 %collective-permute-start.9 = (bf16[2,2,128,1536]{3,2,1,0:T(8,128)(2,1)}, bf16[2,2,128,1536]{3,2,1,0:T(8,128)(2,1)S(1)}, u32[]{:S(2)}, u32[]{:S(2)}) collective-permute-start(bf16[2,2,128,1536]{3,2,1,0:T(8,128)(2,1)} %get-tuple-element.61), channel_id=1, source_target_pairs={{0,96},{32,0},{64,32},{96,64},{1,97},{33,1},{65,33},{97,65},{2,98}... | collective-permute-start | bytes 4718600 | tf_op jit(solution)/shard_map/ppermute | solution.py:416
  51.8 69.8 %collective-permute-start.10 = (bf16[2,2,128,1536]{3,2,1,0:T(8,128)(2,1)}, bf16[2,2,128,1536]{3,2,1,0:T(8,128)(2,1)S(1)}, u32[]{:S(2)}, u32[]{:S(2)}) collective-permute-start(bf16[2,2,128,1536]{3,2,1,0:T(8,128)(2,1)} %get-tuple-element.62), channel_id=1, source_target_pairs={{0,64},{32,96},{64,0},{96,32},{1,65},{33,97},{65,1},{97,33},{2,66}... | collective-permute-start | bytes 4718600 | tf_op jit(solution)/shard_map/ppermute | solution.py:416
  53.0 80.4 %collective-permute-start.11 = (bf16[2,2,128,1536]{3,2,1,0:T(8,128)(2,1)}, bf16[2,2,128,1536]{3,2,1,0:T(8,128)(2,1)}, u32[]{:S(2)}, u32[]{:S(2)}) collective-permute-start(bf16[2,2,128,1536]{3,2,1,0:T(8,128)(2,1)} %get-tuple-element.63), channel_id=1, source_target_pairs={{0,32},{32,64},{64,96},{96,0},{1,33},{33,65},{65,97},{97,1},{2,34}... | collective-permute-start | bytes 4718600 | tf_op jit(solution)/shard_map/ppermute | solution.py:416
  56.5 95.6 %collective-permute-start.6 = (bf16[2,2,128,512]{3,2,1,0:T(8,128)(2,1)}, bf16[2,2,128,512]{3,2,1,0:T(8,128)(2,1)}, u32[]{:S(2)}, u32[]{:S(2)}) collective-permute-start(bf16[2,2,128,512]{3,2,1,0:T(8,128)(2,1)} %get-tuple-element.54), channel_id=1, source_target_pairs={{0,96},{32,0},{64,32},{96,64},{1,97},{33,1},{65,33},{97,65},{2,98}... | collective-permute-start | bytes 1572872 | tf_op jit(solution)/shard_map/ppermute | solution.py:416
  59.6 92.6 %collective-permute-start.7 = (bf16[2,2,128,512]{3,2,1,0:T(8,128)(2,1)}, bf16[2,2,128,512]{3,2,1,0:T(8,128)(2,1)}, u32[]{:S(2)}, u32[]{:S(2)}) collective-permute-start(bf16[2,2,128,512]{3,2,1,0:T(8,128)(2,1)} %get-tuple-element.55), channel_id=1, source_target_pairs={{0,64},{32,96},{64,0},{96,32},{1,65},{33,97},{65,1},{97,33},{2,66}... | collective-permute-start | bytes 1572872 | tf_op jit(solution)/shard_map/ppermute | solution.py:416
  82.0 38.6 %copy-start.16 = (bf16[2,2,128,512]{3,2,1,0:T(8,128)(2,1)S(1)}, bf16[2,2,128,512]{3,2,1,0:T(8,128)(2,1)}, u32[]{:S(2)}) copy-start(bf16[2,2,128,512]{3,2,1,0:T(8,128)(2,1)} %get-tuple-element.57) | copy-start | bytes 1572868
  120.5 12.9 %copy-start = (bf16[2,2,128,1536]{3,2,1,0:T(8,128)(2,1)}, bf16[2,2,128,1536]{3,2,1,0:T(8,128)(2,1)S(1)}, u32[]{:S(2)}) copy-start(bf16[2,2,128,1536]{3,2,1,0:T(8,128)(2,1)S(1)} %collective-permute-done.9.refs_8_) | copy-start | bytes 4718596
  120.5 31.6 %collective-permute-start.8 = (bf16[2,2,128,512]{3,2,1,0:T(8,128)(2,1)S(1)}, bf16[2,2,128,512]{3,2,1,0:T(8,128)(2,1)S(1)}, u32[]{:S(2)}, u32[]{:S(2)}) collective-permute-start(bf16[2,2,128,512]{3,2,1,0:T(8,128)(2,1)S(1)} %copy-done.16), channel_id=1, source_target_pairs={{0,32},{32,64},{64,96},{96,0},{1,33},{33,65},{65,97},{97,1},{2,34}... | collective-permute-start | bytes 1572872 | tf_op jit(solution)/shard_map/ppermute | solution.py:416
  121.6 11.7 %copy-start.1 = (bf16[2,2,128,1536]{3,2,1,0:T(8,128)(2,1)}, bf16[2,2,128,1536]{3,2,1,0:T(8,128)(2,1)S(1)}, u32[]{:S(2)}) copy-start(bf16[2,2,128,1536]{3,2,1,0:T(8,128)(2,1)S(1)} %collective-permute-done.10.refs_9_) | copy-start | bytes 4718596
  143.1 9.0 %copy-start.15 = (bf16[2,64,2048]{2,1,0:T(8,128)(2,1)S(1)}, bf16[2,64,2048]{2,1,0:T(8,128)(2,1)}, u32[]{:S(2)}) copy-start(bf16[2,64,2048]{2,1,0:T(8,128)(2,1)} %get-tuple-element.74) | copy-start | bytes 1572868
  143.1 9.1 %copy-start.14 = (bf16[2,64,2048]{2,1,0:T(8,128)(2,1)S(1)}, bf16[2,64,2048]{2,1,0:T(8,128)(2,1)}, u32[]{:S(2)}) copy-start(bf16[2,64,2048]{2,1,0:T(8,128)(2,1)} %get-tuple-element.75) | copy-start | bytes 1572868
  143.2 9.2 %copy-start.13 = (bf16[2,64,2048]{2,1,0:T(8,128)(2,1)S(1)}, bf16[2,64,2048]{2,1,0:T(8,128)(2,1)}, u32[]{:S(2)}) copy-start(bf16[2,64,2048]{2,1,0:T(8,128)(2,1)} %get-tuple-element.76) | copy-start | bytes 1572868
  152.2 24.1 %collective-permute-start.12 = (bf16[2,64,2048]{2,1,0:T(8,128)(2,1)S(1)}, bf16[2,64,2048]{2,1,0:T(8,128)(2,1)S(1)}, u32[]{:S(2)}, u32[]{:S(2)}) collective-permute-start(bf16[2,64,2048]{2,1,0:T(8,128)(2,1)S(1)} %copy-done.15), channel_id=1, source_target_pairs={{0,32},{32,64},{64,96},{96,0},{1,33},{33,65},{65,97},{97,1},{2,34}... | collective-permute-start | bytes 1572872 | tf_op jit(solution)/shard_map/ppermute | solution.py:416
  152.3 24.0 %collective-permute-start.13 = (bf16[2,64,2048]{2,1,0:T(8,128)(2,1)S(1)}, bf16[2,64,2048]{2,1,0:T(8,128)(2,1)S(1)}, u32[]{:S(2)}, u32[]{:S(2)}) collective-permute-start(bf16[2,64,2048]{2,1,0:T(8,128)(2,1)S(1)} %copy-done.14), channel_id=1, source_target_pairs={{0,64},{32,96},{64,0},{96,32},{1,65},{33,97},{65,1},{97,33},{2,66}... | collective-permute-start | bytes 1572872 | tf_op jit(solution)/shard_map/ppermute | solution.py:416
  152.4 23.9 %collective-permute-start.14 = (bf16[2,64,2048]{2,1,0:T(8,128)(2,1)S(1)}, bf16[2,64,2048]{2,1,0:T(8,128)(2,1)S(1)}, u32[]{:S(2)}, u32[]{:S(2)}) collective-permute-start(bf16[2,64,2048]{2,1,0:T(8,128)(2,1)S(1)} %copy-done.13), channel_id=1, source_target_pairs={{0,96},{32,0},{64,32},{96,64},{1,97},{33,1},{65,33},{97,65},{2,98}... | collective-permute-start | bytes 1572872 | tf_op jit(solution)/shard_map/ppermute | solution.py:416
  161.2 15.1 %all-to-all-start = ((f32[4,2,64,128]{3,2,1,0:T(8,128)}), f32[4,2,64,128]{3,2,1,0:T(8,128)S(1)}, u32[]{:S(2)}, u32[]{:S(2)}) async-start(f32[4,2,64,128]{3,2,1,0:T(8,128)} %get-tuple-element.77), calls=%async_computation | async-start | bytes 524288 | tf_op jit(solution)/shard_map/all_to_all | solution.py:450
  (10 other events, 30.0 us)
Sparse Core Ops, SparseCore 0:
  10.3 71.6 all-gather.1

commit v6 on v5

--- a/solution.py
+++ b/solution.py
@@ -445,7 +445,7 @@
         partial = grad_hidden
         grad_hidden = grad(gq, weights, partial, last, col, cw)
         if before is None:
-            qs = [q] + to_owner(after(sends, pairs[1], grad_hidden))
+            qs = [q] + to_owner(after(sends, grad_hidden))
             before = after((back[0], attended), grad_hidden)
     back = lax.all_to_all(back[0], "enc", split_axis=0, concat_axis=0, tiled=True)
     grad_keys, grad_values = terms(me, pick, asked, qs, c, keys, values, back)

time: 200 us -> 197 us (0.985)
  the two profiles are of different devices: /device:TPU:100 before, /device:TPU:106 now
where the time goes in v6:
time: 197 us; the launch traced here: 196 us
  waiting for transfers between devices  75.4 us (38%)
  Pallas kernels  67.1 us (34%)
  starting transfers between devices  33.5 us (17%)
  between operations  14.3 us (7%)
  local copies, waits for them, and re-layouts  4.82 us (2%)
    ppermute x15, waiting for transfers between devices, shift(): return lax.ppermute(x, 'enc', [(i, (i + d) % 4) for i in range(4)])  51.4 us
    ppermute x15, starting transfers between devices, shift(): return lax.ppermute(x, 'enc', [(i, (i + d) % 4) for i in range(4)])  28.1 us
    all_gather x1, waiting for transfers between devices, per_device(): weights = lax.all_gather(query_weight, 'fsdp', axis=0, tiled=True)  23.3 us
    pallas_call x2, Pallas kernels, home(): pl.pallas_call(body, out_shape=out_shape, grid=(1,), in_specs=[SMEM] * 4...  15.4 us
    pallas_call x2, Pallas kernels, grad(): pl.pallas_call(grad_kernel, out_shape=shape((GROUPS * ROWS, depth), BF16...  15 us
    pallas_call x1, Pallas kernels, terms(): pl.pallas_call(functools.partial(terms_kernel, tw), out_shape=(full,) * 2...  14.5 us
    pallas_call x1, Pallas kernels, query(): pl.pallas_call(query_kernel, out_shape=(shape((GROUPS, ROWS, WIDTH), BF16...  9.68 us
    pallas_call x2, Pallas kernels, collect(): pl.pallas_call(functools.partial(collect_kernel, col, cw), out_shape=(one...  8.88 us
  transfers between devices with their start and end apart: 17, of which 6 were waited for; matrix products, arithmetic and copies ran while one was open for 1% of the time, Pallas kernels for 27%

profile of v6, /device:TPU:106, one launch (start us, length us, event | category | flops | bytes accessed | tf_op | source)
XLA Modules:
  0.0 195.7 jit_solution(2706051222970049690)
XLA Ops:
  10.1 1.3 route.1
  11.4 1.6 collective-permute-start
  13.0 2.4 %spread.1 = (bf16[2,64,2048]{2,1,0:T(8,128)(2,1)}, bf16[2,64,2048]{2,1,0:T(8,128)(2,1)}, bf16[2,64,2048]{2,1,0:T(8,128)(2,1)}) custom-call(s32[8]{0:T(128)} %get-tuple-element.42.pick.refs_0_.refs_1_, bf16[3,64,2048]{2,1,0:T(8,128)(2,1)} %bitcast.2), custom_call_target="tpu_custom_call" | custom-call | flops 1 | bytes 2621440 | tf_op jit(solution)/shard_map/spread/pallas_call | solution.py:95
  15.4 1.4 collective-permute-start.3
  16.8 2.2 %collective-permute-start.4 = (bf16[2,64,2048]{2,1,0:T(8,128)(2,1)}, bf16[2,64,2048]{2,1,0:T(8,128)(2,1)S(1)}, u32[]{:S(2)}, u32[]{:S(2)}) collective-permute-start(bf16[2,64,2048]{2,1,0:T(8,128)(2,1)} %get-tuple-element.52), channel_id=1, source_target_pairs={{0,64},{32,96},{64,0},{96,32},{1,65},{33,97},{65,1},{97,33},{2,66}... | collective-permute-start | bytes 1572872 | tf_op jit(solution)/shard_map/ppermute | solution.py:416
  20.1 1.3 collective-permute-start.2
  22.4 19.9 %collective-permute-done.2.refs_3_.refs_5_ = s32[8]{0:T(128)S(1)} collective-permute-done((s32[8]{0:T(128)}, s32[8]{0:T(128)S(1)}, u32[]{:S(2)}, u32[]{:S(2)}) %collective-permute-start.2) | collective-permute-done | bytes 64 | tf_op jit(solution)/shard_map/ppermute | solution.py:416
  43.4 5.8 %collect.3 = (bf16[2,2,128,1536]{3,2,1,0:T(8,128)(2,1)}, bf16[2,2,128,1536]{3,2,1,0:T(8,128)(2,1)}, bf16[2,2,128,1536]{3,2,1,0:T(8,128)(2,1)}) custom-call(s32[8]{0:T(128)} %get-tuple-element.44.refs_0_.refs_2_, s32[8]{0:T(128)} %copy-done.10, s32[8]{0:T(128)} %copy-done.12, s32[8]{0:T(128)} %copy-done.11, bf16[6,128,2048]{2,1,0:T(8,128)(2,1)} %refs_14_.1, ...), custom_call_target="tpu_custom_call" | custom-call | flops 1 | bytes 9437184 | tf_op jit(solution)/shard_map/collect/pallas_call | solution.py:172
  49.7 2.2 %collective-permute-start.10 = (bf16[2,2,128,1536]{3,2,1,0:T(8,128)(2,1)}, bf16[2,2,128,1536]{3,2,1,0:T(8,128)(2,1)S(1)}, u32[]{:S(2)}, u32[]{:S(2)}) collective-permute-start(bf16[2,2,128,1536]{3,2,1,0:T(8,128)(2,1)} %get-tuple-element.62), channel_id=1, source_target_pairs={{0,64},{32,96},{64,0},{96,32},{1,65},{33,97},{65,1},{97,33},{2,66}... | collective-permute-start | bytes 4718600 | tf_op jit(solution)/shard_map/ppermute | solution.py:416
  51.9 1.9 collective-permute-start.11
  53.7 3.1 %collect.2 = (bf16[2,2,128,512]{3,2,1,0:T(8,128)(2,1)}, bf16[2,2,128,512]{3,2,1,0:T(8,128)(2,1)}, bf16[2,2,128,512]{3,2,1,0:T(8,128)(2,1)}) custom-call(s32[8]{0:T(128)} %get-tuple-element.44.refs_0_.refs_2_, s32[8]{0:T(128)} %copy-done.10, s32[8]{0:T(128)} %copy-done.12, s32[8]{0:T(128)} %copy-done.11, bf16[6,128,2048]{2,1,0:T(8,128)(2,1)} %refs_14_.1, ...), custom_call_target="tpu_custom_call" | custom-call | flops 1 | bytes 3145728 | tf_op jit(solution)/shard_map/collect/pallas_call | solution.py:172
  57.1 1.7 collective-permute-start.7
  58.8 23.3 %all-gather.2.cloned.1.call-done.w = bf16[4096,2048]{1,0:T(8,128)(2,1)} async-done(((bf16[128,2048]{1,0:T(8,128)(2,1)}), bf16[4096,2048]{1,0:T(8,128)(2,1)}) %all-gather.2.cloned.1.call-update) | async-done | bytes 16777232 | tf_op jit(solution)/shard_map/all_gather | solution.py:433
  82.1 9.7 %query.1 = (bf16[3,64,2048]{2,1,0:T(8,128)(2,1)}, bf16[2,64,2048]{2,1,0:T(8,128)(2,1)}, bf16[2,64,2048]{2,1,0:T(8,128)(2,1)}, bf16[2,64,2048]{2,1,0:T(8,128)(2,1)}) custom-call(s32[8]{0:T(128)} %get-tuple-element.42.pick.refs_0_.refs_1_, bf16[192,4096]{1,0:T(8,128)(2,1)} %hid.1, bf16[4096,2048]{1,0:T(8,128)(2,1)} %all-gather.2.cloned.1.call-done.w), custom_call_target="tpu_custom_call" | custom-call | flops 3221225472 | bytes 18350080 | tf_op jit(solution)/shard_map/query/pallas_call | solution.py:120
  91.8 28.3 %collective-permute-done.9.refs_8_ = bf16[2,2,128,1536]{3,2,1,0:T(8,128)(2,1)S(1)} collective-permute-done((bf16[2,2,128,1536]{3,2,1,0:T(8,128)(2,1)}, bf16[2,2,128,1536]{3,2,1,0:T(8,128)(2,1)S(1)}, u32[]{:S(2)}, u32[]{:S(2)}) %collective-permute-start.9) | collective-permute-done | bytes 1572896 | tf_op jit(solution)/shard_map/ppermute | solution.py:416
  121.1 1.7 collective-permute-done.11.refs_10_
  122.8 9.8 %home.2 = (bf16[192,2048]{1,0:T(8,128)(2,1)}, bf16[192,1536]{1,0:T(8,128)(2,1)}, f32[3,64,128]{2,1,0:T(8,128)}) custom-call(s32[8]{0:T(128)} %get-tuple-element.42.pick.refs_0_.refs_1_, s32[8]{0:T(128)} %get-tuple-element.43.refs_1_, s32[8]{0:T(128)} %get-tuple-element.44.refs_0_.refs_2_, s32[1]{0:T(128)} %bitcast.me.refs_3_.refs_0_, ...), custom_call_target="tpu_custom_call" | custom-call | flops 603979776 | bytes 5898240 | tf_op jit(solution)/shard_map/home/pallas_call | solution.py:284
  132.6 9.0 %grad.2.refs_0_ = f32[192,4096]{1,0:T(8,128)} custom-call(bf16[192,1536]{1,0:T(8,128)(2,1)} %get-tuple-element.66.gq, bf16[4096,2048]{1,0:T(8,128)(2,1)} %all-gather.2.cloned.1.call-done.w), custom_call_target="tpu_custom_call" | custom-call | flops 2415919104 | bytes 15728640 | tf_op jit(solution)/shard_map/grad/pallas_call | solution.py:402
  141.6 2.4 %collective-permute-start.12 = (bf16[2,64,2048]{2,1,0:T(8,128)(2,1)S(1)}, bf16[2,64,2048]{2,1,0:T(8,128)(2,1)S(1)}, u32[]{:S(2)}, u32[]{:S(2)}) collective-permute-start(bf16[2,64,2048]{2,1,0:T(8,128)(2,1)S(1)} %copy-done.15), channel_id=1, source_target_pairs={{0,32},{32,64},{64,96},{96,0},{1,33},{33,65},{65,97},{97,1},{2,34}... | collective-permute-start | bytes 1572872 | tf_op jit(solution)/shard_map/ppermute | solution.py:416
  144.0 10.7 %collective-permute-start.13 = (bf16[2,64,2048]{2,1,0:T(8,128)(2,1)S(1)}, bf16[2,64,2048]{2,1,0:T(8,128)(2,1)S(1)}, u32[]{:S(2)}, u32[]{:S(2)}) collective-permute-start(bf16[2,64,2048]{2,1,0:T(8,128)(2,1)S(1)} %copy-done.14), channel_id=1, source_target_pairs={{0,64},{32,96},{64,0},{96,32},{1,65},{33,97},{65,1},{97,33},{2,66}... | collective-permute-start | bytes 1572872 | tf_op jit(solution)/shard_map/ppermute | solution.py:416
  155.5 5.6 %home.3 = (bf16[192,2048]{1,0:T(8,128)(2,1)}, bf16[192,512]{1,0:T(8,128)(2,1)}, f32[4,2,64,128]{3,2,1,0:T(8,128)}) custom-call(s32[8]{0:T(128)} %get-tuple-element.42.pick.refs_0_.refs_1_, s32[8]{0:T(128)} %get-tuple-element.43.refs_1_, s32[8]{0:T(128)} %get-tuple-element.44.refs_0_.refs_2_, ...), custom_call_target="tpu_custom_call", output_to_operand_aliasing={{0}: (12, {})} | custom-call | flops 201326592 | bytes 1966080 | tf_op jit(solution)/shard_map/home/pallas_call | solution.py:284
  161.1 5.4 %all-to-all-start = ((f32[4,2,64,128]{3,2,1,0:T(8,128)}), f32[4,2,64,128]{3,2,1,0:T(8,128)S(1)}, u32[]{:S(2)}, u32[]{:S(2)}) async-start(f32[4,2,64,128]{3,2,1,0:T(8,128)} %get-tuple-element.77), calls=%async_computation | async-start | bytes 524288 | tf_op jit(solution)/shard_map/all_to_all | solution.py:450
  166.5 6.0 %grad.3 = bf16[192,4096]{1,0:T(8,128)(2,1)} custom-call(bf16[192,512]{1,0:T(8,128)(2,1)} %get-tuple-element.70.gq, bf16[4096,2048]{1,0:T(8,128)(2,1)} %all-gather.2.cloned.1.call-done.w, f32[192,4096]{1,0:T(8,128)} %grad.2.refs_0_), custom_call_target="tpu_custom_call" | custom-call | flops 805306368 | bytes 7340032 | tf_op jit(solution)/shard_map/grad/pallas_call | solution.py:402
  174.3 14.5 %terms.1 = (bf16[6,128,2048]{2,1,0:T(8,128)(2,1)}, bf16[6,128,2048]{2,1,0:T(8,128)(2,1)}) custom-call(s32[1]{0:T(128)} %bitcast.me.refs_3_.refs_0_, s32[8]{0:T(128)} %get-tuple-element.42.pick.refs_0_.refs_1_, s32[8]{0:T(128)} %get-tuple-element.44.refs_0_.refs_2_, s32[8]{0:T(128)} %copy-done.10, s32[8]{0:T(128)} %copy-done.12, s32[8]{0:T(128)} %copy-done.11, ...), custom_call_target="tpu_custom_call" | custom-call | flops 1073741824 | bytes 11534336 | tf_op jit(solution)/shard_map/terms/pallas_call | solution.py:372
  (58 shorter events, 10.6 us)
Async XLA Ops:
  7.2 74.9 %all-gather.2.cloned.1.call-start = ((), (), s32[]{:S(2)}) async-start(), calls=%async_computation.1 | async-start | bytes 17301504 | tf_op jit(solution)/shard_map/all_gather | solution.py:433
  11.4 4.0 %collective-permute-start = (s32[8]{0:T(128)}, s32[8]{0:T(128)S(1)}, u32[]{:S(2)}, u32[]{:S(2)}) collective-permute-start(s32[8]{0:T(128)} %get-tuple-element.44.refs_0_.refs_2_), channel_id=1, source_target_pairs={{0,32},{32,64},{64,96},{96,0},{1,33},{33,65},{65,97},{97,1},{2,34}... | collective-permute-start | bytes 104 | tf_op jit(solution)/shard_map/ppermute | solution.py:416
  15.4 27.4 %copy-start.10 = (s32[8]{0:T(128)}, s32[8]{0:T(128)S(1)}, u32[]{:S(2)}) copy-start(s32[8]{0:T(128)S(1)} %collective-permute-done.refs_1_.refs_3_) | copy-start | bytes 100
  15.4 33.8 %collective-permute-start.3 = (bf16[2,64,2048]{2,1,0:T(8,128)(2,1)}, bf16[2,64,2048]{2,1,0:T(8,128)(2,1)S(1)}, u32[]{:S(2)}, u32[]{:S(2)}) collective-permute-start(bf16[2,64,2048]{2,1,0:T(8,128)(2,1)} %get-tuple-element.51), channel_id=1, source_target_pairs={{0,32},{32,64},{64,96},{96,0},{1,33},{33,65},{65,97},{97,1},{2,34}... | collective-permute-start | bytes 1572872 | tf_op jit(solution)/shard_map/ppermute | solution.py:416
  16.8 32.5 %collective-permute-start.4 = (bf16[2,64,2048]{2,1,0:T(8,128)(2,1)}, bf16[2,64,2048]{2,1,0:T(8,128)(2,1)S(1)}, u32[]{:S(2)}, u32[]{:S(2)}) collective-permute-start(bf16[2,64,2048]{2,1,0:T(8,128)(2,1)} %get-tuple-element.52), channel_id=1, source_target_pairs={{0,64},{32,96},{64,0},{96,32},{1,65},{33,97},{65,1},{97,33},{2,66}... | collective-permute-start | bytes 1572872 | tf_op jit(solution)/shard_map/ppermute | solution.py:416
  18.9 30.3 %collective-permute-start.5 = (bf16[2,64,2048]{2,1,0:T(8,128)(2,1)}, bf16[2,64,2048]{2,1,0:T(8,128)(2,1)S(1)}, u32[]{:S(2)}, u32[]{:S(2)}) collective-permute-start(bf16[2,64,2048]{2,1,0:T(8,128)(2,1)} %get-tuple-element.53), channel_id=1, source_target_pairs={{0,96},{32,0},{64,32},{96,64},{1,97},{33,1},{65,33},{97,65},{2,98}... | collective-permute-start | bytes 1572872 | tf_op jit(solution)/shard_map/ppermute | solution.py:416
  20.1 22.2 %collective-permute-start.2 = (s32[8]{0:T(128)}, s32[8]{0:T(128)S(1)}, u32[]{:S(2)}, u32[]{:S(2)}) collective-permute-start(s32[8]{0:T(128)} %get-tuple-element.44.refs_0_.refs_2_), channel_id=1, source_target_pairs={{0,96},{32,0},{64,32},{96,64},{1,97},{33,1},{65,33},{97,65},{2,98}... | collective-permute-start | bytes 104 | tf_op jit(solution)/shard_map/ppermute | solution.py:416
  21.5 21.3 %collective-permute-start.1 = (s32[8]{0:T(128)}, s32[8]{0:T(128)S(1)}, u32[]{:S(2)}, u32[]{:S(2)}) collective-permute-start(s32[8]{0:T(128)} %get-tuple-element.44.refs_0_.refs_2_), channel_id=1, source_target_pairs={{0,64},{32,96},{64,0},{96,32},{1,65},{33,97},{65,1},{97,33},{2,66}... | collective-permute-start | bytes 104 | tf_op jit(solution)/shard_map/ppermute | solution.py:416
  49.2 7.6 %copy-start.3 = (bf16[2,64,2048]{2,1,0:T(8,128)(2,1)}, bf16[2,64,2048]{2,1,0:T(8,128)(2,1)S(1)}, u32[]{:S(2)}) copy-start(bf16[2,64,2048]{2,1,0:T(8,128)(2,1)S(1)} %collective-permute-done.3.refs_11_) | copy-start | bytes 1572868
  49.2 7.6 %copy-start.4 = (bf16[2,64,2048]{2,1,0:T(8,128)(2,1)}, bf16[2,64,2048]{2,1,0:T(8,128)(2,1)S(1)}, u32[]{:S(2)}) copy-start(bf16[2,64,2048]{2,1,0:T(8,128)(2,1)S(1)} %collective-permute-done.4.refs_12_) | copy-start | bytes 1572868
  49.3 70.8 %collective-permute-start.9 = (bf16[2,2,128,1536]{3,2,1,0:T(8,128)(2,1)}, bf16[2,2,128,1536]{3,2,1,0:T(8,128)(2,1)S(1)}, u32[]{:S(2)}, u32[]{:S(2)}) collective-permute-start(bf16[2,2,128,1536]{3,2,1,0:T(8,128)(2,1)} %get-tuple-element.61), channel_id=1, source_target_pairs={{0,96},{32,0},{64,32},{96,64},{1,97},{33,1},{65,33},{97,65},{2,98}... | collective-permute-start | bytes 4718600 | tf_op jit(solution)/shard_map/ppermute | solution.py:416
  49.7 71.4 %collective-permute-start.10 = (bf16[2,2,128,1536]{3,2,1,0:T(8,128)(2,1)}, bf16[2,2,128,1536]{3,2,1,0:T(8,128)(2,1)S(1)}, u32[]{:S(2)}, u32[]{:S(2)}) collective-permute-start(bf16[2,2,128,1536]{3,2,1,0:T(8,128)(2,1)} %get-tuple-element.62), channel_id=1, source_target_pairs={{0,64},{32,96},{64,0},{96,32},{1,65},{33,97},{65,1},{97,33},{2,66}... | collective-permute-start | bytes 4718600 | tf_op jit(solution)/shard_map/ppermute | solution.py:416
  51.9 70.9 %collective-permute-start.11 = (bf16[2,2,128,1536]{3,2,1,0:T(8,128)(2,1)}, bf16[2,2,128,1536]{3,2,1,0:T(8,128)(2,1)}, u32[]{:S(2)}, u32[]{:S(2)}) collective-permute-start(bf16[2,2,128,1536]{3,2,1,0:T(8,128)(2,1)} %get-tuple-element.63), channel_id=1, source_target_pairs={{0,32},{32,64},{64,96},{96,0},{1,33},{33,65},{65,97},{97,1},{2,34}... | collective-permute-start | bytes 4718600 | tf_op jit(solution)/shard_map/ppermute | solution.py:416
  56.9 97.8 %collective-permute-start.6 = (bf16[2,2,128,512]{3,2,1,0:T(8,128)(2,1)}, bf16[2,2,128,512]{3,2,1,0:T(8,128)(2,1)}, u32[]{:S(2)}, u32[]{:S(2)}) collective-permute-start(bf16[2,2,128,512]{3,2,1,0:T(8,128)(2,1)} %get-tuple-element.54), channel_id=1, source_target_pairs={{0,96},{32,0},{64,32},{96,64},{1,97},{33,1},{65,33},{97,65},{2,98}... | collective-permute-start | bytes 1572872 | tf_op jit(solution)/shard_map/ppermute | solution.py:416
  57.1 97.5 %collective-permute-start.7 = (bf16[2,2,128,512]{3,2,1,0:T(8,128)(2,1)}, bf16[2,2,128,512]{3,2,1,0:T(8,128)(2,1)}, u32[]{:S(2)}, u32[]{:S(2)}) collective-permute-start(bf16[2,2,128,512]{3,2,1,0:T(8,128)(2,1)} %get-tuple-element.55), channel_id=1, source_target_pairs={{0,64},{32,96},{64,0},{96,32},{1,65},{33,97},{65,1},{97,33},{2,66}... | collective-permute-start | bytes 1572872 | tf_op jit(solution)/shard_map/ppermute | solution.py:416
  82.1 38.0 %copy-start.16 = (bf16[2,2,128,512]{3,2,1,0:T(8,128)(2,1)S(1)}, bf16[2,2,128,512]{3,2,1,0:T(8,128)(2,1)}, u32[]{:S(2)}) copy-start(bf16[2,2,128,512]{3,2,1,0:T(8,128)(2,1)} %get-tuple-element.57) | copy-start | bytes 1572868
  120.0 34.6 %collective-permute-start.8 = (bf16[2,2,128,512]{3,2,1,0:T(8,128)(2,1)S(1)}, bf16[2,2,128,512]{3,2,1,0:T(8,128)(2,1)S(1)}, u32[]{:S(2)}, u32[]{:S(2)}) collective-permute-start(bf16[2,2,128,512]{3,2,1,0:T(8,128)(2,1)S(1)} %copy-done.16), channel_id=1, source_target_pairs={{0,32},{32,64},{64,96},{96,0},{1,33},{33,65},{65,97},{97,1},{2,34}... | collective-permute-start | bytes 1572872 | tf_op jit(solution)/shard_map/ppermute | solution.py:416
  132.6 9.0 %copy-start.15 = (bf16[2,64,2048]{2,1,0:T(8,128)(2,1)S(1)}, bf16[2,64,2048]{2,1,0:T(8,128)(2,1)}, u32[]{:S(2)}) copy-start(bf16[2,64,2048]{2,1,0:T(8,128)(2,1)} %get-tuple-element.74) | copy-start | bytes 1572868
  132.6 11.4 %copy-start.14 = (bf16[2,64,2048]{2,1,0:T(8,128)(2,1)S(1)}, bf16[2,64,2048]{2,1,0:T(8,128)(2,1)}, u32[]{:S(2)}) copy-start(bf16[2,64,2048]{2,1,0:T(8,128)(2,1)} %get-tuple-element.75) | copy-start | bytes 1572868
  132.6 22.1 %copy-start.13 = (bf16[2,64,2048]{2,1,0:T(8,128)(2,1)S(1)}, bf16[2,64,2048]{2,1,0:T(8,128)(2,1)}, u32[]{:S(2)}) copy-start(bf16[2,64,2048]{2,1,0:T(8,128)(2,1)} %get-tuple-element.76) | copy-start | bytes 1572868
  141.6 30.9 %collective-permute-start.12 = (bf16[2,64,2048]{2,1,0:T(8,128)(2,1)S(1)}, bf16[2,64,2048]{2,1,0:T(8,128)(2,1)S(1)}, u32[]{:S(2)}, u32[]{:S(2)}) collective-permute-start(bf16[2,64,2048]{2,1,0:T(8,128)(2,1)S(1)} %copy-done.15), channel_id=1, source_target_pairs={{0,32},{32,64},{64,96},{96,0},{1,33},{33,65},{65,97},{97,1},{2,34}... | collective-permute-start | bytes 1572872 | tf_op jit(solution)/shard_map/ppermute | solution.py:416
  144.0 28.5 %collective-permute-start.13 = (bf16[2,64,2048]{2,1,0:T(8,128)(2,1)S(1)}, bf16[2,64,2048]{2,1,0:T(8,128)(2,1)S(1)}, u32[]{:S(2)}, u32[]{:S(2)}) collective-permute-start(bf16[2,64,2048]{2,1,0:T(8,128)(2,1)S(1)} %copy-done.14), channel_id=1, source_target_pairs={{0,64},{32,96},{64,0},{96,32},{1,65},{33,97},{65,1},{97,33},{2,66}... | collective-permute-start | bytes 1572872 | tf_op jit(solution)/shard_map/ppermute | solution.py:416
  154.7 17.8 %collective-permute-start.14 = (bf16[2,64,2048]{2,1,0:T(8,128)(2,1)S(1)}, bf16[2,64,2048]{2,1,0:T(8,128)(2,1)S(1)}, u32[]{:S(2)}, u32[]{:S(2)}) collective-permute-start(bf16[2,64,2048]{2,1,0:T(8,128)(2,1)S(1)} %copy-done.13), channel_id=1, source_target_pairs={{0,96},{32,0},{64,32},{96,64},{1,97},{33,1},{65,33},{97,65},{2,98}... | collective-permute-start | bytes 1572872 | tf_op jit(solution)/shard_map/ppermute | solution.py:416
  161.1 11.4 %all-to-all-start = ((f32[4,2,64,128]{3,2,1,0:T(8,128)}), f32[4,2,64,128]{3,2,1,0:T(8,128)S(1)}, u32[]{:S(2)}, u32[]{:S(2)}) async-start(f32[4,2,64,128]{3,2,1,0:T(8,128)} %get-tuple-element.77), calls=%async_computation | async-start | bytes 524288 | tf_op jit(solution)/shard_map/all_to_all | solution.py:450
  (10 other events, 17.6 us)
Sparse Core Ops, SparseCore 0:
  10.3 71.7 all-gather.1
